TPU v7x, 32 devices: a whole 2x2x4 slice. The times are simulated.
32 devices in a mesh: row: 8 (over y, x, core), col: 4 (over z).
Axes of the slice: x: 2, y: 2, z: 4, core: 2. Of those that a mesh axis runs over, the one named last changes fastest.
Arguments:
- inputs: bfloat16 [8192, 2048], P('row', 'col'), may hold values from -6 to 6
- cotangent: bfloat16 [8192, 2048], P('row', 'col'), may hold values from -6 to 6
- attention_norm_gain: float32 [2048], replicated, may hold values from 0.28 to 2.6
- expert_norm_gain: float32 [2048], replicated, may hold values from 0.5 to 1.5
- query_norm_gain: float32 [128], replicated, may hold values from 0.5 to 1.5
- key_norm_gain: float32 [128], replicated, may hold values from 0.5 to 1.5
- frozen_query_weight: bfloat16 [2048, 4096], P('row', 'col'), may hold values from -0.125 to 0.125
- frozen_key_weight: bfloat16 [2048, 512], P('row'), may hold values from -0.125 to 0.125
- frozen_value_weight: bfloat16 [2048, 512], P('row'), may hold values from -0.125 to 0.125
- frozen_output_weight: bfloat16 [4096, 2048], P('col', 'row'), may hold values from -1.5 to 1.5
- frozen_router_weight: bfloat16 [2048, 16], P('row'), may hold values from -0.0625 to 0.0625
- expert_gate_up_weight: bfloat16 [16, 2048, 1536], P('col', 'row'), may hold values from -0.125 to 0.125
- expert_down_weight: bfloat16 [16, 768, 2048], P('col', None, 'row'), may hold values from -1.25 to 1.25
- adapter_input_down: float32 [8, 2048, 48], P(None, 'row'), may hold values from -0.125 to 0.125
- adapter_query_up: float32 [8, 16, 4096], P(None, None, 'col'), may hold values from -0.75 to 0.75
- adapter_key_value_up: float32 [8, 2, 16, 512], replicated, may hold values from -0.75 to 0.75
- adapter_output_down: float32 [8, 4096, 16], P(None, 'col'), may hold values from -1.5 to 1.5
- adapter_output_up: float32 [8, 2048, 16], P(None, 'row'), may hold values from -0.75 to 0.75
- input_first_moment: float32 [8, 2048, 48], P(None, 'row'), may hold values from -0.0004272461 to 0.0004272461
- input_second_moment: float32 [8, 2048, 48], P(None, 'row'), may hold values from 4.4878792e-10 to 1.7951517e-09
- query_first_moment: float32 [8, 16, 4096], P(None, None, 'col'), may hold values from -7.6293945e-05 to 7.6293945e-05
- query_second_moment: float32 [8, 16, 4096], P(None, None, 'col'), may hold values from 1.3463637e-11 to 5.385455e-11
- key_value_first_moment: float32 [8, 2, 16, 512], replicated, may hold values from -0.0004272461 to 0.0004272461
- key_value_second_moment: float32 [8, 2, 16, 512], replicated, may hold values from 4.4878792e-10 to 1.7951517e-09
- output_down_first_moment: float32 [8, 4096, 16], P(None, 'col'), may hold values from -4.5776367e-05 to 4.5776367e-05
- output_down_second_moment: float32 [8, 4096, 16], P(None, 'col'), may hold values from 4.4878793e-12 to 1.7951517e-11
- output_up_first_moment: float32 [8, 2048, 16], P(None, 'row'), may hold values from -9.1552734e-05 to 9.1552734e-05
- output_up_second_moment: float32 [8, 2048, 16], P(None, 'row'), may hold values from 1.7951517e-11 to 7.180607e-11
- routes: int32 [8192, 8], P('row'), may hold values from 0 to 15, all different within a row; in each aligned block of 1024 rows (0 to 1023, 1024 to 2047, ...) at most 1024 rows name the same one
- tree_adapter_index: int32 [8], P('row'), may hold values from 0 to 7
- tree_node_length: int32 [8, 13], P('row'), may hold values from 1 to 512, 1024 in all within a row
- parents: int32 [8, 13], P('row'), may hold values from 0 to 4, as said below
Outputs:
- layer_output: float32 [8192, 2048], P('row', 'col')
- input_grad: float32 [8192, 2048], P('row', 'col')
- grad_norm: float32 [], replicated
- lora_in_next: float32 [8, 2048, 48], P(None, 'row')
- first_in_next: float32 [8, 2048, 48], P(None, 'row')
- second_in_next: float32 [8, 2048, 48], P(None, 'row')
- lora_query_next: float32 [8, 16, 4096], P(None, None, 'col')
- first_query_next: float32 [8, 16, 4096], P(None, None, 'col')
- second_query_next: float32 [8, 16, 4096], P(None, None, 'col')
- lora_kv_next: float32 [8, 2, 16, 512], replicated
- first_kv_next: float32 [8, 2, 16, 512], replicated
- second_kv_next: float32 [8, 2, 16, 512], replicated
- lora_out_down_next: float32 [8, 4096, 16], P(None, 'col')
- first_out_down_next: float32 [8, 4096, 16], P(None, 'col')
- second_out_down_next: float32 [8, 4096, 16], P(None, 'col')
- lora_out_up_next: float32 [8, 2048, 16], P(None, 'row')
- first_out_up_next: float32 [8, 2048, 16], P(None, 'row')
- second_out_up_next: float32 [8, 2048, 16], P(None, 'row')
- expert_output: float32 [8192, 2048], P('row', 'col')
Inputs may be any that keep to these rules, and one draw needn't show every extreme that they name: `parents`: node 0 is the trunk and its own parent; nodes 1 to 4 hang from node 0; every later node hangs from one of nodes 1 to 4. `routes`: no expert is named by more than 1024 rows of one tree.
All inputs are finite; a program needn't handle non-finite values.
Results may differ from a plain program's by a relative error of at most 0.025.
Values may be sent and summed in bfloat16 or wider, within the bound.
No kernel may reach another device: no remote copies, remote signals or barrier semaphores. Data moves between devices by JAX's collectives and lax.ppermute only.
A program may use at most 384 MiB of HBM per device.

v0:
```python
import jax
import jax.numpy as jnp
from jax import lax
from jax.sharding import PartitionSpec as P

HEAD_WIDTH = 128
STEP = 10


highest = lax.Precision.HIGHEST
norm_eps = 1e-06
rope_base = 1000000.0
beta_first = 0.9
beta_second = 0.999
adam_eps = 1e-08
decay_rate = 0.01
learning_rate_lower = 0.02
learning_rate_upper = 0.1
learning_rate_output = 0.25
clip_limit = 1.0
masked_score = -1e30


def rms_norm(values, gain):
    return values * lax.rsqrt(jnp.mean(values * values, axis=-1, keepdims=True) + norm_eps) * gain


def rotate(values, positions):
    half_dim = values.shape[-1] // 2
    frequency = rope_base ** (-jnp.arange(half_dim, dtype=jnp.float32) / half_dim)
    angles = positions.astype(jnp.float32)[:, None] * frequency[None, :]
    cosine = jnp.cos(angles)[:, None, :]
    sine_part = jnp.sin(angles)[:, None, :]
    lower_half = values[..., :half_dim]
    upper_half = values[..., half_dim:]
    return jnp.concatenate(
        [
            lower_half * cosine - upper_half * sine_part,
            upper_half * cosine + lower_half * sine_part,
        ],
        axis=-1,
    )


def tree_layout(lengths, parents, token_count):
    node_ids = jnp.arange(lengths.shape[0], dtype=jnp.int32)
    node_ends = jnp.cumsum(lengths, dtype=jnp.int32)
    node_starts = node_ends - lengths
    token_ids = jnp.arange(token_count, dtype=jnp.int32)
    node_of = jnp.sum(
        (token_ids[:, None] >= node_ends[None, :]).astype(jnp.int32), axis=1, dtype=jnp.int32
    )
    grandparent = parents[parents]
    ancestor = (
        (node_ids[None, :] == node_ids[:, None])
        | (node_ids[None, :] == parents[:, None])
        | (node_ids[None, :] == grandparent[:, None])
    )
    strict = ancestor & (node_ids[None, :] != node_ids[:, None])
    before = jnp.sum(jnp.where(strict, lengths[None, :], 0), axis=1, dtype=jnp.int32)
    node_hot = node_of[:, None] == node_ids[None, :]
    positions = (
        jnp.sum(jnp.where(node_hot, (before - node_starts)[None, :], 0), axis=1, dtype=jnp.int32)
        + token_ids
    )
    reachable = ancestor[node_of][:, node_of]
    allowed = reachable & (token_ids[None, :] <= token_ids[:, None])
    return (positions, allowed)


def contract_last(left, right, precision=None):
    return lax.dot_general(
        left,
        right,
        (((1,), (1,)), ((), ())),
        precision=precision,
        preferred_element_type=jnp.float32,
    )


def contract_leading(left, right, precision=None):
    return lax.dot_general(
        left,
        right,
        (((0,), (0,)), ((), ())),
        precision=precision,
        preferred_element_type=jnp.float32,
    )


def moment_update(weight, first, second, grad, rate):
    first = beta_first * first + (1.0 - beta_first) * grad
    second = beta_second * second + (1.0 - beta_second) * grad * grad
    first_hat = first / (1.0 - beta_first**STEP)
    second_hat = second / (1.0 - beta_second**STEP)
    weight = weight - rate * (first_hat / (jnp.sqrt(second_hat) + adam_eps) + decay_rate * weight)
    return (weight, first, second)


def shards(
    inputs,
    cotangent,
    attention_norm_gain,
    expert_norm_gain,
    query_norm_gain,
    key_norm_gain,
    frozen_query_weight,
    frozen_key_weight,
    frozen_value_weight,
    frozen_output_weight,
    frozen_router_weight,
    expert_gate_up_weight,
    expert_down_weight,
    adapter_input_down,
    adapter_query_up,
    adapter_key_value_up,
    adapter_output_down,
    adapter_output_up,
    input_first_moment,
    input_second_moment,
    query_first_moment,
    query_second_moment,
    key_value_first_moment,
    key_value_second_moment,
    output_down_first_moment,
    output_down_second_moment,
    output_up_first_moment,
    output_up_second_moment,
    routes,
    tree_adapter_index,
    tree_node_length,
    parents,
):
    col_count = lax.axis_size("col")
    row_count = lax.axis_size("row")
    col_index = lax.axis_index("col")
    length = inputs.shape[0]
    col_width = inputs.shape[1]
    width_size = col_width * col_count
    local_heads = frozen_query_weight.shape[1] // HEAD_WIDTH
    kv_total = frozen_key_weight.shape[1] // HEAD_WIDTH
    adapter_rank_size = adapter_query_up.shape[1]
    adapter_number = adapter_input_down.shape[0]
    local_experts = expert_gate_up_weight.shape[0]
    expert_total = frozen_router_weight.shape[1]
    top_count = routes.shape[1]
    inner_width = expert_down_weight.shape[1]
    capacity = 2 * length * top_count // expert_total
    key_value_head = col_index * kv_total // col_count
    adapter_slot = tree_adapter_index[0]
    col_start = col_index * col_width
    key_cols = lax.dynamic_slice_in_dim(
        frozen_key_weight, key_value_head * HEAD_WIDTH, HEAD_WIDTH, 1
    )
    value_cols = lax.dynamic_slice_in_dim(
        frozen_value_weight, key_value_head * HEAD_WIDTH, HEAD_WIDTH, 1
    )
    (
        query_full,
        key_full,
        value_full,
        out_full,
        router_full,
        gate_up_full,
        down_full,
        adapter_input_whole,
        adapter_up_whole,
    ) = (
        lax.all_gather(frozen_query_weight, "row", axis=0, tiled=True),
        lax.all_gather(key_cols, "row", axis=0, tiled=True),
        lax.all_gather(value_cols, "row", axis=0, tiled=True),
        lax.all_gather(frozen_output_weight, "row", axis=1, tiled=True),
        lax.all_gather(frozen_router_weight, "row", axis=0, tiled=True),
        lax.all_gather(expert_gate_up_weight, "row", axis=1, tiled=True),
        lax.all_gather(expert_down_weight, "row", axis=2, tiled=True),
        lax.all_gather(adapter_input_down.astype(jnp.bfloat16), "row", axis=1, tiled=True),
        lax.all_gather(adapter_output_up.astype(jnp.bfloat16), "row", axis=1, tiled=True),
    )
    full_in = lax.all_gather(inputs, "col", axis=1, tiled=True)
    hidden_input = full_in.astype(jnp.float32)
    positions, allowed = tree_layout(tree_node_length[0], parents[0], length)

    def norm_in(values):
        return rms_norm(values, attention_norm_gain)

    normalized_input = norm_in(hidden_input).astype(jnp.bfloat16)
    down_input = adapter_input_whole[adapter_slot]
    adapter_middle = jnp.dot(
        normalized_input, down_input, preferred_element_type=jnp.float32
    ).astype(jnp.bfloat16)
    query_raise = adapter_query_up[adapter_slot].astype(jnp.bfloat16)
    key_value_raise = lax.dynamic_slice_in_dim(
        adapter_key_value_up[adapter_slot], key_value_head * HEAD_WIDTH, HEAD_WIDTH, 2
    ).astype(jnp.bfloat16)
    query_projected = jnp.dot(
        normalized_input, query_full, preferred_element_type=jnp.float32
    ) + jnp.dot(
        adapter_middle[:, :adapter_rank_size], query_raise, preferred_element_type=jnp.float32
    )
    key_projected = jnp.dot(
        normalized_input, key_full, preferred_element_type=jnp.float32
    ) + jnp.dot(
        adapter_middle[:, adapter_rank_size : 2 * adapter_rank_size],
        key_value_raise[0],
        preferred_element_type=jnp.float32,
    )
    value_projected = jnp.dot(
        normalized_input, value_full, preferred_element_type=jnp.float32
    ) + jnp.dot(
        adapter_middle[:, 2 * adapter_rank_size :],
        key_value_raise[1],
        preferred_element_type=jnp.float32,
    )

    def shape_heads(query_vals, key_vals):
        query_rot = rotate(
            rms_norm(query_vals.reshape(length, local_heads, HEAD_WIDTH), query_norm_gain),
            positions,
        )
        key_rot = rotate(
            rms_norm(key_vals.reshape(length, 1, HEAD_WIDTH), key_norm_gain), positions
        )
        return (query_rot, key_rot)

    (query_rot, key_rot), heads_back = jax.vjp(shape_heads, query_projected, key_projected)
    queries = query_rot.astype(jnp.bfloat16)
    keys_low = key_rot[:, 0].astype(jnp.bfloat16)
    values_low = value_projected.astype(jnp.bfloat16)
    score_scale = HEAD_WIDTH ** (-0.5)

    def score_block():
        raw_scores = (
            jnp.einsum("ihd,jd->hij", queries, keys_low, preferred_element_type=jnp.float32)
            * score_scale
        )
        return jnp.where(allowed[None], raw_scores, masked_score)

    scores = score_block()
    row_max = jnp.max(scores, axis=-1, keepdims=True)
    log_total = row_max + jnp.log(jnp.sum(jnp.exp(scores - row_max), axis=-1, keepdims=True))
    probs_low = jnp.exp(scores - log_total).astype(jnp.bfloat16)
    head_rows = (
        jnp.einsum("hij,jd->ihd", probs_low, values_low, preferred_element_type=jnp.float32)
        .astype(jnp.bfloat16)
        .reshape(length, local_heads * HEAD_WIDTH)
    )
    down_output = adapter_output_down[adapter_slot].astype(jnp.bfloat16)
    mid_part = jnp.dot(head_rows, down_output, preferred_element_type=jnp.float32)
    middle_output = lax.psum(mid_part.astype(jnp.bfloat16), "col")
    attn_part = jnp.dot(head_rows, out_full, preferred_element_type=jnp.float32)
    attn_slice = lax.psum_scatter(
        attn_part.astype(jnp.bfloat16), "col", scatter_dimension=1, tiled=True
    ).astype(jnp.float32)
    up_output = adapter_up_whole[adapter_slot]
    up_slice = lax.dynamic_slice_in_dim(up_output, col_start, col_width, 0)
    tree_branch = attn_slice + contract_last(middle_output, up_slice)
    resid = inputs.astype(jnp.float32) + tree_branch
    resid_full = lax.all_gather(resid.astype(jnp.bfloat16), "col", axis=1, tiled=True).astype(
        resid.dtype
    )

    def norm_post(values):
        return rms_norm(values, expert_norm_gain)

    normed_post = norm_post(resid_full).astype(jnp.bfloat16)
    logits = jnp.dot(normed_post, router_full, preferred_element_type=jnp.float32)
    route_hot = routes[:, :, None] == jnp.arange(expert_total, dtype=jnp.int32)[None, None, :]
    chosen = jnp.sum(jnp.where(route_hot, logits[:, None, :], 0.0), axis=2)
    gate_probs = jax.nn.softmax(chosen, axis=-1)
    expert_ids = col_index * local_experts + jnp.arange(local_experts, dtype=jnp.int32)
    match = routes[:, :, None] == expert_ids[None, None, :]
    chosen_mask = jnp.any(match, axis=1)
    weight_tok = jnp.sum(jnp.where(match, gate_probs[:, :, None], 0.0), axis=1)
    slot_place = jnp.cumsum(chosen_mask.astype(jnp.int32), axis=0, dtype=jnp.int32) - 1
    slot_place = jnp.where(chosen_mask, slot_place, capacity)
    expert_col = jnp.broadcast_to(
        jnp.arange(local_experts, dtype=jnp.int32)[None, :], (length, local_experts)
    )
    token_row = jnp.broadcast_to(
        jnp.arange(length, dtype=jnp.int32)[:, None], (length, local_experts)
    )
    slot_token = (
        jnp.zeros((local_experts, capacity), jnp.int32)
        .at[expert_col, slot_place]
        .set(token_row, mode="drop")
    )
    slot_live = (
        jnp.zeros((local_experts, capacity), jnp.float32)
        .at[expert_col, slot_place]
        .set(1.0, mode="drop")
    )
    slot_weight = (
        jnp.zeros((local_experts, capacity), jnp.float32)
        .at[expert_col, slot_place]
        .set(weight_tok, mode="drop")
    )
    flat_token = slot_token.reshape(-1)
    expert_rows = jnp.where(
        slot_live[..., None] > 0.0, normed_post[slot_token], jnp.zeros((), jnp.bfloat16)
    )
    gate_up = jnp.einsum(
        "ecd,edf->ecf", expert_rows, gate_up_full, preferred_element_type=jnp.float32
    )
    gate_vals = gate_up[..., :inner_width]
    up_vals = gate_up[..., inner_width:]

    def swiglu(gate_in, up_in):
        return jax.nn.silu(gate_in) * up_in

    inner_act, swiglu_back = jax.vjp(swiglu, gate_vals, up_vals)
    expert_out = jnp.einsum(
        "ecf,efd->ecd",
        inner_act.astype(jnp.bfloat16),
        down_full,
        preferred_element_type=jnp.float32,
    )
    moe_part = (
        jnp.zeros((length, width_size), jnp.float32)
        .at[flat_token]
        .add((expert_out * slot_weight[..., None]).reshape(-1, width_size))
    )
    moe_slice = lax.psum_scatter(
        moe_part.astype(jnp.bfloat16), "col", scatter_dimension=1, tiled=True
    ).astype(jnp.float32)
    layer_output = resid + moe_slice
    cotangent_full = lax.all_gather(cotangent, "col", axis=1, tiled=True)
    cotangent_rows = cotangent_full[slot_token].astype(jnp.float32)
    gate_grad_slot = jnp.sum(cotangent_rows * expert_out, axis=-1) * slot_live
    expert_grad = (cotangent_rows * slot_weight[..., None]).astype(jnp.bfloat16)
    inner_grad = jnp.einsum(
        "ecd,efd->ecf", expert_grad, down_full, preferred_element_type=jnp.float32
    )
    gate_grad, up_grad = swiglu_back(inner_grad)
    gate_up_grad = jnp.concatenate([gate_grad, up_grad], axis=-1).astype(jnp.bfloat16)
    rows_grad = jnp.einsum(
        "ecf,edf->ecd", gate_up_grad, gate_up_full, preferred_element_type=jnp.float32
    )
    post_part = (
        jnp.zeros((length, width_size), jnp.float32)
        .at[flat_token]
        .add((rows_grad * slot_live[..., None]).reshape(-1, width_size))
    )
    slot_expert = jnp.broadcast_to(
        jnp.arange(local_experts, dtype=jnp.int32)[:, None], (local_experts, capacity)
    )
    token_gate = (
        jnp.zeros((length, local_experts), jnp.float32)
        .at[slot_token, slot_expert]
        .add(gate_grad_slot)
    )
    gates_part = jnp.sum(jnp.where(match, token_gate[:, None, :], 0.0), axis=2)
    post_sum, gates_grad = (
        lax.psum(post_part.astype(jnp.bfloat16), "col").astype(jnp.float32),
        lax.psum(gates_part.astype(jnp.bfloat16), "col").astype(jnp.float32),
    )
    chosen_grad = gate_probs * (
        gates_grad - jnp.sum(gate_probs * gates_grad, axis=-1, keepdims=True)
    )
    logits_grad = jnp.sum(jnp.where(route_hot, chosen_grad[:, :, None], 0.0), axis=1).astype(
        jnp.bfloat16
    )
    normed_post_grad = post_sum + contract_last(logits_grad, router_full)
    unused_post, post_back = jax.vjp(norm_post, resid_full)
    resid_grad = cotangent_full.astype(jnp.float32) + post_back(normed_post_grad)[0]
    resid_grad_slice = lax.dynamic_slice_in_dim(resid_grad, col_start, col_width, 1)
    branch_grad = resid_grad.astype(jnp.bfloat16)
    mid_out_grad = jnp.dot(branch_grad, up_output, preferred_element_type=jnp.float32)
    heads_grad = contract_last(branch_grad, out_full) + contract_last(
        mid_out_grad, down_output.astype(jnp.float32), highest
    )
    heads_grad_low = heads_grad.astype(jnp.bfloat16).reshape(length, local_heads, HEAD_WIDTH)
    scores_again = score_block()
    probs_again = jnp.exp(scores_again - log_total)
    probs_grad = jnp.einsum(
        "ihd,jd->hij", heads_grad_low, values_low, preferred_element_type=jnp.float32
    )
    scores_grad = (
        probs_again * (probs_grad - jnp.sum(probs_again * probs_grad, axis=-1, keepdims=True))
    ).astype(jnp.bfloat16)
    value_grad = jnp.einsum(
        "hij,ihd->jd",
        probs_again.astype(jnp.bfloat16),
        heads_grad_low,
        preferred_element_type=jnp.float32,
    )
    query_rot_grad = (
        jnp.einsum("hij,jd->ihd", scores_grad, keys_low, preferred_element_type=jnp.float32)
        * score_scale
    )
    key_rot_grad = (
        jnp.einsum("hij,ihd->jd", scores_grad, queries, preferred_element_type=jnp.float32)
        * score_scale
    )
    query_proj_grad, key_proj_grad = heads_back((query_rot_grad, key_rot_grad[:, None, :]))
    query_gradient_reduced = query_proj_grad.astype(jnp.bfloat16)
    key_gradient_reduced = key_proj_grad.astype(jnp.bfloat16)
    value_gradient_reduced = value_grad.astype(jnp.bfloat16)
    mid_grad_part = jnp.concatenate(
        [
            contract_last(query_gradient_reduced, query_raise),
            contract_last(key_gradient_reduced, key_value_raise[0]),
            contract_last(value_gradient_reduced, key_value_raise[1]),
        ],
        axis=1,
    )
    key_value_portion = jnp.stack(
        [
            contract_leading(
                adapter_middle[:, adapter_rank_size : 2 * adapter_rank_size], key_gradient_reduced
            ),
            contract_leading(adapter_middle[:, 2 * adapter_rank_size :], value_gradient_reduced),
        ]
    )
    key_value_block = lax.dynamic_update_slice(
        jnp.zeros(adapter_key_value_up.shape[1:], jnp.float32),
        key_value_portion,
        (0, 0, key_value_head * HEAD_WIDTH),
    )
    key_value_gradient_share = (
        jnp.zeros(adapter_key_value_up.shape, jnp.float32).at[adapter_slot].set(key_value_block)
    )
    mid_grad, kv_grad_col = (
        lax.psum(mid_grad_part.astype(jnp.bfloat16), "col").astype(jnp.float32),
        lax.psum(key_value_gradient_share.astype(jnp.bfloat16), "col").astype(jnp.float32),
    )
    normed_in_part = (
        contract_last(query_gradient_reduced, query_full)
        + contract_last(key_gradient_reduced, key_full)
        + contract_last(value_gradient_reduced, value_full)
    )
    normed_in_grad = lax.psum(normed_in_part.astype(jnp.bfloat16), "col").astype(
        jnp.float32
    ) + contract_last(mid_grad, down_input.astype(jnp.float32), highest)
    unused_in, in_back = jax.vjp(norm_in, hidden_input)
    input_part = lax.dynamic_slice_in_dim(in_back(normed_in_grad)[0], col_start, col_width, 1)
    input_grad = resid_grad_slice + input_part
    input_portion = contract_leading(normalized_input.astype(jnp.float32), mid_grad, highest)
    up_portion = contract_leading(branch_grad, middle_output)
    query_portion = contract_leading(adapter_middle[:, :adapter_rank_size], query_gradient_reduced)
    down_portion = contract_leading(head_rows.astype(jnp.float32), mid_out_grad, highest)
    in_grad_full = (
        jnp.zeros((adapter_number, width_size, 3 * adapter_rank_size), jnp.float32)
        .at[adapter_slot]
        .set(input_portion)
    )
    up_grad_full = (
        jnp.zeros((adapter_number, width_size, adapter_rank_size), jnp.float32)
        .at[adapter_slot]
        .set(up_portion)
    )
    input_gradient, output_up_gradient = (
        lax.psum_scatter(
            in_grad_full.astype(jnp.bfloat16), "row", scatter_dimension=1, tiled=True
        ).astype(jnp.float32),
        lax.psum_scatter(
            up_grad_full.astype(jnp.bfloat16), "row", scatter_dimension=1, tiled=True
        ).astype(jnp.float32),
    )
    query_gradient_share = (
        jnp.zeros(adapter_query_up.shape, jnp.float32).at[adapter_slot].set(query_portion)
    )
    down_gradient_share = (
        jnp.zeros(adapter_output_down.shape, jnp.float32).at[adapter_slot].set(down_portion)
    )
    query_gradient, output_down_gradient, key_value_gradient = (
        lax.psum(query_gradient_share.astype(jnp.bfloat16), "row").astype(jnp.float32),
        lax.psum(down_gradient_share.astype(jnp.bfloat16), "row").astype(jnp.float32),
        lax.psum(kv_grad_col.astype(jnp.bfloat16), "row").astype(jnp.float32),
    )
    squares = (
        (
            jnp.sum(input_gradient * input_gradient)
            + jnp.sum(output_up_gradient * output_up_gradient)
        )
        / col_count
        + (
            jnp.sum(query_gradient * query_gradient)
            + jnp.sum(output_down_gradient * output_down_gradient)
        )
        / row_count
        + jnp.sum(key_value_gradient * key_value_gradient) / (row_count * col_count)
    )
    total = lax.psum(squares, ("row", "col"))
    grad_norm = jnp.sqrt(total)
    scale_factor = jnp.minimum(1.0, clip_limit / (grad_norm + 1e-06))
    input_following = moment_update(
        adapter_input_down,
        input_first_moment,
        input_second_moment,
        input_gradient * scale_factor,
        learning_rate_lower,
    )
    query_following = moment_update(
        adapter_query_up,
        query_first_moment,
        query_second_moment,
        query_gradient * scale_factor,
        learning_rate_upper,
    )
    key_value_following = moment_update(
        adapter_key_value_up,
        key_value_first_moment,
        key_value_second_moment,
        key_value_gradient * scale_factor,
        learning_rate_upper,
    )
    down_following = moment_update(
        adapter_output_down,
        output_down_first_moment,
        output_down_second_moment,
        output_down_gradient * scale_factor,
        learning_rate_output,
    )
    up_following = moment_update(
        adapter_output_up,
        output_up_first_moment,
        output_up_second_moment,
        output_up_gradient * scale_factor,
        learning_rate_upper,
    )
    return (
        layer_output,
        input_grad,
        grad_norm,
        input_following[0],
        input_following[1],
        input_following[2],
        query_following[0],
        query_following[1],
        query_following[2],
        key_value_following[0],
        key_value_following[1],
        key_value_following[2],
        down_following[0],
        down_following[1],
        down_following[2],
        up_following[0],
        up_following[1],
        up_following[2],
        moe_slice,
    )


def solution(mesh):
    return jax.shard_map(
        shards,
        mesh=mesh,
        in_specs=(
            P("row", "col"),
            P("row", "col"),
            P(),
            P(),
            P(),
            P(),
            P("row", "col"),
            P("row", None),
            P("row", None),
            P("col", "row"),
            P("row", None),
            P("col", "row", None),
            P("col", None, "row"),
            P(None, "row", None),
            P(None, None, "col"),
            P(),
            P(None, "col", None),
            P(None, "row", None),
            P(None, "row", None),
            P(None, "row", None),
            P(None, None, "col"),
            P(None, None, "col"),
            P(),
            P(),
            P(None, "col", None),
            P(None, "col", None),
            P(None, "row", None),
            P(None, "row", None),
            P("row", None),
            P("row"),
            P("row", None),
            P("row", None),
        ),
        out_specs=(
            P("row", "col"),
            P("row", "col"),
            P(),
            P(None, "row", None),
            P(None, "row", None),
            P(None, "row", None),
            P(None, None, "col"),
            P(None, None, "col"),
            P(None, None, "col"),
            P(),
            P(),
            P(),
            P(None, "col", None),
            P(None, "col", None),
            P(None, "col", None),
            P(None, "row", None),
            P(None, "row", None),
            P(None, "row", None),
            P("row", "col"),
        ),
        check_vma=False,
    )
```

profile of v0, /device:TPU:0, one launch (start us, length us, event | category | flops | bytes accessed | tf_op | source)
XLA Modules:
  0.0 1639.7 jit_solution(1809053570498071689)
XLA Ops:
  11.8 11.3 all_gather.39
  36.9 9.8 all_gather.37
  49.5 43.6 %all-gather.9.cloned.1.call-done = bf16[1024,2048]{1,0:T(8,128)(2,1)} async-done(((bf16[1024,512]{1,0:T(8,128)(2,1)}), bf16[1024,2048]{1,0:T(8,128)(2,1)}) %all-gather.9.cloned.1.call-update) | async-done | bytes 4194320 | tf_op jit(solution)/shard_map/all_gather | solution.py:179
  101.5 18.5 %all-gather.11.cloned.1.call-done = bf16[8,2048,48]{1,2,0:T(8,128)(2,1)} async-done(((bf16[8,256,48]{1,2,0:T(8,128)(2,1)}), bf16[8,2048,48]{1,2,0:T(8,128)(2,1)}) %all-gather.11.cloned.1.call-update) | async-done | bytes 1572880 | tf_op jit(solution)/shard_map/all_gather | solution.py:176
  130.1 28.5 %all-gather.13.cloned.1.call-done = bf16[2048,1024]{1,0:T(8,128)(2,1)} async-done(((bf16[256,1024]{1,0:T(8,128)(2,1)}), bf16[2048,1024]{1,0:T(8,128)(2,1)}) %all-gather.13.cloned.1.call-update) | async-done | bytes 4194320 | tf_op jit(solution)/shard_map/all_gather | solution.py:169
  158.7 7.6 fusion.171
  180.6 14.7 fusion.6
  195.3 14.5 exponential_reduce_fusion
  209.9 15.2 convolution_convert_fusion.1
  225.2 9.1 convolution_convert_fusion
  235.1 11.9 all_gather.42
  248.2 20.0 %psum.70 = bf16[1024,16]{0,1:T(8,128)(2,1)S(1)} all-reduce(bf16[1024,16]{0,1:T(8,128)(2,1)S(1)} %convolution_convert_fusion.5), channel_id=1, replica_groups=mesh['row'=8,'col'=4] {'col'}, use_global_device_ids=true, to_apply=%region_10.11 | all-reduce | flops 16384 | bytes 65536 | tf_op jit(solution)/shard_map/psum | solution.py:249
  268.2 44.2 %reduce-scatter.5.cloned.1.call-done = bf16[1024,512]{1,0:T(8,128)(2,1)} async-done(((bf16[1024,2048]{1,0:T(8,128)(2,1)}), bf16[1024,512]{1,0:T(8,128)(2,1)}) %reduce-scatter.5.cloned.1.call-update) | async-done | bytes 1048592 | tf_op jit(solution)/shard_map/reduce_scatter | solution.py:251
  320.3 15.5 scatter_custom_fusion.2
  335.9 15.5 scatter_custom_fusion.3
  352.3 9.4 all_gather.46
  362.4 32.8 %all-gather.23.cloned.1.call-done = bf16[1024,2048]{1,0:T(8,128)(2,1)} async-done(((bf16[1024,512]{1,0:T(8,128)(2,1)}), bf16[1024,2048]{1,0:T(8,128)(2,1)}) %all-gather.23.cloned.1.call-update) | async-done | bytes 4194320 | tf_op jit(solution)/shard_map/all_gather | solution.py:326
  395.2 34.1 %gather_fusion.4 = bf16[4096,2048]{1,0:T(8,128)(2,1)} fusion(bf16[1024,2048]{1,0:T(8,128)(2,1)} %all-gather.23.cloned.1.call-done, s32[4096]{0:T(1024)S(1)} %bitcast_clamp_fusion), kind=kCustom, calls=%fused_computation.4 | custom fusion | bytes 33570816 | tf_op jit(solution)/shard_map/gather | solution.py:327
  429.3 46.9 %all-gather.17.cloned.1.call-done = bf16[1024,2048]{1,0:T(8,128)(2,1)} async-done(((bf16[1024,512]{1,0:T(8,128)(2,1)}), bf16[1024,2048]{1,0:T(8,128)(2,1)}) %all-gather.17.cloned.1.call-update) | async-done | bytes 4194320 | tf_op jit(solution)/shard_map/all_gather | solution.py:258
  484.9 34.8 %gather_fusion.3 = bf16[4096,2048]{1,0:T(8,128)(2,1)} fusion(bf16[1024,2048]{1,0:T(8,128)(2,1)} %fusion.23, s32[4096]{0:T(1024)S(1)} %bitcast_clamp_fusion), kind=kCustom, calls=%fused_computation.3 | custom fusion | bytes 33570816 | tf_op jit(solution)/shard_map/gather | solution.py:299
  523.3 78.8 %all-gather.19.cloned.1.call-done = bf16[4,2048,1536]{2,1,0:T(8,128)(2,1)} async-done(((bf16[4,256,1536]{2,1,0:T(8,128)(2,1)}), bf16[4,2048,1536]{2,1,0:T(8,128)(2,1)}) %all-gather.19.cloned.1.call-update) | async-done | bytes 25165840 | tf_op jit(solution)/shard_map/all_gather | solution.py:174
  602.1 35.5 %fusion.10 = f32[4,1024,1536]{2,1,0:T(8,128)} fusion(bf16[4,2048,1536]{2,1,0:T(8,128)(2,1)} %all-gather.19.cloned.1.call-done, bf16[4,1024,2048]{2,1,0:T(8,128)(2,1)} %bitcast.251, pred[4,1024]{1,0:T(4,128)(4,1)S(1)} %broadcast_compare_fusion), kind=kOutput, calls=%fused_computation.30 | convolution fusion | flops 25778192384 | bytes 67112960 | tf_op jit(solution)/shard_map/ecd,edf->ecf/dot_general | solution.py:301
  637.6 41.1 %all-gather.21.cloned.1.call-done = bf16[4,768,2048]{2,1,0:T(8,128)(2,1)} async-done(((bf16[4,768,256]{2,1,0:T(8,128)(2,1)}), bf16[4,768,2048]{2,1,0:T(8,128)(2,1)}) %all-gather.21.cloned.1.call-update) | async-done | bytes 12582928 | tf_op jit(solution)/shard_map/all_gather | solution.py:175
  678.7 32.8 %fusion.1 = (f32[4,1024]{1,0:T(4,128)S(1)}, f32[4,1024,2048]{2,1,0:T(8,128)}) fusion(bf16[4,1024,2048]{2,1,0:T(8,128)(2,1)} %bitcast.249, bf16[4,768,2048]{2,1,0:T(8,128)(2,1)} %all-gather.21.cloned.1.call-done, f32[4,1024,1536]{2,1,0:T(8,128)} %fusion.10), kind=kOutput, calls=%fused_computation.14 | convolution fusion | flops 12928937984 | bytes 88096768 | tf_op jit(solution)/shard_map/ecf,efd->ecd/dot_general | solution.py:311
  711.5 29.0 %scatter_custom_fusion.5 = f32[4096]{0:T(1024)S(1)} fusion(s32[4096]{0:T(1024)} %bitcast.264, f32[4096]{0:T(1024)S(1)} %bitcast.265, f32[]{:T(128)} %constant.278.clone.1), kind=kCustom, calls=%fused_computation.258 | custom fusion | flops 4096 | bytes 16896
  741.2 15.7 scatter_custom_fusion.4
  756.9 29.3 %fusion.15 = (bf16[4,1024,768]{2,1,0:T(8,128)(2,1)}, bf16[4,1024,768]{2,1,0:T(8,128)(2,1)}) fusion(f32[4,1024,1536]{2,1,0:T(8,128)} %fusion.10, bf16[4,768,2048]{2,1,0:T(8,128)(2,1)} %all-gather.21.cloned.1.call-done, bf16[4,1024,2048]{2,1,0:T(8,128)(2,1)} %bitcast.250, f32[4,1024]{1,0:T(4,128)S(1)} %reshape.665), kind=kOutput, calls=%fused_computation.39 | convolution fusion | flops 12954107904 | bytes 67125248 | tf_op jit(solution)/shard_map/ecd,efd->ecf/dot_general | solution.py:330
  786.2 33.9 %convolution_multiply_fusion = f32[4,1024,2048]{2,1,0:T(8,128)} fusion(bf16[4,2048,1536]{2,1,0:T(8,128)(2,1)} %all-gather.19.cloned.1.call-done, f32[4,1024]{1,0:T(4,128)S(1)} %copy-done.70, bf16[4,1024,768]{2,1,0:T(8,128)(2,1)} %get-tuple-element.103, bf16[4,1024,768]{2,1,0:T(8,128)(2,1)} %get-tuple-element.102), kind=kOutput, calls=%fused_computation.24 | convolution fusion | flops 25803358208 | bytes 71319552 | tf_op jit(solution)/shard_map/ecf,edf->ecd/dot_general | solution.py:335
  820.1 56.0 %scatter_custom_fusion.1 = f32[1024,2048]{1,0:T(8,128)} fusion(s32[4096]{0:T(1024)} %bitcast.262, f32[4096,2048]{1,0:T(8,128)} %bitcast.271, f32[]{:T(128)} %constant.278.clone.1), kind=kCustom, calls=%fused_computation.69 | custom fusion | flops 8388608 | bytes 8389120 | tf_op jit(solution)/shard_map/scatter-add | solution.py:341
  876.1 6.1 convert_element_type.223
  883.1 19.9 %psum.72 = bf16[1024,8]{0,1:T(8,128)(2,1)S(1)} all-reduce(bf16[1024,8]{0,1:T(8,128)(2,1)S(1)} %get-tuple-element.79), channel_id=1, replica_groups=mesh['row'=8,'col'=4] {'col'}, use_global_device_ids=true, to_apply=%region_29.30 | all-reduce | flops 8192 | bytes 32768 | tf_op jit(solution)/shard_map/psum | solution.py:354
  903.1 134.6 %all-reduce.10.cloned.1.call-done = bf16[1024,2048]{1,0:T(8,128)(2,1)} async-done(((bf16[1024,2048]{1,0:T(8,128)(2,1)}), bf16[1024,2048]{1,0:T(8,128)(2,1)}) %all-reduce.10.cloned.1.call-update) | async-done | bytes 4194320 | tf_op jit(solution)/shard_map/psum | solution.py:353
  1062.2 14.5 fusion.41
  1076.7 23.2 %fusion.2 = (f32[8,1024]{1,0:T(8,128)S(1)}, f32[1024,1024,8]{1,0,2:T(8,128)}) fusion(f32[1024,1024,8]{1,0,2:T(8,128)} %get-tuple-element.121, f32[8,1024]{1,0:T(8,128)S(1)} %copy-done.33, pred[1024,1024]{0,1:T(8,128)(4,1)S(1)} %copy-done.9, bf16[1024,128,1]{1,0,2:T(8,128)(2,1)S(1)} %copy-done.40, bf16[1024,8,128]{0,2,1:T(8,128)(2,1)S(1)} %bitcast.254), kind=kOutput, calls=%fused_computation.17 | convolution fusion | flops 2189418496 | bytes 70582272 | tf_op jit(solution)/shard_map/ihd,jd->hij/dot_general | solution.py:374
  1101.6 28.6 %fusion.4 = bf16[8,1024,1024]{1,2,0:T(8,128)(2,1)} fusion(f32[1024,1024,8]{1,0,2:T(8,128)} %get-tuple-element.129, f32[1024,1024,8]{1,0,2:T(8,128)} %get-tuple-element.121, f32[8,1024]{1,0:T(8,128)S(1)} %get-tuple-element.128, f32[8,1024]{1,0:T(8,128)S(1)} %copy-done.33, pred[1024,1024]{0,1:T(8,128)(4,1)S(1)} %copy-done.9), kind=kLoop, calls=%fused_computation.19 | loop fusion | flops 50331648 | bytes 85000192 | tf_op jit(solution)/shard_map/convert_element_type | solution.py:379
  1130.3 12.2 fusion.40
  1146.2 14.8 multiply_bitcast_fusion
  1180.0 6.5 fusion.173
  1197.2 22.8 %broadcast_multiply_fusion = f32[4,1024,2048]{2,1,0:T(8,128)} fusion(f32[4,1024,2048]{2,1,0:T(8,128)} %get-tuple-element.125, f32[4,1024]{1,0:T(4,128)S(1)} %copy-done.83), kind=kLoop, calls=%fused_computation.29 | loop fusion | flops 8388608 | bytes 67125248 | tf_op jit(solution)/shard_map/mul | solution.py:320
  1220.0 55.7 %scatter_custom_fusion = f32[1024,2048]{1,0:T(8,128)} fusion(s32[4096]{0:T(1024)} %bitcast.263, f32[4096,2048]{1,0:T(8,128)} %bitcast.245, f32[]{:T(128)} %constant.278.clone.1), kind=kCustom, calls=%fused_computation.71 | custom fusion | flops 8388608 | bytes 8389120 | tf_op jit(solution)/shard_map/scatter-add | solution.py:320
  1275.7 6.3 convert_element_type.218
  1288.2 68.7 %all-reduce.14.cloned.1.call-done = (bf16[1024,2048]{1,0:T(8,128)(2,1)}, bf16[1024,48]{0,1:T(8,128)(2,1)}, bf16[8,2,16,512]{3,2,1,0:T(8,128)(2,1)}) async-done(((bf16[1024,2048]{1,0:T(8,128)(2,1)}, bf16[1024,48]{0,1:T(8,128)(2,1)}, bf16[8,2,16,512]{3,2,1,0:T(8,128)(2,1)}), (bf16[1024,2048]{1,0:T(8,128)(2,1)}, bf16[1024,48]{0,1:T(8,128)(2,1)}, ...) | async-done | bytes 4554768 | tf_op jit(solution)/shard_map/psum | solution.py:431
  1363.1 6.7 convert_element_type.193
  1369.8 23.9 %reduce-scatter.11.cloned.1.call-done = bf16[8,256,16]{1,2,0:T(8,128)(2,1)} async-done(((bf16[8,2048,16]{1,2,0:T(8,128)(2,1)}), bf16[8,256,16]{1,2,0:T(8,128)(2,1)}) %reduce-scatter.11.cloned.1.call-update) | async-done | bytes 65552 | tf_op jit(solution)/shard_map/reduce_scatter | solution.py:455
  1395.1 77.7 %reduce-scatter.7.cloned.1.call-done = bf16[1024,512]{1,0:T(8,128)(2,1)} async-done(((bf16[1024,2048]{1,0:T(8,128)(2,1)}), bf16[1024,512]{1,0:T(8,128)(2,1)}) %reduce-scatter.7.cloned.1.call-update) | async-done | bytes 1048592 | tf_op jit(solution)/shard_map/reduce_scatter | solution.py:322
  1485.4 47.7 %all-reduce.12.cloned.1.call-done = (bf16[8,16,1024]{2,1,0:T(8,128)(2,1)}, bf16[8,1024,16]{1,2,0:T(8,128)(2,1)}, bf16[8,2,16,512]{3,2,1,0:T(8,128)(2,1)}) async-done(((bf16[8,16,1024]{2,1,0:T(8,128)(2,1)}, bf16[8,1024,16]{1,2,0:T(8,128)(2,1)}, bf16[8,2,16,512]{3,2,1,0:T(8,128)(2,1)}), (bf16[8,16,1024]{2,1,0:T(8,128)(2,1)}, bf16[8,1024,16]{1,2,0:T(8,128)(2,1)}, ...) | async-done | bytes 786448 | tf_op jit(solution)/shard_map/psum | solution.py:466
  1540.1 33.8 %reduce-scatter.9.cloned.1.call-done = bf16[8,256,48]{1,2,0:T(8,128)(2,1)} async-done(((bf16[8,2048,48]{1,2,0:T(8,128)(2,1)}), bf16[8,256,48]{1,2,0:T(8,128)(2,1)}) %reduce-scatter.9.cloned.1.call-update) | async-done | bytes 196624 | tf_op jit(solution)/shard_map/reduce_scatter | solution.py:452
  1581.7 39.3 %psum.79 = f32[]{:T(128)} all-reduce(f32[]{:T(128)S(6)} %add.382), channel_id=1, replica_groups=mesh['row'=8,'col'=4] {'row','col'}, use_global_device_ids=true, to_apply=%region_52.53 | all-reduce | flops 1 | bytes 8 | tf_op jit(solution)/shard_map/psum | solution.py:483
  (411 shorter events, 184.9 us)
Async XLA Ops:
  7.2 85.9 %all-gather.9.cloned.1.call-start = ((), (), s32[]{:S(2)}) async-start(), calls=%async_computation.4 | async-start | bytes 5242880 | tf_op jit(solution)/shard_map/all_gather | solution.py:179
  7.9 112.1 %all-gather.11.cloned.1.call-start = ((), (), s32[]{:S(2)}) async-start(), calls=%async_computation.5 | async-start | bytes 1769472 | tf_op jit(solution)/shard_map/all_gather | solution.py:176
  9.7 148.9 %all-gather.13.cloned.1.call-start = ((), (), s32[]{:S(2)}) async-start(), calls=%async_computation.6 | async-start | bytes 4718592 | tf_op jit(solution)/shard_map/all_gather | solution.py:169
  10.4 214.7 %all-gather.15.cloned.1.call-start = ((), (), s32[]{:S(2)}) async-start(), calls=%async_computation.7 | async-start | bytes 4718592 | tf_op jit(solution)/shard_map/all_gather | solution.py:172
  11.0 301.3 %reduce-scatter.5.cloned.1.call-start = ((), (), s32[]{:S(2)}) async-start(), calls=%async_computation.8 | async-start | bytes 5242880 | tf_op jit(solution)/shard_map/reduce_scatter | solution.py:251
  11.1 115.7 %copy-start.106 = (f32[64]{0:T(128)}, f32[64]{0:T(128)S(1)}, u32[]{:S(2)}) copy-start(f32[64]{0:T(128)S(1)} %multiply_power_fusion) | copy-start | bytes 772
  23.1 101.2 %copy-start.20 = (bf16[2048,128]{1,0:T(8,128)(2,1)}, bf16[2048,128]{1,0:T(8,128)(2,1)S(1)}, u32[]{:S(2)}) copy-start(bf16[2048,128]{1,0:T(8,128)(2,1)S(1)} %all_gather.39) | copy-start | bytes 1572868
  28.4 98.4 %copy-start.80 = (f32[1024]{0:T(1024)}, f32[1024]{0:T(1024)S(1)}, u32[]{:S(2)}) copy-start(f32[1024]{0:T(1024)S(1)} %add_convert_fusion.3) | copy-start | bytes 12292
  36.0 173.9 %copy-start.8 = (pred[1024,1024]{0,1:T(8,128)(4,1)}, pred[1024,1024]{0,1:T(8,128)(4,1)S(1)}, u32[]{:S(2)}) copy-start(pred[1024,1024]{0,1:T(8,128)(4,1)S(1)} %fusion.32) | copy-start | bytes 3145732
  48.6 130.4 %copy-start.22 = (f32[1024,64]{1,0:T(8,128)}, f32[1024,64]{1,0:T(8,128)S(1)}, u32[]{:S(2)}) copy-start(f32[1024,64]{1,0:T(8,128)S(1)} %get-tuple-element.114) | copy-start | bytes 786436
  48.6 130.4 %copy-start.24 = (f32[1024,64]{1,0:T(8,128)}, f32[1024,64]{1,0:T(8,128)S(1)}, u32[]{:S(2)}) copy-start(f32[1024,64]{1,0:T(8,128)S(1)} %get-tuple-element.115) | copy-start | bytes 786436
  225.2 87.2 %copy-start.27 = (bf16[1024,512]{1,0:T(8,128)(2,1)S(1)}, bf16[1024,512]{1,0:T(8,128)(2,1)}, u32[]{:S(2)}) copy-start(bf16[1024,512]{1,0:T(8,128)(2,1)} %param.42) | copy-start | bytes 3145732
  234.3 83.1 %copy-start.56 = (s32[1024,8]{0,1:T(8,128)S(1)}, s32[1024,8]{0,1:T(8,128)}, u32[]{:S(2)}) copy-start(s32[1024,8]{0,1:T(8,128)} %param.70) | copy-start | bytes 98308
  234.4 84.9 %copy-start.113 = (s32[2]{0:T(128)S(1)}, s32[2]{0:T(128)}, u32[]{:S(2)}) copy-start(s32[2]{0:T(128)} %constant.334) | copy-start | bytes 28
  234.4 85.0 %copy-start.112 = (s32[2]{0:T(128)S(1)}, s32[2]{0:T(128)}, u32[]{:S(2)}) copy-start(s32[2]{0:T(128)} %constant.337) | copy-start | bytes 28
  234.4 160.8 %all-gather.23.cloned.1.call-start = ((), (), s32[]{:S(2)}) async-start(), calls=%async_computation.13 | async-start | bytes 5242880 | tf_op jit(solution)/shard_map/all_gather | solution.py:326
  235.0 241.2 %all-gather.17.cloned.1.call-start = ((), (), s32[]{:S(2)}) async-start(), calls=%async_computation.9 | async-start | bytes 5242880 | tf_op jit(solution)/shard_map/all_gather | solution.py:258
  235.0 116.5 %copy-start.111 = (s32[2]{0:T(128)S(1)}, s32[2]{0:T(128)}, u32[]{:S(2)}) copy-start(s32[2]{0:T(128)} %constant.352) | copy-start | bytes 28
  235.0 116.5 %copy-start.110 = (s32[2]{0:T(128)S(1)}, s32[2]{0:T(128)}, u32[]{:S(2)}) copy-start(s32[2]{0:T(128)} %constant.355) | copy-start | bytes 28
  235.1 117.2 %copy-start.101 = (bf16[256,16]{0,1:T(8,128)(2,1)S(1)}, bf16[256,16]{0,1:T(8,128)(2,1)}, u32[]{:S(2)}) copy-start(bf16[256,16]{0,1:T(8,128)(2,1)} %param.52) | copy-start | bytes 24580
  268.2 83.5 %copy-start.64 = (bf16[1024,16]{0,1:T(8,128)(2,1)}, bf16[1024,16]{0,1:T(8,128)(2,1)S(1)}, u32[]{:S(2)}) copy-start(bf16[1024,16]{0,1:T(8,128)(2,1)S(1)} %psum.70) | copy-start | bytes 98308
  315.9 286.2 %all-gather.19.cloned.1.call-start = ((), (), s32[]{:S(2)}) async-start(), calls=%async_computation.10 | async-start | bytes 28311552 | tf_op jit(solution)/shard_map/all_gather | solution.py:174
  316.7 362.1 %all-gather.21.cloned.1.call-start = ((), (), s32[]{:S(2)}) async-start(), calls=%async_computation.11 | async-start | bytes 14155776 | tf_op jit(solution)/shard_map/all_gather | solution.py:175
  317.4 720.4 %all-reduce.10.cloned.1.call-start = ((), (), s32[]{:S(2)}) async-start(), calls=%async_computation.14 | async-start | bytes 8388608 | tf_op jit(solution)/shard_map/psum | solution.py:353
  361.7 158.0 %copy-start.53 = (bf16[2048,16]{0,1:T(8,128)(2,1)}, bf16[2048,16]{0,1:T(8,128)(2,1)S(1)}, u32[]{:S(2)}) copy-start(bf16[2048,16]{0,1:T(8,128)(2,1)S(1)} %all_gather.46) | copy-start | bytes 196612
  362.4 116.9 %copy-start.76 = (f32[2048]{0:T(1024)S(1)}, f32[2048]{0:T(1024)}, u32[]{:S(2)}) copy-start(f32[2048]{0:T(1024)} %param.45) | copy-start | bytes 24580
  523.2 114.4 %copy-start.34 = (f32[1024,8]{0,1:T(8,128)}, f32[1024,8]{0,1:T(8,128)S(1)}, u32[]{:S(2)}) copy-start(f32[1024,8]{0,1:T(8,128)S(1)} %select_reduce_fusion.1) | copy-start | bytes 98308
  523.3 114.3 %copy-start.74 = (f32[1024]{0:T(1024)}, f32[1024]{0:T(1024)S(1)}, u32[]{:S(2)}) copy-start(f32[1024]{0:T(1024)S(1)} %reduce_max.19) | copy-start | bytes 12292
  523.3 114.3 %copy-start.84 = (f32[1024]{0:T(1024)}, f32[1024]{0:T(1024)S(1)}, u32[]{:S(2)}) copy-start(f32[1024]{0:T(1024)S(1)} %fusion.103) | copy-start | bytes 12292
  876.1 161.7 %copy-start.54 = (bf16[2048,16]{0,1:T(8,128)(2,1)S(1)}, bf16[2048,16]{0,1:T(8,128)(2,1)}, u32[]{:S(2)}) copy-start(bf16[2048,16]{0,1:T(8,128)(2,1)} %copy-done.53) | copy-start | bytes 196612
  876.1 161.6 %copy-start.77 = (f32[2048]{0:T(1024)S(1)}, f32[2048]{0:T(1024)}, u32[]{:S(2)}) copy-start(f32[2048]{0:T(1024)} %param.45) | copy-start | bytes 24580
  882.3 474.7 %all-reduce.14.cloned.1.call-start = ((), (), s32[]{:S(2)}) async-start(), calls=%async_computation.18 | async-start | bytes 9109504 | tf_op jit(solution)/shard_map/psum | solution.py:431
  903.1 140.2 %copy-start.97 = (f32[1024]{0:T(1024)S(1)}, f32[1024]{0:T(1024)}, u32[]{:S(2)}) copy-start(f32[1024]{0:T(1024)} %copy-done.96) | copy-start | bytes 12292
  903.1 140.2 %copy-start.91 = (f32[1024]{0:T(1024)S(1)}, f32[1024]{0:T(1024)}, u32[]{:S(2)}) copy-start(f32[1024]{0:T(1024)} %copy-done.90) | copy-start | bytes 12292
  1190.5 203.2 %reduce-scatter.11.cloned.1.call-start = ((), (), s32[]{:S(2)}) async-start(), calls=%async_computation.16 | async-start | bytes 589824 | tf_op jit(solution)/shard_map/reduce_scatter | solution.py:455
  1197.1 275.7 %reduce-scatter.7.cloned.1.call-start = ((), (), s32[]{:S(2)}) async-start(), calls=%async_computation.12 | async-start | bytes 5242880 | tf_op jit(solution)/shard_map/reduce_scatter | solution.py:322
  1282.0 251.0 %all-reduce.12.cloned.1.call-start = ((), (), s32[]{:S(2)}) async-start(), calls=%async_computation.17 | async-start | bytes 1572864 | tf_op jit(solution)/shard_map/psum | solution.py:466
  1357.0 217.0 %reduce-scatter.9.cloned.1.call-start = ((), (), s32[]{:S(2)}) async-start(), calls=%async_computation.15 | async-start | bytes 1769472 | tf_op jit(solution)/shard_map/reduce_scatter | solution.py:452
  1363.0 112.8 %copy-start.16 = (f32[1024,512]{1,0:T(8,128)S(1)}, f32[1024,512]{1,0:T(8,128)}, u32[]{:S(2)}) copy-start(f32[1024,512]{1,0:T(8,128)} %get-tuple-element.123) | copy-start | bytes 6291460
  1363.1 116.2 %copy-start.59 = (bf16[1024,48]{0,1:T(8,128)(2,1)S(1)}, bf16[1024,48]{0,1:T(8,128)(2,1)}, u32[]{:S(2)}) copy-start(bf16[1024,48]{0,1:T(8,128)(2,1)} %get-tuple-element.85) | copy-start | bytes 294916
  1363.1 116.2 %copy-start.99 = (f32[2048]{0:T(1024)S(1)}, f32[2048]{0:T(1024)}, u32[]{:S(2)}) copy-start(f32[2048]{0:T(1024)} %param.44) | copy-start | bytes 24580
  1479.3 97.7 %copy-start.87 = (f32[1024]{0:T(1024)S(1)}, f32[1024]{0:T(1024)}, u32[]{:S(2)}) copy-start(f32[1024]{0:T(1024)} %copy-done.86) | copy-start | bytes 12292
  1485.3 136.4 %copy-start.49 = (f32[8,1024,16]{1,2,0:T(8,128)S(1)}, f32[8,1024,16]{1,2,0:T(8,128)}, u32[]{:S(2)}) copy-start(f32[8,1024,16]{1,2,0:T(8,128)} %param.58) | copy-start | bytes 1572868
  1485.3 139.2 %copy-start.55 = (f32[8,2,16,512]{3,2,1,0:T(8,128)S(1)}, f32[8,2,16,512]{3,2,1,0:T(8,128)}, u32[]{:S(2)}) copy-start(f32[8,2,16,512]{3,2,1,0:T(8,128)} %param.57) | copy-start | bytes 1572868
  1485.3 141.8 %copy-start.50 = (f32[8,16,1024]{2,1,0:T(8,128)S(1)}, f32[8,16,1024]{2,1,0:T(8,128)}, u32[]{:S(2)}) copy-start(f32[8,16,1024]{2,1,0:T(8,128)} %param.56) | copy-start | bytes 1572868
  1533.0 88.7 %copy-start.43 = (bf16[8,1024,16]{1,2,0:T(8,128)(2,1)S(1)}, bf16[8,1024,16]{1,2,0:T(8,128)(2,1)}, u32[]{:S(2)}) copy-start(bf16[8,1024,16]{1,2,0:T(8,128)(2,1)} %get-tuple-element.82) | copy-start | bytes 786436
  1533.0 91.5 %copy-start.42 = (bf16[8,2,16,512]{3,2,1,0:T(8,128)(2,1)S(1)}, bf16[8,2,16,512]{3,2,1,0:T(8,128)(2,1)}, u32[]{:S(2)}) copy-start(bf16[8,2,16,512]{3,2,1,0:T(8,128)(2,1)} %get-tuple-element.83) | copy-start | bytes 786436
  1533.0 94.1 %copy-start.41 = (bf16[8,16,1024]{2,1,0:T(8,128)(2,1)S(1)}, bf16[8,16,1024]{2,1,0:T(8,128)(2,1)}, u32[]{:S(2)}) copy-start(bf16[8,16,1024]{2,1,0:T(8,128)(2,1)} %get-tuple-element.81) | copy-start | bytes 786436
  (86 other events, 1690.2 us)
Sparse Core Ops, SparseCore 0:
  9.6 83.4 all-gather.8
  95.6 24.3 all-gather.10
  121.9 36.7 all-gather.12
  160.4 37.4 all-gather.14
  234.5 77.8 reduce-scatter.4
  313.9 81.2 all-gather.22
  396.8 79.2 all-gather.16
  478.2 123.8 all-gather.18
  604.2 74.5 all-gather.20
  882.4 155.3 all-reduce.9
  1190.6 166.3 all-reduce.13
  1360.5 33.1 reduce-scatter.10
  1396.0 76.7 reduce-scatter.6
  1476.7 56.2 all-reduce.11
  1536.2 37.7 reduce-scatter.8
where the time goes:
time: 1650 us; the launch traced here: 1640 us
  waiting for transfers between devices  725 us (44%)
  matrix products  317 us (19%)
  other arithmetic  310 us (19%)
  local copies, waits for them, and re-layouts  144 us (9%)
  blocking collectives  122 us (7%)
  between operations  21.8 us (1%)
    psum x1, waiting for transfers between devices, shards(): lax.psum(post_part.astype(jnp.bfloat16), 'col').astype(jnp.float32)  135 us
    all_gather x1, waiting for transfers between devices, shards(): lax.all_gather(expert_gate_up_weight, 'row', axis=1, tiled=True)  78.8 us
    reduce_scatter x1, waiting for transfers between devices, shards(): lax.psum_scatter(moe_part.astype(jnp.bfloat16), 'col', scatter_dimension=...  77.7 us
    psum x1, waiting for transfers between devices, shards(): lax.psum(normed_in_part.astype(jnp.bfloat16), 'col').astype(jnp.float32)  68.7 us
    scatter-add x1, other arithmetic, shards(): post_part = jnp.zeros((length, width_size), jnp.float32).at[flat_token].a...  56 us
    scatter-add x1, other arithmetic, shards(): moe_part = jnp.zeros((length, width_size), jnp.float32).at[flat_token].ad...  55.7 us
    unnamed x248, local copies, waits for them, and re-layouts  53.7 us
    psum x1, waiting for transfers between devices, shards(): lax.psum(query_gradient_share.astype(jnp.bfloat16), 'row')  47.7 us
  transfers between devices with their start and end apart: 15, of which 14 were waited for; matrix products, arithmetic and copies ran while one was open for 24% of the time, Pallas kernels for 0%

commit v1 on v0

v1 whole, which is shorter than its diff:
```python
import functools

import jax
import jax.numpy as jnp
from jax import lax
from jax.experimental import pallas as pl
from jax.experimental.pallas import tpu as pltpu
from jax.sharding import PartitionSpec as P

HEAD_WIDTH = 128
STEP = 10


norm_eps = 1e-06
rope_base = 1000000.0
beta_first = 0.9
beta_second = 0.999
adam_eps = 1e-08
decay_rate = 0.01
learning_rate_lower = 0.02
learning_rate_upper = 0.1
learning_rate_output = 0.25
clip_limit = 1.0
masked_score = -1e30
score_scale = HEAD_WIDTH ** (-0.5)
low = jnp.bfloat16
wide = jnp.float32


def contract_last(left, right):
    return lax.dot_general(left, right, (((1,), (1,)), ((), ())), preferred_element_type=wide)


def contract_leading(left, right):
    return lax.dot_general(left, right, (((0,), (0,)), ((), ())), preferred_element_type=wide)


def product(left, right):
    return jnp.dot(left, right, preferred_element_type=wide)


def rms_norm(values, gain):
    return values * lax.rsqrt(jnp.mean(values * values, axis=-1, keepdims=True) + norm_eps) * gain


def moment_update(weight, first, second, grad, rate):
    first = beta_first * first + (1.0 - beta_first) * grad
    second = beta_second * second + (1.0 - beta_second) * grad * grad
    first_hat = first / (1.0 - beta_first**STEP)
    second_hat = second / (1.0 - beta_second**STEP)
    weight = weight - rate * (first_hat / (jnp.sqrt(second_hat) + adam_eps) + decay_rate * weight)
    return (weight, first, second)


def nought(values):
    return jnp.isnan(values[0, 0].astype(wide)).astype(jnp.int32)


def held(kernel, inputs, waits):
    def run(*refs):
        return kernel(*refs[:inputs], *refs[inputs + waits :])

    return run


anywhere = pl.BlockSpec(memory_space=pl.ANY)


def project_kernel(turned, left_ref, weight_ref, thin_ref, thin_weight_ref, out_ref):
    whole = contract_last if turned else product
    total = whole(left_ref[...], weight_ref[...]) + product(thin_ref[...], thin_weight_ref[...])
    out_ref[...] = total.astype(out_ref.dtype)


def project(left, weight, thin, thin_weight, turned, dtype, waits=()):
    tokens, depth = left.shape
    cols = weight.shape[0 if turned else 1]
    rank = thin.shape[1]
    block = 512 if depth <= 2048 else 256
    if turned:
        weight_spec = pl.BlockSpec((block, depth), lambda j: (j, 0))
    else:
        weight_spec = pl.BlockSpec((depth, block), lambda j: (0, j))
    return pl.pallas_call(
        held(functools.partial(project_kernel, turned), 4, len(waits)),
        grid=(cols // block,),
        in_specs=[
            pl.BlockSpec((tokens, depth), lambda j: (0, 0)),
            weight_spec,
            pl.BlockSpec((tokens, rank), lambda j: (0, 0)),
            pl.BlockSpec((rank, block), lambda j: (0, j)),
            *[anywhere] * len(waits),
        ],
        out_specs=pl.BlockSpec((tokens, block), lambda j: (0, j)),
        out_shape=jax.ShapeDtypeStruct((tokens, cols), dtype),
        compiler_params=pltpu.CompilerParams(vmem_limit_bytes=60 << 20),
        cost_estimate=pl.CostEstimate(flops=0, bytes_accessed=0, transcendentals=0),
        name="project",
    )(left, weight, thin, thin_weight, *waits)


def shift(values, step):
    count = lax.axis_size("col")
    pairs = [(i, (i + step) % count) for i in range(count)]
    return lax.ppermute(values, "col", pairs)


def ring_gather(values):
    parts = [values]
    for _ in range(lax.axis_size("col") - 1):
        parts.append(shift(parts[-1], 1))
    return parts


def origin(k):
    count = lax.axis_size("col")
    return lax.rem(lax.axis_index("col") + count - k, count)


def in_order(parts, axis, wait=0):
    size = parts[0].shape[axis]
    shape = list(parts[0].shape)
    shape[axis] = size * len(parts)
    out = jnp.zeros(shape, parts[0].dtype)
    for k, part in enumerate(parts):
        out = lax.dynamic_update_slice_in_dim(out, part, origin(k) * size + wait, axis)
    return out


def ring_scatter(part_of):
    count = lax.axis_size("col")
    total = part_of(origin(1))
    for k in range(1, count):
        total = shift(total.astype(low), 1).astype(wide) + part_of(origin(k + 1))
    return total


def exchange(piece_of):
    count = lax.axis_size("col")
    return [piece_of(origin(0))] + [shift(piece_of(origin(count - k)), k) for k in range(1, count)]


def tree_sum(parts):
    if len(parts) == 1:
        return parts[0].astype(wide)
    return tree_sum(parts[0::2]) + tree_sum(parts[1::2])


def hop_kernel(arrives, count, *refs):
    arrived, own, out_ref = refs[1 : 1 + arrives], refs[1 + arrives : 1 + arrives + count], refs[-1]
    start = 0
    for ref in own:
        span = pl.ds(start, ref.shape[1])
        total = ref[...].astype(wide)
        if arrives:
            total = total + arrived[0][:, span].astype(wide)
        out_ref[:, span] = total.astype(out_ref.dtype)
        start += ref.shape[1]


def hop(place, arrived, own, block, dtype, waits=()):
    rows, cols = block
    across = own[0].shape[1] != cols
    step = min(rows, 256 if across else 64)
    steps = rows // step
    total = cols * len(own)

    def whole(i, p):
        return (i, 0)

    def mine(i, p):
        return (i, p[0]) if across else (p[0] * steps + i, 0)

    arrivals = () if arrived is None else (arrived,)
    return pl.pallas_call(
        held(functools.partial(hop_kernel, len(arrivals), len(own)), 1 + len(arrivals) + len(own), len(waits)),
        grid_spec=pltpu.PrefetchScalarGridSpec(
            num_scalar_prefetch=1,
            grid=(steps,),
            in_specs=[pl.BlockSpec((step, total), whole)] * len(arrivals)
            + [pl.BlockSpec((step, cols), mine)] * len(own)
            + [anywhere] * len(waits),
            out_specs=pl.BlockSpec((step, total), whole),
        ),
        out_shape=jax.ShapeDtypeStruct((rows, total), dtype),
        compiler_params=pltpu.CompilerParams(vmem_limit_bytes=60 << 20),
        name="hop",
    )(place.reshape(1), *arrivals, *own, *waits)


def sum_kernel(*refs):
    refs[-1][...] = tree_sum([ref[...] for ref in refs[:-1]]).astype(refs[-1].dtype)


def summed(parts, waits):
    shape = parts[0].shape
    return pl.pallas_call(
        held(sum_kernel, len(parts), len(waits)),
        grid=(1,),
        in_specs=[pl.BlockSpec(shape, lambda i: (0, 0))] * len(parts) + [anywhere] * len(waits),
        out_specs=pl.BlockSpec(shape, lambda i: (0, 0)),
        out_shape=jax.ShapeDtypeStruct(shape, parts[0].dtype),
        compiler_params=pltpu.CompilerParams(vmem_limit_bytes=60 << 20),
        name="summed",
    )(*parts, *waits)


def head_forward(proj, gain, cos, sin):
    inv = lax.rsqrt(jnp.mean(proj * proj, axis=-1, keepdims=True) + norm_eps)
    scaled = proj * inv * gain
    return scaled * cos + pltpu.roll(scaled, HEAD_WIDTH // 2, 1) * sin, inv


def attend_kernel(share, proj_ref, cos_ref, sin_ref, gain_ref, bias_ref, key_ref, value_ref,
                  out_ref, lse_ref, value_t):
    @pl.when(lax.rem(pl.program_id(0), share) == 0)
    def _():
        value_t[...] = value_ref[...].T

    query, _ = head_forward(proj_ref[...], gain_ref[...], cos_ref[...], sin_ref[...])
    scores = contract_last(key_ref[...], query.astype(low)) * score_scale + bias_ref[...]
    top = jnp.max(scores, axis=0, keepdims=True)
    probs = jnp.exp(scores - top)
    total = jnp.sum(probs, axis=0, keepdims=True)
    mixed = product(value_t[...], probs.astype(low)) / total
    out_ref[...] = mixed.T.astype(low)
    lse_ref[0] = top + jnp.log(total)


def attend_back_kernel(share, proj_ref, cos_ref, sin_ref, gain_ref, bias_ref, key_ref, value_ref,
                       lse_ref, branch_ref, weight_ref, middle_ref, down_ref,
                       out_ref, key_grad_ref, value_grad_ref, key_t):
    @pl.when(lax.rem(pl.program_id(0), share) == 0)
    def _():
        key_t[...] = key_ref[...].T
        key_grad_ref[...] = jnp.zeros_like(key_grad_ref)
        value_grad_ref[...] = jnp.zeros_like(value_grad_ref)

    proj, gain, cos, sin = proj_ref[...], gain_ref[...], cos_ref[...], sin_ref[...]
    query, inv = head_forward(proj, gain, cos, sin)
    query = query.astype(low)
    grad = contract_last(branch_ref[...], weight_ref[...])
    grad = (grad + product(middle_ref[...], down_ref[...])).astype(low)
    scores = contract_last(key_ref[...], query) * score_scale + bias_ref[...]
    probs = jnp.exp(scores - lse_ref[0])
    probs_grad = contract_last(value_ref[...], grad)
    delta = jnp.sum(probs * probs_grad, axis=0, keepdims=True)
    scores_grad = (probs * (probs_grad - delta)).astype(low)
    value_grad_ref[...] += product(probs.astype(low), grad)
    key_grad_ref[...] += product(scores_grad, query) * score_scale
    rotated = product(key_t[...], scores_grad).T * score_scale
    scaled = rotated * cos + pltpu.roll(rotated * sin, HEAD_WIDTH // 2, 1)
    scaled = scaled * gain
    slope = jnp.mean(scaled * proj, axis=-1, keepdims=True)
    out_ref[...] = (inv * scaled - proj * (inv * inv * inv * slope)).astype(low)


def head_specs(tokens, length, first, share, kv_total):
    def head(h):
        return (0, first + h)

    def fixed(h):
        return (0, 0)

    return [
        pl.BlockSpec((tokens, HEAD_WIDTH), head),
        pl.BlockSpec((tokens, HEAD_WIDTH), fixed),
        pl.BlockSpec((tokens, HEAD_WIDTH), fixed),
        pl.BlockSpec((1, HEAD_WIDTH), fixed),
        pl.BlockSpec((length, tokens), fixed),
        pl.BlockSpec((length, HEAD_WIDTH), lambda h: (0, (first + h) // share)),
        pl.BlockSpec((length, HEAD_WIDTH), lambda h: (0, kv_total + (first + h) // share)),
    ]


def attend_cost(products, tokens, length, heads):
    return pl.CostEstimate(
        flops=4 * products * tokens * length * heads * HEAD_WIDTH,
        bytes_accessed=8 * tokens * heads * HEAD_WIDTH,
        transcendentals=tokens * length * heads,
    )


def attend(proj, cos, sin, gain, bias, keys_values):
    tokens, cols = proj.shape
    length, heads = keys_values.shape[0], cols // HEAD_WIDTH
    kv_total = keys_values.shape[1] // (2 * HEAD_WIDTH)
    share = heads // kv_total
    return pl.pallas_call(
        functools.partial(attend_kernel, share),
        grid=(heads,),
        in_specs=head_specs(tokens, length, 0, share, kv_total),
        out_specs=[
            pl.BlockSpec((tokens, HEAD_WIDTH), lambda h: (0, h)),
            pl.BlockSpec((1, 1, tokens), lambda h: (h, 0, 0)),
        ],
        scratch_shapes=[pltpu.VMEM((HEAD_WIDTH, length), low)],
        out_shape=[
            jax.ShapeDtypeStruct((tokens, cols), low),
            jax.ShapeDtypeStruct((heads, 1, tokens), wide),
        ],
        compiler_params=pltpu.CompilerParams(vmem_limit_bytes=60 << 20),
        cost_estimate=attend_cost(3, tokens, length, heads),
        name="attend",
    )(proj, cos, sin, gain, bias, keys_values, keys_values)


def attend_back(part, parts, proj, cos, sin, gain, bias, keys_values, lse, branch, weight, middle, down,
                filled, waits):
    tokens, length = proj.shape[0], keys_values.shape[0]
    total, width, rank = proj.shape[1] // HEAD_WIDTH, branch.shape[1], middle.shape[1]
    kv_total = keys_values.shape[1] // (2 * HEAD_WIDTH)
    share, heads = total // kv_total, total // parts
    first = part * heads

    def fixed(h):
        return (0, 0)

    def head(h):
        return (0, first + h)

    def kv_head(h):
        return (0, (first + h) // share)

    return pl.pallas_call(
        held(functools.partial(attend_back_kernel, share), 12, len(filled) + len(waits)),
        grid=(heads,),
        in_specs=head_specs(tokens, length, first, share, kv_total)
        + [
            pl.BlockSpec((1, 1, tokens), lambda h: (first + h, 0, 0)),
            pl.BlockSpec((tokens, width), fixed),
            pl.BlockSpec((HEAD_WIDTH, width), lambda h: (first + h, 0)),
            pl.BlockSpec((tokens, rank), fixed),
            pl.BlockSpec((rank, HEAD_WIDTH), head),
            *[anywhere] * (len(filled) + len(waits)),
        ],
        out_specs=[
            pl.BlockSpec((tokens, HEAD_WIDTH), head),
            pl.BlockSpec((length, HEAD_WIDTH), kv_head),
            pl.BlockSpec((length, HEAD_WIDTH), kv_head),
        ],
        scratch_shapes=[pltpu.VMEM((HEAD_WIDTH, length), low)],
        out_shape=[
            jax.ShapeDtypeStruct(proj.shape, low),
            jax.ShapeDtypeStruct((length, kv_total * HEAD_WIDTH), wide),
            jax.ShapeDtypeStruct((length, kv_total * HEAD_WIDTH), wide),
        ],
        input_output_aliases={12 + i: i for i in range(len(filled))},
        compiler_params=pltpu.CompilerParams(vmem_limit_bytes=60 << 20),
        cost_estimate=pl.CostEstimate(flops=0, bytes_accessed=0, transcendentals=0),
        name="attend_back",
    )(proj, cos, sin, gain, bias, keys_values, keys_values, lse, branch, weight, middle, down, *filled, *waits)


def experts_kernel(place_ref, normed_ref, back_ref, weight_ref, gate_ref, up_ref, down_ref,
                   post_ref, out_ref, out_sum):
    e = pl.program_id(0)
    width = normed_ref.shape[1]

    @pl.when(e == 0)
    def _():
        post_ref[...] = jnp.zeros_like(post_ref)
        out_sum[...] = jnp.zeros_like(out_sum)

    normed = normed_ref[...]
    gate = product(normed, gate_ref[0])
    up = product(normed, up_ref[0])
    back = back_ref[...]
    weights = weight_ref[...]
    lane = lax.broadcasted_iota(jnp.int32, weights.shape, 1)
    weight = jnp.sum(jnp.where(lane == e, weights, 0.0), axis=1, keepdims=True)
    sig = jax.nn.sigmoid(gate)
    act = gate * sig
    inner = act * up
    lane = lax.broadcasted_iota(jnp.int32, (normed.shape[0], HEAD_WIDTH), 1)
    gate_sum = jnp.sum(inner * back, axis=1, keepdims=True)
    post_ref[:, width:] += jnp.where(lane == place_ref[1] + e, gate_sum, 0.0)
    back = back * weight
    gate_grad = (back * up * (sig + act * (1.0 - sig))).astype(low)
    up_grad = (back * act).astype(low)
    out_sum[...] += product((inner * weight).astype(low), down_ref[...])
    post_ref[:, :width] += contract_last(gate_grad, gate_ref[0]) + contract_last(up_grad, up_ref[0])

    @pl.when(e == pl.num_programs(0) - 1)
    def _():
        out_ref[...] = out_sum[...].astype(low)


def experts(chunk, first_expert, tokens, normed, back, weights, gate_up, down, mixture, waits):
    filled = () if mixture is None else (mixture,)
    waits = (*filled, *waits)
    width = normed.shape[1]
    count, inner_width = gate_up.shape[0], gate_up.shape[2] // 2
    return pl.pallas_call(
        held(experts_kernel, 7, len(waits)),
        grid_spec=pltpu.PrefetchScalarGridSpec(
            num_scalar_prefetch=1,
            grid=(count,),
            in_specs=[
                pl.BlockSpec((tokens, width), lambda e, p: (p[0], 0)),
                pl.BlockSpec((tokens, inner_width), lambda e, p: (p[0], e)),
                pl.BlockSpec((tokens, count), lambda e, p: (p[0], 0)),
                pl.BlockSpec((1, width, inner_width), lambda e, p: (e, 0, 0)),
                pl.BlockSpec((1, width, inner_width), lambda e, p: (e, 0, 1)),
                pl.BlockSpec((inner_width, width), lambda e, p: (e, 0)),
                *[anywhere] * len(waits),
            ],
            out_specs=[
                pl.BlockSpec((tokens, width + HEAD_WIDTH), lambda e, p: (0, 0)),
                pl.BlockSpec((tokens, width), lambda e, p: (p[0], 0)),
            ],
            scratch_shapes=[pltpu.VMEM((tokens, width), wide)],
        ),
        out_shape=[
            jax.ShapeDtypeStruct((tokens, width + HEAD_WIDTH), wide),
            jax.ShapeDtypeStruct(normed.shape, low),
        ],
        input_output_aliases={7: 1} if filled else {},
        compiler_params=pltpu.CompilerParams(vmem_limit_bytes=60 << 20),
        cost_estimate=pl.CostEstimate(
            flops=10 * tokens * width * count * inner_width,
            bytes_accessed=6 * width * count * inner_width,
            transcendentals=tokens * count * inner_width,
        ),
        name="experts",
    )(jnp.stack([chunk, first_expert]), normed, back, weights, gate_up, gate_up, down, *waits)


def settle_kernel(arrived_ref, post_ref, probs_ref, router_ref, resid_ref, gain_ref, cot_ref, up_ref,
                  grad_ref, branch_ref, middle_ref):
    width = resid_ref.shape[1]
    gate_grad = arrived_ref[:, width:].astype(wide) + post_ref[:, width:]
    probs = probs_ref[...]
    logits_grad = probs * (gate_grad - jnp.sum(probs * gate_grad, axis=1, keepdims=True))
    grad = arrived_ref[:, :width].astype(wide) + post_ref[:, :width]
    grad = (grad + product(logits_grad.astype(low), router_ref[...])) * gain_ref[...]
    resid = resid_ref[...]
    inv = lax.rsqrt(jnp.mean(resid * resid, axis=1, keepdims=True) + norm_eps)
    slope = jnp.mean(grad * resid, axis=1, keepdims=True)
    grad = cot_ref[...].astype(wide) + inv * grad - resid * (inv * inv * inv * slope)
    grad_ref[...] = grad
    branch = grad.astype(low)
    branch_ref[...] = branch
    middle_ref[...] = contract_last(branch, up_ref[...]).astype(low)


def settle(arrived, post, probs, router, resid, gain, cot, up):
    tokens, width = resid.shape
    rank = up.shape[0]
    block = min(tokens, 64)
    lanes = arrived.shape[1] - width

    def rows(cols):
        return pl.BlockSpec((block, cols), lambda i: (i, 0))

    def whole(*shape):
        return pl.BlockSpec(shape, lambda i: (0, 0))

    return pl.pallas_call(
        settle_kernel,
        grid=(tokens // block,),
        in_specs=[
            rows(width + lanes),
            rows(width + lanes),
            rows(lanes),
            whole(lanes, width),
            rows(width),
            whole(1, width),
            rows(width),
            whole(rank, width),
        ],
        out_specs=[rows(width), rows(width), rows(rank)],
        out_shape=[
            jax.ShapeDtypeStruct((tokens, width), wide),
            jax.ShapeDtypeStruct((tokens, width), low),
            jax.ShapeDtypeStruct((tokens, rank), low),
        ],
        compiler_params=pltpu.CompilerParams(vmem_limit_bytes=60 << 20),
        cost_estimate=pl.CostEstimate(flops=0, bytes_accessed=0, transcendentals=0),
        name="settle",
    )(arrived, post, probs, router, resid, gain, cot, up)


def update_kernel(rates, count, slot_ref, square_ref, *refs):
    size = len(rates)
    whole, own = refs[:count], refs[count : count + size]
    state = refs[count + size : count + 4 * size]
    norm_ref = refs[count + 4 * size]
    outs = refs[count + 4 * size + 1 : count + 7 * size + 1]
    sums, factor_ref = refs[count + 7 * size + 1 : -1], refs[-1]
    now = pl.program_id(0)

    @pl.when(now == 0)
    def _():
        total = square_ref[...]
        for trees_ref, sum_ref in zip((*whole, *own), sums):
            sum_ref[...] = jnp.zeros_like(sum_ref)

            def tree(t, carry, trees_ref=trees_ref, sum_ref=sum_ref):
                at = slot_ref[t]
                sum_ref[at] += trees_ref[t].astype(wide)
                return carry

            lax.fori_loop(0, trees_ref.shape[0], tree, 0)
        for sum_ref in sums[:count]:

            def square(s, carry, sum_ref=sum_ref):
                part = jnp.sum(sum_ref[s] * sum_ref[s], axis=0, keepdims=True)
                return carry + jnp.sum(part, axis=1, keepdims=True)

            total = lax.fori_loop(0, sum_ref.shape[0], square, total)
        norm = jnp.sqrt(total)
        norm_ref[...] = norm
        factor_ref[...] = jnp.minimum(1.0, clip_limit / (norm + 1e-06))

    factor = factor_ref[...]
    for i, rate in enumerate(rates):
        weight, first, second = (ref[0] for ref in state[3 * i : 3 * i + 3])
        new = moment_update(weight, first, second, sums[count + i][now] * factor, rate)
        for ref, value in zip(outs[3 * i : 3 * i + 3], new):
            ref[0] = value


def update(slots, square, whole, own, states, rates):
    state = [array for triple in states for array in triple]
    adapters = state[0].shape[0]

    def all_of(array):
        return pl.BlockSpec(array.shape, lambda s: (0,) * array.ndim)

    def one_of(array):
        return pl.BlockSpec((1, *array.shape[1:]), lambda s: (s, 0, 0))

    out = pl.pallas_call(
        functools.partial(update_kernel, tuple(rates), len(whole)),
        grid=(adapters,),
        in_specs=[pl.BlockSpec(memory_space=pltpu.SMEM)]
        + [all_of(a) for a in (square, *whole, *own)]
        + [one_of(a) for a in state],
        out_specs=[all_of(square)] + [one_of(a) for a in state],
        out_shape=[jax.ShapeDtypeStruct((1, 1), wide)]
        + [jax.ShapeDtypeStruct(a.shape, wide) for a in state],
        scratch_shapes=[pltpu.VMEM((adapters, *a.shape[1:]), wide) for a in (*whole, *own)]
        + [pltpu.VMEM((1, 1), wide)],
        compiler_params=pltpu.CompilerParams(vmem_limit_bytes=60 << 20),
        name="update",
    )(slots, square, *whole, *own, *state)
    return out[0], [out[1 + 3 * i : 4 + 3 * i] for i in range(len(states))]


def tree_layout(lengths, parents, token_count, first, count):
    nodes = lengths.shape[0]
    node_ids = jnp.arange(nodes, dtype=jnp.int32)
    node_ends = jnp.cumsum(lengths, dtype=jnp.int32)
    node_starts = node_ends - lengths
    parent_hot = parents[:, None] == node_ids[None, :]
    eye = node_ids[:, None] == node_ids[None, :]
    grand_hot = jnp.any(parent_hot[:, :, None] & parent_hot[None, :, :], axis=1)
    ancestor = eye | parent_hot | grand_hot
    before = jnp.sum(jnp.where(ancestor & ~eye, lengths[None, :], 0), axis=1, dtype=jnp.int32)

    def hot_of(tokens):
        return (tokens[:, None] >= node_starts[None, :]) & (tokens[:, None] < node_ends[None, :])

    keys = jnp.arange(token_count, dtype=jnp.int32)
    queries = first + jnp.arange(count, dtype=jnp.int32)
    query_hot = hot_of(queries)
    positions = queries + jnp.sum(
        jnp.where(query_hot, (before - node_starts)[None, :], 0), axis=1, dtype=jnp.int32
    )
    reach = product(query_hot.astype(low), ancestor.astype(low)).astype(low)
    reachable = contract_last(hot_of(keys).astype(low), reach) > 0.5
    allowed = reachable & (keys[:, None] <= queries[None, :])
    return positions, jnp.where(allowed, 0.0, masked_score)


def shards(
    inputs,
    cotangent,
    attention_norm_gain,
    expert_norm_gain,
    query_norm_gain,
    key_norm_gain,
    frozen_query_weight,
    frozen_key_weight,
    frozen_value_weight,
    frozen_output_weight,
    frozen_router_weight,
    expert_gate_up_weight,
    expert_down_weight,
    adapter_input_down,
    adapter_query_up,
    adapter_key_value_up,
    adapter_output_down,
    adapter_output_up,
    input_first_moment,
    input_second_moment,
    query_first_moment,
    query_second_moment,
    key_value_first_moment,
    key_value_second_moment,
    output_down_first_moment,
    output_down_second_moment,
    output_up_first_moment,
    output_up_second_moment,
    routes,
    tree_adapter_index,
    tree_node_length,
    parents,
):
    col_count = lax.axis_size("col")
    row_count = lax.axis_size("row")
    col_index = lax.axis_index("col")
    row_index = lax.axis_index("row")
    length, col_width = inputs.shape
    width = col_width * col_count
    tokens = length // col_count
    first_token = col_index * tokens
    row_width = frozen_key_weight.shape[0]
    group_cols = frozen_query_weight.shape[1]
    kv_total = frozen_key_weight.shape[1] // HEAD_WIDTH
    kv_cols = kv_total * HEAD_WIDTH
    rank = adapter_query_up.shape[1]
    adapters = adapter_input_down.shape[0]
    local_experts = expert_gate_up_weight.shape[0]
    expert_total = frozen_router_weight.shape[1]
    inner_width = expert_down_weight.shape[1]
    slot = tree_adapter_index[0]

    def gather_rows(values, axis):
        return lax.all_gather(values, "row", axis=axis, tiled=True)

    local_inner = local_experts * inner_width
    first = gather_rows(
        jnp.concatenate(
            [
                expert_down_weight.reshape(local_inner, row_width),
                adapter_input_down.transpose(0, 2, 1).reshape(-1, row_width).astype(low),
                adapter_output_up.transpose(0, 2, 1).reshape(-1, row_width).astype(low),
                frozen_router_weight.T,
                jnp.broadcast_to(slot.astype(low), (16, row_width)),
                frozen_key_weight.T,
                frozen_value_weight.T,
            ]
        ),
        1,
    )
    in_start = local_inner
    up_start = in_start + adapters * 3 * rank
    router_start = up_start + adapters * rank
    slot_start = router_start + expert_total
    kv_start = slot_start + 16
    down_input = lax.dynamic_slice_in_dim(first, in_start + slot * 3 * rank, 3 * rank, 0)
    up_output = lax.dynamic_slice_in_dim(first, up_start + slot * rank, rank, 0)
    router = first[router_start:slot_start]
    slots = first[slot_start, ::row_width].astype(jnp.int32)
    key_value_weight = first[kv_start:]
    query_weight = gather_rows(in_order(ring_gather(frozen_query_weight), 1), 0)
    out_weight = gather_rows(in_order(ring_gather(frozen_output_weight), 0), 1)
    gate_up_weight = gather_rows(expert_gate_up_weight, 1)
    head_adapters = in_order(
        ring_gather(
            jnp.concatenate([adapter_query_up[slot], adapter_output_down[slot].T]).astype(low)
        ),
        1,
    )
    query_raise = head_adapters[:rank]
    down_output = head_adapters[rank:]
    key_value_raise = adapter_key_value_up[slot].astype(low)

    pieces = exchange(lambda c: lax.dynamic_slice_in_dim(inputs, c * tokens, tokens, 0))
    hidden_input = in_order(pieces, 1).astype(wide)
    cot_full = in_order(ring_gather(cotangent), 1)
    cot_own = lax.dynamic_slice_in_dim(cot_full, first_token, tokens, 0)
    positions, bias = tree_layout(tree_node_length[0], parents[0], length, first_token, tokens)

    def norm_in(values):
        return rms_norm(values, attention_norm_gain)

    normalized, norm_in_back = jax.vjp(norm_in, hidden_input)
    normalized = normalized.astype(low)
    middle = contract_last(normalized, down_input).astype(low)
    half = HEAD_WIDTH // 2
    frequency = rope_base ** (-jnp.arange(half, dtype=wide) / half)
    angles = positions.astype(wide)[:, None] * frequency[None, :]
    cos = jnp.concatenate([jnp.cos(angles)] * 2, axis=1)
    sin = jnp.concatenate([-jnp.sin(angles), jnp.sin(angles)], axis=1)

    def shape_keys(proj):
        parts = []
        for head in range(kv_total):
            scaled = rms_norm(proj[:, head * HEAD_WIDTH : (head + 1) * HEAD_WIDTH], key_norm_gain)
            turned = jnp.concatenate([scaled[:, half:], scaled[:, :half]], axis=1)
            parts.append(scaled * cos + turned * sin)
        return jnp.concatenate(parts, axis=1)

    key_value_proj = contract_last(normalized, key_value_weight)
    key_proj = key_value_proj[:, :kv_cols] + product(middle[:, rank : 2 * rank], key_value_raise[0])
    value_proj = key_value_proj[:, kv_cols:] + product(middle[:, 2 * rank :], key_value_raise[1])
    key_rot, keys_back = jax.vjp(shape_keys, key_proj)
    keys_values = in_order(
        ring_gather(jnp.concatenate([key_rot.astype(low), value_proj.astype(low)], axis=1)), 0
    )
    query_gain = query_norm_gain[None, :]
    proj = project(normalized, query_weight, middle[:, :rank], query_raise, False, wide)
    heads, totals = attend(proj, cos, sin, query_gain, bias, keys_values)
    inner_back = contract_last(cot_full, first[:local_inner])
    middle_output = contract_last(heads, down_output).astype(low)
    resid = hidden_input + project(
        heads, out_weight, middle_output, up_output, False, wide, (inner_back,)
    )

    resid_full = in_order(ring_gather(resid.astype(low)), 0)
    normed_post = rms_norm(resid_full.astype(wide), expert_norm_gain).astype(low)
    logits = contract_last(normed_post, router)
    expert_ids = jnp.arange(expert_total, dtype=jnp.int32)
    chosen = jnp.any(routes[:, :, None] == expert_ids[None, None, :], axis=1)
    shifted = logits - jnp.max(jnp.where(chosen, logits, -jnp.inf), axis=1, keepdims=True)
    raised = jnp.where(chosen, jnp.exp(jnp.where(chosen, shifted, 0.0)), 0.0)
    gate_probs = raised / jnp.sum(raised, axis=1, keepdims=True)
    local_probs = lax.dynamic_slice_in_dim(gate_probs, col_index * local_experts, local_experts, 1)
    own_probs = jnp.pad(
        lax.dynamic_slice_in_dim(gate_probs, first_token, tokens, 0),
        ((0, 0), (0, HEAD_WIDTH - expert_total)),
    )
    router_rows = jnp.pad(router, ((0, HEAD_WIDTH - expert_total), (0, 0)))
    local_in = down_input[rank:]
    mixture, arrived, sent = None, None, ()
    for k in range(col_count):
        post, mixture = experts(
            origin(k + 1),
            col_index * local_experts,
            tokens,
            normed_post,
            inner_back,
            local_probs,
            gate_up_weight,
            first,
            mixture,
            sent if k < col_count - 1 else (*sent, own_probs, router_rows, cot_own, local_in),
        )
        if k < col_count - 1:
            sent = ((post if k == 0 else arrived.astype(wide) + post).astype(low),)
            arrived = shift(sent[0], 1)

    def mixture_hop(k, arrived, dtype, *waits):
        return hop(origin(k), arrived, (mixture,), (length, col_width), dtype, waits)

    resid_grad, branch_grad, mid_out_grad = settle(
        arrived, post, own_probs, router_rows, resid, expert_norm_gain[None, :], cot_own, up_output
    )
    mixture_sent = mixture_hop(1, None, low, arrived)
    filled = ()
    for part in range(4):
        waits = ()
        if part in (1, 3):
            mixture_sent = mixture_hop(part // 2 + 2, shift(mixture_sent, 1), low, filled[0])
            waits = (mixture_sent,)
        filled = attend_back(
            part,
            4,
            proj,
            cos,
            sin,
            query_gain,
            bias,
            keys_values,
            totals,
            branch_grad,
            out_weight,
            mid_out_grad,
            down_output,
            filled,
            waits,
        )
    query_grad, *kv_grads = filled
    mid_query_grad = contract_last(query_grad, query_raise).astype(low)
    mixture_arrived = shift(mixture_sent, 1)

    def kv_hop(k, arrived, dtype, *waits):
        return hop(origin(k), arrived, kv_grads, (tokens, kv_cols), dtype, waits)

    kv_sent = kv_hop(1, None, low, mixture_arrived)
    normed_query_grad = project(query_grad, query_weight, mid_query_grad, down_input[:rank], True, wide, (kv_sent,))
    for k in range(2, col_count):
        kv_sent = kv_hop(k, shift(kv_sent, 1), low, normed_query_grad)
        if k == 2:
            kv_second = kv_sent
    kv_own = kv_hop(col_count, shift(kv_sent, 1), wide)
    for k in range(3, col_count):
        last = k == col_count - 1
        mixture_sent = mixture_hop(k + 1, mixture_arrived, wide if last else low)
        mixture_arrived = None if last else shift(mixture_sent, 1)
    moe_slice = mixture_sent
    resid_slice = lax.dynamic_slice_in_dim(resid_full, col_index * col_width, col_width, 1)
    layer_output = resid_slice.astype(wide) + moe_slice
    key_grad = keys_back(kv_own[:, :kv_cols])[0].astype(low)
    value_grad = kv_own[:, kv_cols:].astype(low)
    kv_proj_grad = jnp.concatenate([key_grad, value_grad], axis=1)
    mid_kv_grad = jnp.concatenate(
        [
            contract_last(key_grad, key_value_raise[0]),
            contract_last(value_grad, key_value_raise[1]),
        ],
        axis=1,
    ).astype(low)
    mid_grad = jnp.concatenate([mid_query_grad, mid_kv_grad], axis=1)
    normed_in_grad = (
        normed_query_grad
        + product(kv_proj_grad, key_value_weight)
        + product(mid_kv_grad, local_in)
    )
    input_grad_own = (resid_grad + norm_in_back(normed_in_grad)[0]).astype(low)
    def of_all(part):
        return tree_sum([part] + [shift(part, k) for k in range(1, col_count)])

    up_part = contract_leading(middle_output, branch_grad).astype(low).reshape(-1, group_cols)
    head_part = jnp.concatenate(
        [contract_leading(middle[:, :rank], query_grad), contract_leading(mid_out_grad, heads)]
    ).astype(low)

    def head_piece(c):
        piece = lax.dynamic_slice_in_dim(head_part, c * group_cols, group_cols, 1)
        return jnp.concatenate([piece, up_part])

    head_trees = lax.all_gather(summed(exchange(head_piece), (kv_second,)), "row", axis=0)
    slot_hot = (slots[None, :] == jnp.arange(adapters, dtype=jnp.int32)[:, None]).astype(low)
    up_trees = head_trees[:, 2 * rank :].reshape(-1, rank, width)
    head_own = head_trees[:, : 2 * rank]
    head_square = jnp.einsum("st,tij->sij", slot_hot, head_own, preferred_element_type=wide)
    head_square = jnp.full((1, HEAD_WIDTH), jnp.sum(head_square * head_square))
    head_square = of_all(head_square)[:, :1]
    wait = nought(head_square)
    pieces = exchange(lambda c: lax.dynamic_slice_in_dim(input_grad_own, c * col_width + wait, col_width, 1))
    input_grad = in_order(pieces, 0).astype(wide)

    kv_portion = jnp.concatenate(
        [
            contract_leading(middle[:, rank : 2 * rank], key_grad),
            contract_leading(middle[:, 2 * rank :], value_grad),
        ]
    )
    in_portion = contract_leading(mid_grad, normalized)
    last_part = of_all(jnp.concatenate([in_portion, kv_portion.reshape(-1, width)]).astype(low))
    last_trees = lax.all_gather(last_part.astype(low), "row", axis=0)
    row_start = row_index * row_width
    in_own = lax.dynamic_slice_in_dim(last_trees[:, : 3 * rank], row_start, row_width, 2)
    up_own = lax.dynamic_slice_in_dim(up_trees, row_start, row_width, 2)
    kv_own_trees = last_trees[:, 3 * rank :].reshape(-1, 2 * rank, kv_cols)

    def flip(array):
        return array.transpose(0, 2, 1)

    def rows_of(array):
        return array.reshape(adapters, 2 * rank, kv_cols)

    grad_norm, following = update(
        slots,
        head_square,
        (up_trees, last_trees),
        (head_own[:, :rank], head_own[:, rank:], up_own, in_own, kv_own_trees),
        (
            (adapter_query_up, query_first_moment, query_second_moment),
            tuple(map(flip, (adapter_output_down, output_down_first_moment, output_down_second_moment))),
            tuple(map(flip, (adapter_output_up, output_up_first_moment, output_up_second_moment))),
            tuple(map(flip, (adapter_input_down, input_first_moment, input_second_moment))),
            tuple(map(rows_of, (adapter_key_value_up, key_value_first_moment, key_value_second_moment))),
        ),
        (
            learning_rate_upper,
            learning_rate_output,
            learning_rate_upper,
            learning_rate_lower,
            learning_rate_upper,
        ),
    )
    query_following, down_following, up_following, input_following, key_value_following = following
    return (
        layer_output,
        input_grad,
        grad_norm.reshape(()),
        *map(flip, input_following),
        *query_following,
        *(a.reshape(adapter_key_value_up.shape) for a in key_value_following),
        *map(flip, down_following),
        *map(flip, up_following),
        moe_slice,
    )


def solution(mesh):
    return jax.shard_map(
        shards,
        mesh=mesh,
        in_specs=(
            P("row", "col"),
            P("row", "col"),
            P(),
            P(),
            P(),
            P(),
            P("row", "col"),
            P("row", None),
            P("row", None),
            P("col", "row"),
            P("row", None),
            P("col", "row", None),
            P("col", None, "row"),
            P(None, "row", None),
            P(None, None, "col"),
            P(),
            P(None, "col", None),
            P(None, "row", None),
            P(None, "row", None),
            P(None, "row", None),
            P(None, None, "col"),
            P(None, None, "col"),
            P(),
            P(),
            P(None, "col", None),
            P(None, "col", None),
            P(None, "row", None),
            P(None, "row", None),
            P("row", None),
            P("row"),
            P("row", None),
            P("row", None),
        ),
        out_specs=(
            P("row", "col"),
            P("row", "col"),
            P(),
            P(None, "row", None),
            P(None, "row", None),
            P(None, "row", None),
            P(None, None, "col"),
            P(None, None, "col"),
            P(None, None, "col"),
            P(),
            P(),
            P(),
            P(None, "col", None),
            P(None, "col", None),
            P(None, "col", None),
            P(None, "row", None),
            P(None, "row", None),
            P(None, "row", None),
            P("row", "col"),
        ),
        check_vma=False,
    )
```

time: 1650 us -> 818 us (0.50)
  waiting for transfers between devices: 725 us -> 302 us
  Pallas kernels: 0 us -> 292 us
  matrix products: 317 us -> 40.3 us
  other arithmetic: 310 us -> 35.5 us
  blocking collectives: 122 us -> 0 us
  local copies, waits for them, and re-layouts: 144 us -> 69.5 us
  starting transfers between devices: 0.81 us -> 50.7 us
    pallas_call x0 -> x23, Pallas kernels: none -> 292 us  [the longest x4 99.5 us: experts(): pl.pallas_call(held(experts_kernel, 7, len(waits)), grid_spec=pltpu.Prefe...]
    dot_general x38 -> x20, matrix products: 317 us -> 40.3 us  [the longest x9 29.6 us: contract_last(): lax.dot_general(left, right, (((1,), (1,)), ((), ())), preferred_element_...]
    ppermute x0 -> x42, waiting for transfers between devices: none -> 266 us  [shift(): return lax.ppermute(values, 'col', pairs)]
    all_gather x8 -> x6, waiting for transfers between devices: 290 us -> 36.2 us  [the longest x4 36.2 us: gather_rows(): return lax.all_gather(values, 'row', axis=axis, tiled=True)]
    psum x3 -> x0, waiting for transfers between devices: 251 us -> none  [the longest x1 135 us: shards(): lax.psum(post_part.astype(jnp.bfloat16), 'col').astype(jnp.float32)]
    reduce_scatter x4 -> x0, waiting for transfers between devices: 180 us -> none  [the longest x1 77.7 us: shards(): lax.psum_scatter(moe_part.astype(jnp.bfloat16), 'col', scatter_dimension=...]
    scatter-add x2 -> x0, other arithmetic: 112 us -> none  [the longest x1 56 us: shards(): post_part = jnp.zeros((length, width_size), jnp.float32).at[flat_token].a...]
    psum x3 -> x0, blocking collectives: 79.2 us -> none  [the longest x1 39.3 us: shards(): total = lax.psum(squares, ('row', 'col'))]
  transfers between devices with their start and end apart: 15 -> 48, of which waited for: 14 -> 31; matrix products, arithmetic and copies ran while one was open for 24% -> 14% of each run, Pallas kernels for 0% -> 29%
where the time goes in v1:
time: 818 us; the launch traced here: 807 us
  waiting for transfers between devices  302 us (37%)
  Pallas kernels  292 us (36%)
  local copies, waits for them, and re-layouts  69.5 us (8%)
  starting transfers between devices  50.7 us (6%)
  matrix products  40.3 us (5%)
  other arithmetic  35.5 us (4%)
  between operations  16.7 us (2%)
    ppermute x42, waiting for transfers between devices, shift(): return lax.ppermute(values, 'col', pairs)  266 us
    pallas_call x4, Pallas kernels, experts(): pl.pallas_call(held(experts_kernel, 7, len(waits)), grid_spec=pltpu.Prefe...  99.5 us
    pallas_call x4, Pallas kernels, attend_back(): pl.pallas_call(held(functools.partial(attend_back_kernel, share), 12, len...  68.7 us
    ppermute x42, starting transfers between devices, shift(): return lax.ppermute(values, 'col', pairs)  50.4 us
    pallas_call x3, Pallas kernels, project(): pl.pallas_call(held(functools.partial(project_kernel, turned), 4, len(wai...  37.5 us
    pallas_call x1, Pallas kernels, attend(): pl.pallas_call(functools.partial(attend_kernel, share), grid=(heads,), in...  36.4 us
    all_gather x4, waiting for transfers between devices, gather_rows(): return lax.all_gather(values, 'row', axis=axis, tiled=True)  36.2 us
    dot_general x9, matrix products, contract_last(): lax.dot_general(left, right, (((1,), (1,)), ((), ())), preferred_element_...  29.6 us
  transfers between devices with their start and end apart: 48, of which 31 were waited for; matrix products, arithmetic and copies ran while one was open for 14% of the time, Pallas kernels for 29%

profile of v1, /device:TPU:0, one launch (start us, length us, event | category | flops | bytes accessed | tf_op | source)
XLA Modules:
  0.0 806.9 jit_solution(15306457925894494334)
XLA Ops:
  18.3 14.2 %collective-permute-done.3 = bf16[256,1024]{1,0:T(8,128)(2,1)S(1)} collective-permute-done((bf16[256,1024]{1,0:T(8,128)(2,1)}, bf16[256,1024]{1,0:T(8,128)(2,1)S(1)}, u32[]{:S(2)}, u32[]{:S(2)}) %collective-permute-start.3) | collective-permute-done | bytes 524320 | tf_op jit(solution)/shard_map/ppermute | solution.py:105
  32.5 15.0 %collective-permute-done.4 = bf16[256,1024]{1,0:T(8,128)(2,1)} collective-permute-done((bf16[256,1024]{1,0:T(8,128)(2,1)S(1)}, bf16[256,1024]{1,0:T(8,128)(2,1)}, u32[]{:S(2)}, u32[]{:S(2)}) %collective-permute-start.4) | collective-permute-done | bytes 524320 | tf_op jit(solution)/shard_map/ppermute | solution.py:105
  49.0 12.8 %collective-permute-done.5 = bf16[256,1024]{1,0:T(8,128)(2,1)} collective-permute-done((bf16[256,1024]{1,0:T(8,128)(2,1)}, bf16[256,1024]{1,0:T(8,128)(2,1)}, u32[]{:S(2)}, u32[]{:S(2)}) %collective-permute-start.5) | collective-permute-done | bytes 524320 | tf_op jit(solution)/shard_map/ppermute | solution.py:105
  64.5 12.9 %collective-permute-done.12 = bf16[1024,256]{1,0:T(8,128)(2,1)S(1)} collective-permute-done((bf16[1024,256]{1,0:T(8,128)(2,1)S(1)}, bf16[1024,256]{1,0:T(8,128)(2,1)S(1)}, u32[]{:S(2)}, u32[]{:S(2)}) %collective-permute-start.12) | collective-permute-done | bytes 524320 | tf_op jit(solution)/shard_map/ppermute | solution.py:105
  77.4 12.1 %collective-permute-done.13 = bf16[1024,256]{1,0:T(8,128)(2,1)S(1)} collective-permute-done((bf16[1024,256]{1,0:T(8,128)(2,1)S(1)}, bf16[1024,256]{1,0:T(8,128)(2,1)S(1)}, u32[]{:S(2)}, u32[]{:S(2)}) %collective-permute-start.13) | collective-permute-done | bytes 524320 | tf_op jit(solution)/shard_map/ppermute | solution.py:105
  89.8 10.8 %collective-permute-done.14 = bf16[1024,256]{1,0:T(8,128)(2,1)S(1)} collective-permute-done((bf16[1024,256]{1,0:T(8,128)(2,1)S(1)}, bf16[1024,256]{1,0:T(8,128)(2,1)S(1)}, u32[]{:S(2)}, u32[]{:S(2)}) %collective-permute-start.14) | collective-permute-done | bytes 524320 | tf_op jit(solution)/shard_map/ppermute | solution.py:105
  106.8 3.8 collective-permute-start.2
  111.1 3.8 collective-permute-start.15
  123.1 25.0 %collective-permute-done.7 = bf16[32,1024]{1,0:T(8,128)(2,1)S(1)} collective-permute-done((bf16[32,1024]{1,0:T(8,128)(2,1)S(1)}, bf16[32,1024]{1,0:T(8,128)(2,1)S(1)}, u32[]{:S(2)}, u32[]{:S(2)}) %collective-permute-start.7) | collective-permute-done | bytes 65568 | tf_op jit(solution)/shard_map/ppermute | solution.py:105
  157.2 21.5 %collective-permute-done.16 = bf16[1024,512]{1,0:T(8,128)(2,1)} collective-permute-done((bf16[1024,512]{1,0:T(8,128)(2,1)}, bf16[1024,512]{1,0:T(8,128)(2,1)}, u32[]{:S(2)}, u32[]{:S(2)}) %collective-permute-start.16) | collective-permute-done | bytes 1048608 | tf_op jit(solution)/shard_map/ppermute | solution.py:105
  181.1 3.6 fusion.7
  195.1 11.3 %collective-permute-done.17 = bf16[1024,512]{1,0:T(8,128)(2,1)} collective-permute-done((bf16[1024,512]{1,0:T(8,128)(2,1)}, bf16[1024,512]{1,0:T(8,128)(2,1)}, u32[]{:S(2)}, u32[]{:S(2)}) %collective-permute-start.17) | collective-permute-done | bytes 1048608 | tf_op jit(solution)/shard_map/ppermute | solution.py:105
  208.7 4.2 collective-permute-done.9
  214.4 17.0 %fusion.refs_4_.refs_2_ = f32[1024,3072]{1,0:T(8,128)} fusion(bf16[1024,2048]{1,0:T(8,128)(2,1)} %constant_dynamic-update-slice_fusion.12, bf16[4640,2048]{1,0:T(8,128)(2,1)S(1)} %copy-done), kind=kOutput, calls=%fused_computation | convolution fusion | flops 12884901888 | bytes 29360128 | tf_op jit(solution)/shard_map/dot_general | solution.py:31
  234.5 12.4 %project.3.proj_ref.refs_0_ = f32[256,4096]{1,0:T(8,128)} custom-call(bf16[256,2048]{1,0:T(8,128)(2,1)} %copy-done.14, bf16[2048,4096]{1,0:T(8,128)(2,1)} %all-gather.9.cloned.1.call-done.refs_1_, bf16[256,16]{1,0:T(8,128)(2,1)} %bitcast.111, bf16[16,4096]{1,0:T(8,128)(2,1)} %get-tuple-element.150.refs_3_), custom_call_target="tpu_custom_call" | custom-call | tf_op jit(solution)/shard_map/project/pallas_call | solution.py:84
  251.6 36.4 %attend.1 = (bf16[256,4096]{1,0:T(8,128)(2,1)}, f32[32,1,256]{2,1,0:T(1,128)}) custom-call(f32[256,4096]{1,0:T(8,128)} %project.3.proj_ref.refs_0_, f32[256,128]{1,0:T(8,128)} %pad_maximum_fusion.5.cos_ref.refs_1_, f32[256,128]{1,0:T(8,128)} %copy-done.12, f32[1,128]{1,0:T(1,128)} %bitcast.130, f32[1024,256]{1,0:T(8,128)} %fusion.25.bias_ref.refs_4_, ...), custom_call_target="tpu_custom_call" | custom-call | flops 12884901888 | bytes 8388608 | tf_op jit(solution)/shard_map/attend/pallas_call | solution.py:289
  291.0 18.0 %all-gather.13.cloned.1.call-done.refs_1_.refs_9_ = bf16[4096,2048]{1,0:T(8,128)(2,1)} async-done(((bf16[4096,256]{1,0:T(8,128)(2,1)}), bf16[4096,2048]{1,0:T(8,128)(2,1)}) %all-gather.13.cloned.1.call-update) | async-done | bytes 16777232 | tf_op jit(solution)/shard_map/all_gather | solution.py:631
  309.0 12.9 %project.4 = f32[256,2048]{1,0:T(8,128)} custom-call(bf16[256,4096]{1,0:T(8,128)(2,1)} %get-tuple-element.60.refs_0_, bf16[4096,2048]{1,0:T(8,128)(2,1)} %all-gather.13.cloned.1.call-done.refs_1_.refs_9_, bf16[256,16]{1,0:T(8,128)(2,1)} %convolution_convert_fusion.5.refs_2_, bf16[16,2048]{1,0:T(8,128)(2,1)} %get-tuple-element.120.refs_3_.up_ref, ...), custom_call_target="tpu_custom_call" | custom-call | tf_op jit(solution)/shard_map/project/pallas_call | solution.py:84
  328.3 25.7 %collective-permute-done.18 = bf16[256,2048]{1,0:T(8,128)(2,1)S(1)} collective-permute-done((bf16[256,2048]{1,0:T(8,128)(2,1)S(1)}, bf16[256,2048]{1,0:T(8,128)(2,1)S(1)}, u32[]{:S(2)}, u32[]{:S(2)}) %collective-permute-start.18) | collective-permute-done | bytes 1048608 | tf_op jit(solution)/shard_map/ppermute | solution.py:105
  355.5 24.8 %collective-permute-done.19 = bf16[256,2048]{1,0:T(8,128)(2,1)S(1)} collective-permute-done((bf16[256,2048]{1,0:T(8,128)(2,1)S(1)}, bf16[256,2048]{1,0:T(8,128)(2,1)S(1)}, u32[]{:S(2)}, u32[]{:S(2)}) %collective-permute-start.19) | collective-permute-done | bytes 1048608 | tf_op jit(solution)/shard_map/ppermute | solution.py:105
  387.8 18.0 %collective-permute-done.20 = bf16[256,2048]{1,0:T(8,128)(2,1)S(1)} collective-permute-done((bf16[256,2048]{1,0:T(8,128)(2,1)S(1)}, bf16[256,2048]{1,0:T(8,128)(2,1)S(1)}, u32[]{:S(2)}, u32[]{:S(2)}) %collective-permute-start.20) | collective-permute-done | bytes 1048608 | tf_op jit(solution)/shard_map/ppermute | solution.py:105
  418.0 18.2 %all-gather.15.cloned.1.call-done.refs_4_.refs_5_ = bf16[4,2048,1536]{2,1,0:T(8,128)(2,1)} async-done(((bf16[4,256,1536]{2,1,0:T(8,128)(2,1)}), bf16[4,2048,1536]{2,1,0:T(8,128)(2,1)}) %all-gather.15.cloned.1.call-update) | async-done | bytes 25165840 | tf_op jit(solution)/shard_map/all_gather | solution.py:631
  436.2 24.9 %experts.4 = (f32[256,2176]{1,0:T(8,128)}, bf16[1024,2048]{1,0:T(8,128)(2,1)}) custom-call(s32[2]{0:T(128)} %get-tuple-element.183.refs_0_, bf16[1024,2048]{1,0:T(8,128)(2,1)} %copy-done.2, f32[1024,3072]{1,0:T(8,128)} %fusion.refs_4_.refs_2_, f32[1024,4]{1,0:T(8,128)} %constant_dynamic-slice_fusion.9.refs_3_, ...), custom_call_target="tpu_custom_call" | custom-call | flops 16106127360 | bytes 37748736 | tf_op jit(solution)/shard_map/experts/pallas_call | solution.py:394
  464.6 24.9 %experts.5 = (f32[256,2176]{1,0:T(8,128)}, bf16[1024,2048]{1,0:T(8,128)(2,1)}) custom-call(s32[2]{0:T(128)} %get-tuple-element.182.refs_0_, bf16[1024,2048]{1,0:T(8,128)(2,1)} %copy-done.2, f32[1024,3072]{1,0:T(8,128)} %fusion.refs_4_.refs_2_, f32[1024,4]{1,0:T(8,128)} %constant_dynamic-slice_fusion.9.refs_3_, ...), custom_call_target="tpu_custom_call", output_to_operand_aliasing={{1}: (7, {})} | custom-call | flops 16106127360 | bytes 37748736 | tf_op jit(solution)/shard_map/experts/pallas_call | solution.py:394
  494.5 24.8 %experts.6 = (f32[256,2176]{1,0:T(8,128)}, bf16[1024,2048]{1,0:T(8,128)(2,1)}) custom-call(s32[2]{0:T(128)} %pad_add_fusion.1.refs_0_, bf16[1024,2048]{1,0:T(8,128)(2,1)} %copy-done.2, f32[1024,3072]{1,0:T(8,128)} %fusion.refs_4_.refs_2_, f32[1024,4]{1,0:T(8,128)} %constant_dynamic-slice_fusion.9.refs_3_, ...), custom_call_target="tpu_custom_call", output_to_operand_aliasing={{1}: (7, {})} | custom-call | flops 16106127360 | bytes 37748736 | tf_op jit(solution)/shard_map/experts/pallas_call | solution.py:394
  524.1 24.8 %experts.7 = (f32[256,2176]{1,0:T(8,128)}, bf16[1024,2048]{1,0:T(8,128)(2,1)}) custom-call(s32[2]{0:T(128)} %pad_add_fusion.refs_0_, bf16[1024,2048]{1,0:T(8,128)(2,1)} %copy-done.2, f32[1024,3072]{1,0:T(8,128)} %fusion.refs_4_.refs_2_, f32[1024,4]{1,0:T(8,128)} %constant_dynamic-slice_fusion.9.refs_3_, ...), custom_call_target="tpu_custom_call", output_to_operand_aliasing={{1}: (7, {})} | custom-call | flops 16106127360 | bytes 37748736 | tf_op jit(solution)/shard_map/experts/pallas_call | solution.py:394
  554.7 6.4 settle.1
  561.1 17.2 %attend_back.4 = (bf16[256,4096]{1,0:T(8,128)(2,1)}, f32[1024,512]{1,0:T(8,128)}, f32[1024,512]{1,0:T(8,128)}) custom-call(f32[256,4096]{1,0:T(8,128)} %project.3.proj_ref.refs_0_, f32[256,128]{1,0:T(8,128)} %pad_maximum_fusion.5.cos_ref.refs_1_, f32[256,128]{1,0:T(8,128)} %copy-done.12, f32[1,128]{1,0:T(1,128)} %bitcast.131, ...), custom_call_target="tpu_custom_call" | custom-call | tf_op jit(solution)/shard_map/attend_back/pallas_call | solution.py:325
  580.4 3.6 hop.9.refs_15_
  584.0 17.2 %attend_back.5 = (bf16[256,4096]{1,0:T(8,128)(2,1)}, f32[1024,512]{1,0:T(8,128)}, f32[1024,512]{1,0:T(8,128)}) custom-call(f32[256,4096]{1,0:T(8,128)} %project.3.proj_ref.refs_0_, f32[256,128]{1,0:T(8,128)} %pad_maximum_fusion.5.cos_ref.refs_1_, f32[256,128]{1,0:T(8,128)} %copy-done.12, ...), custom_call_target="tpu_custom_call", output_to_operand_aliasing={{0}: (12, {}), {1}: (13, {}), {2}: (14, {})} | custom-call | tf_op jit(solution)/shard_map/attend_back/pallas_call | solution.py:325
  601.2 17.2 %attend_back.6 = (bf16[256,4096]{1,0:T(8,128)(2,1)}, f32[1024,512]{1,0:T(8,128)}, f32[1024,512]{1,0:T(8,128)}) custom-call(f32[256,4096]{1,0:T(8,128)} %project.3.proj_ref.refs_0_, f32[256,128]{1,0:T(8,128)} %pad_maximum_fusion.5.cos_ref.refs_1_, f32[256,128]{1,0:T(8,128)} %copy-done.12, ...), custom_call_target="tpu_custom_call", output_to_operand_aliasing={{0}: (12, {}), {1}: (13, {}), {2}: (14, {})} | custom-call | tf_op jit(solution)/shard_map/attend_back/pallas_call | solution.py:325
  619.5 3.6 hop.10.refs_15_
  625.1 17.2 %attend_back.7 = (bf16[256,4096]{1,0:T(8,128)(2,1)}, f32[1024,512]{1,0:T(8,128)}, f32[1024,512]{1,0:T(8,128)}) custom-call(f32[256,4096]{1,0:T(8,128)} %project.3.proj_ref.refs_0_, f32[256,128]{1,0:T(8,128)} %pad_maximum_fusion.5.cos_ref.refs_1_, f32[256,128]{1,0:T(8,128)} %copy-done.12, ...), custom_call_target="tpu_custom_call", output_to_operand_aliasing={{0}: (12, {}), {1}: (13, {}), {2}: (14, {})} | custom-call | tf_op jit(solution)/shard_map/attend_back/pallas_call | solution.py:325
  642.3 5.4 collective-permute-done.26.refs_1_.refs_3_
  654.8 12.2 %project.5.refs_4_ = f32[256,2048]{1,0:T(8,128)} custom-call(bf16[256,4096]{1,0:T(8,128)(2,1)} %get-tuple-element.82.refs_0_, bf16[2048,4096]{1,0:T(8,128)(2,1)} %all-gather.9.cloned.1.call-done.refs_1_, bf16[256,16]{1,0:T(8,128)(2,1)} %copy.101.refs_2_, bf16[16,2048]{1,0:T(8,128)(2,1)} %get-tuple-element.118.refs_3_, bf16[256,1024]{1,0:T(8,128)(2,1)} %hop.12.refs_4_), custom_call_target="tpu_custom_call" | custom-call | tf_op jit(solution)/shard_map/project/pallas_call | solution.py:84
  667.1 3.6 hop.13.refs_4_
  672.7 10.4 %collective-permute-done.28.refs_1_ = bf16[256,1024]{1,0:T(8,128)(2,1)} collective-permute-done((bf16[256,1024]{1,0:T(8,128)(2,1)}, bf16[256,1024]{1,0:T(8,128)(2,1)}, u32[]{:S(2)}, u32[]{:S(2)}) %collective-permute-start.28) | collective-permute-done | bytes 524320 | tf_op jit(solution)/shard_map/ppermute | solution.py:105
  687.7 3.8 collective-permute-start.32
  692.6 3.8 hop.11
  696.4 4.3 collective-permute-done.32.refs_3_
  700.7 4.5 collective-permute-done.30.refs_1_
  711.2 3.5 hop.15
  720.1 3.7 collective-permute-start.41
  730.0 5.0 collective-permute-done.39
  737.8 4.9 fusion.23
  746.7 4.6 collective-permute-start.34
  767.1 8.9 %collective-permute-done.36 = bf16[256,512]{1,0:T(8,128)(2,1)S(1)} collective-permute-done((bf16[256,512]{1,0:T(8,128)(2,1)}, bf16[256,512]{1,0:T(8,128)(2,1)S(1)}, u32[]{:S(2)}, u32[]{:S(2)}) %collective-permute-start.36) | collective-permute-done | bytes 262176 | tf_op jit(solution)/shard_map/ppermute | solution.py:105
  786.6 13.2 %update.1 = (f32[1,1]{1,0:T(1,128)}, f32[8,16,1024]{2,1,0:T(8,128)}, f32[8,16,1024]{2,1,0:T(8,128)}, f32[8,16,1024]{2,1,0:T(8,128)}, f32[8,16,1024]{2,1,0:T(8,12...) custom-call(s32[8]{0:T(128)} %bitcast_convert_fusion.slot_ref, ...), custom_call_target="tpu_custom_call" | custom-call | tf_op jit(solution)/shard_map/update/pallas_call | solution.py:534
  (414 shorter events, 182.4 us)
Async XLA Ops:
  7.2 172.5 %all-gather.11.cloned.1.call-start = ((), (), s32[]{:S(2)}) async-start(), calls=%async_computation.1 | async-start | bytes 21381120 | tf_op jit(solution)/shard_map/all_gather | solution.py:631
  15.2 219.3 %all-gather.9.cloned.1.call-start = ((), (), s32[]{:S(2)}) async-start(), calls=%async_computation | async-start | bytes 18874368 | tf_op jit(solution)/shard_map/all_gather | solution.py:631
  15.2 17.2 %collective-permute-start.3 = (bf16[256,1024]{1,0:T(8,128)(2,1)}, bf16[256,1024]{1,0:T(8,128)(2,1)S(1)}, u32[]{:S(2)}, u32[]{:S(2)}) collective-permute-start(bf16[256,1024]{1,0:T(8,128)(2,1)} %param.38), channel_id=1, source_target_pairs={{0,1},{1,2},{2,3},{3,0},{4,5},{5,6},{6,7},{7,4},{8,9},{9,10},{10,1... | collective-permute-start | bytes 1572872 | tf_op jit(solution)/shard_map/ppermute | solution.py:105
  32.5 15.0 %collective-permute-start.4 = (bf16[256,1024]{1,0:T(8,128)(2,1)S(1)}, bf16[256,1024]{1,0:T(8,128)(2,1)}, u32[]{:S(2)}, u32[]{:S(2)}) collective-permute-start(bf16[256,1024]{1,0:T(8,128)(2,1)S(1)} %collective-permute-done.3), channel_id=1, source_target_pairs={{0,1},{1,2},{2,3},{3,0},{4,5},{5,6},{6,7},{7,4},{8,9},{9,10},{10,1... | collective-permute-start | bytes 1572872 | tf_op jit(solution)/shard_map/ppermute | solution.py:105
  47.5 14.3 %collective-permute-start.5 = (bf16[256,1024]{1,0:T(8,128)(2,1)}, bf16[256,1024]{1,0:T(8,128)(2,1)}, u32[]{:S(2)}, u32[]{:S(2)}) collective-permute-start(bf16[256,1024]{1,0:T(8,128)(2,1)} %collective-permute-done.4), channel_id=1, source_target_pairs={{0,1},{1,2},{2,3},{3,0},{4,5},{5,6},{6,7},{7,4},{8,9},{9,10},{10,1... | collective-permute-start | bytes 1572872 | tf_op jit(solution)/shard_map/ppermute | solution.py:105
  64.4 244.6 %all-gather.13.cloned.1.call-start = ((), (), s32[]{:S(2)}) async-start(), calls=%async_computation.2 | async-start | bytes 18874368 | tf_op jit(solution)/shard_map/all_gather | solution.py:631
  64.4 13.0 %collective-permute-start.12 = (bf16[1024,256]{1,0:T(8,128)(2,1)S(1)}, bf16[1024,256]{1,0:T(8,128)(2,1)S(1)}, u32[]{:S(2)}, u32[]{:S(2)}) collective-permute-start(bf16[1024,256]{1,0:T(8,128)(2,1)S(1)} %copy-done.47), channel_id=1, source_target_pairs={{0,1},{1,2},{2,3},{3,0},{4,5},{5,6},{6,7},{7,4},{8,9},{9,10},{10,1... | collective-permute-start | bytes 1572872 | tf_op jit(solution)/shard_map/ppermute | solution.py:105
  77.4 12.1 %collective-permute-start.13 = (bf16[1024,256]{1,0:T(8,128)(2,1)S(1)}, bf16[1024,256]{1,0:T(8,128)(2,1)S(1)}, u32[]{:S(2)}, u32[]{:S(2)}) collective-permute-start(bf16[1024,256]{1,0:T(8,128)(2,1)S(1)} %collective-permute-done.12), channel_id=1, source_target_pairs={{0,1},{1,2},{2,3},{3,0},{4,5},{5,6},{6,7},{7,4},{8,9},{9,10},{10,1... | collective-permute-start | bytes 1572872 | tf_op jit(solution)/shard_map/ppermute | solution.py:105
  89.5 11.1 %collective-permute-start.14 = (bf16[1024,256]{1,0:T(8,128)(2,1)S(1)}, bf16[1024,256]{1,0:T(8,128)(2,1)S(1)}, u32[]{:S(2)}, u32[]{:S(2)}) collective-permute-start(bf16[1024,256]{1,0:T(8,128)(2,1)S(1)} %collective-permute-done.13), channel_id=1, source_target_pairs={{0,1},{1,2},{2,3},{3,0},{4,5},{5,6},{6,7},{7,4},{8,9},{9,10},{10,1... | collective-permute-start | bytes 1572872 | tf_op jit(solution)/shard_map/ppermute | solution.py:105
  102.0 334.2 %all-gather.15.cloned.1.call-start = ((), (), s32[]{:S(2)}) async-start(), calls=%async_computation.3 | async-start | bytes 28311552 | tf_op jit(solution)/shard_map/all_gather | solution.py:631
  102.6 640.2 %all-gather.17.cloned.1.call-start = ((), (), s32[]{:S(2)}) async-start(), calls=%async_computation.4 | async-start | bytes 1179648 | tf_op jit(solution)/shard_map/all_gather | solution.py:826
  104.5 18.5 %collective-permute-start.6 = (bf16[32,1024]{1,0:T(8,128)(2,1)S(1)}, bf16[32,1024]{1,0:T(8,128)(2,1)S(1)}, u32[]{:S(2)}, u32[]{:S(2)}) collective-permute-start(bf16[32,1024]{1,0:T(8,128)(2,1)S(1)} %get-tuple-element.171), channel_id=1, source_target_pairs={{0,1},{1,2},{2,3},{3,0},{4,5},{5,6},{6,7},{7,4},{8,9},{9,10},{10,1... | collective-permute-start | bytes 196616 | tf_op jit(solution)/shard_map/ppermute | solution.py:105
  106.8 49.7 %collective-permute-start.2 = (bf16[256,512]{1,0:T(8,128)(2,1)}, bf16[256,512]{1,0:T(8,128)(2,1)S(1)}, u32[]{:S(2)}, u32[]{:S(2)}) collective-permute-start(bf16[256,512]{1,0:T(8,128)(2,1)} %get-tuple-element.133), channel_id=1, source_target_pairs={{0,3},{1,0},{2,1},{3,2},{4,7},{5,4},{6,5},{7,6},{8,11},{9,8},{10,9... | collective-permute-start | bytes 786440 | tf_op jit(solution)/shard_map/ppermute | solution.py:105
  110.6 43.6 %collective-permute-start = (bf16[256,512]{1,0:T(8,128)(2,1)}, bf16[256,512]{1,0:T(8,128)(2,1)}, u32[]{:S(2)}, u32[]{:S(2)}) collective-permute-start(bf16[256,512]{1,0:T(8,128)(2,1)} %get-tuple-element.134), channel_id=1, source_target_pairs={{0,1},{1,2},{2,3},{3,0},{4,5},{5,6},{6,7},{7,4},{8,9},{9,10},{10,1... | collective-permute-start | bytes 786440 | tf_op jit(solution)/shard_map/ppermute | solution.py:105
  110.6 45.9 %collective-permute-start.1 = (bf16[256,512]{1,0:T(8,128)(2,1)}, bf16[256,512]{1,0:T(8,128)(2,1)S(1)}, u32[]{:S(2)}, u32[]{:S(2)}) collective-permute-start(bf16[256,512]{1,0:T(8,128)(2,1)} %get-tuple-element.136), channel_id=1, source_target_pairs={{0,2},{1,3},{2,0},{3,1},{4,6},{5,7},{6,4},{7,5},{8,10},{9,11},{10,... | collective-permute-start | bytes 786440 | tf_op jit(solution)/shard_map/ppermute | solution.py:105
  111.1 44.1 %collective-permute-start.15 = (bf16[1024,512]{1,0:T(8,128)(2,1)S(1)}, bf16[1024,512]{1,0:T(8,128)(2,1)}, u32[]{:S(2)}, u32[]{:S(2)}) collective-permute-start(bf16[1024,512]{1,0:T(8,128)(2,1)S(1)} %copy-done.41), channel_id=1, source_target_pairs={{0,1},{1,2},{2,3},{3,0},{4,5},{5,6},{6,7},{7,4},{8,9},{9,10},{10,1... | collective-permute-start | bytes 3145736 | tf_op jit(solution)/shard_map/ppermute | solution.py:105
  123.0 25.1 %collective-permute-start.7 = (bf16[32,1024]{1,0:T(8,128)(2,1)S(1)}, bf16[32,1024]{1,0:T(8,128)(2,1)S(1)}, u32[]{:S(2)}, u32[]{:S(2)}) collective-permute-start(bf16[32,1024]{1,0:T(8,128)(2,1)S(1)} %collective-permute-done.6), channel_id=1, source_target_pairs={{0,1},{1,2},{2,3},{3,0},{4,5},{5,6},{6,7},{7,4},{8,9},{9,10},{10,1... | collective-permute-start | bytes 196616 | tf_op jit(solution)/shard_map/ppermute | solution.py:105
  148.1 6.1 collective-permute-start.8
  155.3 23.4 %collective-permute-start.16 = (bf16[1024,512]{1,0:T(8,128)(2,1)}, bf16[1024,512]{1,0:T(8,128)(2,1)}, u32[]{:S(2)}, u32[]{:S(2)}) collective-permute-start(bf16[1024,512]{1,0:T(8,128)(2,1)} %collective-permute-done.15), channel_id=1, source_target_pairs={{0,1},{1,2},{2,3},{3,0},{4,5},{5,6},{6,7},{7,4},{8,9},{9,10},{10,1... | collective-permute-start | bytes 3145736 | tf_op jit(solution)/shard_map/ppermute | solution.py:105
  178.7 27.7 %collective-permute-start.17 = (bf16[1024,512]{1,0:T(8,128)(2,1)}, bf16[1024,512]{1,0:T(8,128)(2,1)}, u32[]{:S(2)}, u32[]{:S(2)}) collective-permute-start(bf16[1024,512]{1,0:T(8,128)(2,1)} %collective-permute-done.16), channel_id=1, source_target_pairs={{0,1},{1,2},{2,3},{3,0},{4,5},{5,6},{6,7},{7,4},{8,9},{9,10},{10,1... | collective-permute-start | bytes 3145736 | tf_op jit(solution)/shard_map/ppermute | solution.py:105
  187.2 25.6 %collective-permute-start.9 = (bf16[256,1024]{1,0:T(8,128)(2,1)S(1)}, bf16[256,1024]{1,0:T(8,128)(2,1)S(1)}, u32[]{:S(2)}, u32[]{:S(2)}) collective-permute-start(bf16[256,1024]{1,0:T(8,128)(2,1)S(1)} %fusion.37), channel_id=1, source_target_pairs={{0,1},{1,2},{2,3},{3,0},{4,5},{5,6},{6,7},{7,4},{8,9},{9,10},{10,1... | collective-permute-start | bytes 1572872 | tf_op jit(solution)/shard_map/ppermute | solution.py:105
  212.9 18.5 %collective-permute-start.10 = (bf16[256,1024]{1,0:T(8,128)(2,1)S(1)}, bf16[256,1024]{1,0:T(8,128)(2,1)}, u32[]{:S(2)}, u32[]{:S(2)}) collective-permute-start(bf16[256,1024]{1,0:T(8,128)(2,1)S(1)} %collective-permute-done.9), channel_id=1, source_target_pairs={{0,1},{1,2},{2,3},{3,0},{4,5},{5,6},{6,7},{7,4},{8,9},{9,10},{10,1... | collective-permute-start | bytes 1572872 | tf_op jit(solution)/shard_map/ppermute | solution.py:105
  231.4 17.9 %collective-permute-start.11 = (bf16[256,1024]{1,0:T(8,128)(2,1)}, bf16[256,1024]{1,0:T(8,128)(2,1)}, u32[]{:S(2)}, u32[]{:S(2)}) collective-permute-start(bf16[256,1024]{1,0:T(8,128)(2,1)} %collective-permute-done.10), channel_id=1, source_target_pairs={{0,1},{1,2},{2,3},{3,0},{4,5},{5,6},{6,7},{7,4},{8,9},{9,10},{10,1... | collective-permute-start | bytes 1572872 | tf_op jit(solution)/shard_map/ppermute | solution.py:105
  326.8 27.2 %collective-permute-start.18 = (bf16[256,2048]{1,0:T(8,128)(2,1)S(1)}, bf16[256,2048]{1,0:T(8,128)(2,1)S(1)}, u32[]{:S(2)}, u32[]{:S(2)}) collective-permute-start(bf16[256,2048]{1,0:T(8,128)(2,1)S(1)} %get-tuple-element.114), channel_id=1, source_target_pairs={{0,1},{1,2},{2,3},{3,0},{4,5},{5,6},{6,7},{7,4},{8,9},{9,10},{10,1... | collective-permute-start | bytes 3145736 | tf_op jit(solution)/shard_map/ppermute | solution.py:105
  353.9 26.3 %collective-permute-start.19 = (bf16[256,2048]{1,0:T(8,128)(2,1)S(1)}, bf16[256,2048]{1,0:T(8,128)(2,1)S(1)}, u32[]{:S(2)}, u32[]{:S(2)}) collective-permute-start(bf16[256,2048]{1,0:T(8,128)(2,1)S(1)} %collective-permute-done.18), channel_id=1, source_target_pairs={{0,1},{1,2},{2,3},{3,0},{4,5},{5,6},{6,7},{7,4},{8,9},{9,10},{10,1... | collective-permute-start | bytes 3145736 | tf_op jit(solution)/shard_map/ppermute | solution.py:105
  380.3 25.6 %collective-permute-start.20 = (bf16[256,2048]{1,0:T(8,128)(2,1)S(1)}, bf16[256,2048]{1,0:T(8,128)(2,1)S(1)}, u32[]{:S(2)}, u32[]{:S(2)}) collective-permute-start(bf16[256,2048]{1,0:T(8,128)(2,1)S(1)} %collective-permute-done.19), channel_id=1, source_target_pairs={{0,1},{1,2},{2,3},{3,0},{4,5},{5,6},{6,7},{7,4},{8,9},{9,10},{10,1... | collective-permute-start | bytes 3145736 | tf_op jit(solution)/shard_map/ppermute | solution.py:105
  462.9 28.8 %collective-permute-start.21 = (bf16[256,2176]{1,0:T(8,128)(2,1)S(1)}, bf16[256,2176]{1,0:T(8,128)(2,1)S(1)}, u32[]{:S(2)}, u32[]{:S(2)}) collective-permute-start(bf16[256,2176]{1,0:T(8,128)(2,1)S(1)} %convert_element_type.139.refs_8_), channel_id=1, source_target_pairs={{0,1},{1,2},{2,3},{3,0},{4,5},{5,6},{6,7},{7,4},{8,9},{9,10},{10,1... | collective-permute-start | bytes 3342344 | tf_op jit(solution)/shard_map/ppermute | solution.py:105
  493.5 27.8 %collective-permute-start.22 = (bf16[256,2176]{1,0:T(8,128)(2,1)S(1)}, bf16[256,2176]{1,0:T(8,128)(2,1)S(1)}, u32[]{:S(2)}, u32[]{:S(2)}) collective-permute-start(bf16[256,2176]{1,0:T(8,128)(2,1)S(1)} %add_convert_fusion.1.refs_8_), channel_id=1, source_target_pairs={{0,1},{1,2},{2,3},{3,0},{4,5},{5,6},{6,7},{7,4},{8,9},{9,10},{10,1... | collective-permute-start | bytes 3342344 | tf_op jit(solution)/shard_map/ppermute | solution.py:105
  523.1 27.2 %collective-permute-start.23 = (bf16[256,2176]{1,0:T(8,128)(2,1)S(1)}, bf16[256,2176]{1,0:T(8,128)(2,1)S(1)}, u32[]{:S(2)}, u32[]{:S(2)}) collective-permute-start(bf16[256,2176]{1,0:T(8,128)(2,1)S(1)} %add_convert_fusion.refs_8_), channel_id=1, source_target_pairs={{0,1},{1,2},{2,3},{3,0},{4,5},{5,6},{6,7},{7,4},{8,9},{9,10},{10,1... | collective-permute-start | bytes 3342344 | tf_op jit(solution)/shard_map/ppermute | solution.py:105
  554.7 24.7 %collective-permute-start.24 = (bf16[1024,512]{1,0:T(8,128)(2,1)}, bf16[1024,512]{1,0:T(8,128)(2,1)S(1)}, u32[]{:S(2)}, u32[]{:S(2)}) collective-permute-start(bf16[1024,512]{1,0:T(8,128)(2,1)} %hop.8), channel_id=1, source_target_pairs={{0,1},{1,2},{2,3},{3,0},{4,5},{5,6},{6,7},{7,4},{8,9},{9,10},{10,1... | collective-permute-start | bytes 3145736 | tf_op jit(solution)/shard_map/ppermute | solution.py:105
  584.0 34.4 %collective-permute-start.25 = (bf16[1024,512]{1,0:T(8,128)(2,1)}, bf16[1024,512]{1,0:T(8,128)(2,1)S(1)}, u32[]{:S(2)}, u32[]{:S(2)}) collective-permute-start(bf16[1024,512]{1,0:T(8,128)(2,1)} %hop.9.refs_15_), channel_id=1, source_target_pairs={{0,1},{1,2},{2,3},{3,0},{4,5},{5,6},{6,7},{7,4},{8,9},{9,10},{10,1... | collective-permute-start | bytes 3145736 | tf_op jit(solution)/shard_map/ppermute | solution.py:105
  623.1 24.6 %collective-permute-start.26 = (bf16[1024,512]{1,0:T(8,128)(2,1)}, bf16[1024,512]{1,0:T(8,128)(2,1)S(1)}, u32[]{:S(2)}, u32[]{:S(2)}) collective-permute-start(bf16[1024,512]{1,0:T(8,128)(2,1)} %hop.10.refs_15_), channel_id=1, source_target_pairs={{0,1},{1,2},{2,3},{3,0},{4,5},{5,6},{6,7},{7,4},{8,9},{9,10},{10,1... | collective-permute-start | bytes 3145736 | tf_op jit(solution)/shard_map/ppermute | solution.py:105
  652.1 15.0 %collective-permute-start.27 = (bf16[256,1024]{1,0:T(8,128)(2,1)}, bf16[256,1024]{1,0:T(8,128)(2,1)}, u32[]{:S(2)}, u32[]{:S(2)}) collective-permute-start(bf16[256,1024]{1,0:T(8,128)(2,1)} %hop.12.refs_4_), channel_id=1, source_target_pairs={{0,1},{1,2},{2,3},{3,0},{4,5},{5,6},{6,7},{7,4},{8,9},{9,10},{10,1... | collective-permute-start | bytes 1572872 | tf_op jit(solution)/shard_map/ppermute | solution.py:105
  670.7 12.4 %collective-permute-start.28 = (bf16[256,1024]{1,0:T(8,128)(2,1)}, bf16[256,1024]{1,0:T(8,128)(2,1)}, u32[]{:S(2)}, u32[]{:S(2)}) collective-permute-start(bf16[256,1024]{1,0:T(8,128)(2,1)} %hop.13.refs_4_), channel_id=1, source_target_pairs={{0,1},{1,2},{2,3},{3,0},{4,5},{5,6},{6,7},{7,4},{8,9},{9,10},{10,1... | collective-permute-start | bytes 1572872 | tf_op jit(solution)/shard_map/ppermute | solution.py:105
  686.6 23.9 %collective-permute-start.29 = (bf16[256,1024]{1,0:T(8,128)(2,1)}, bf16[256,1024]{1,0:T(8,128)(2,1)S(1)}, u32[]{:S(2)}, u32[]{:S(2)}) collective-permute-start(bf16[256,1024]{1,0:T(8,128)(2,1)} %hop.14), channel_id=1, source_target_pairs={{0,1},{1,2},{2,3},{3,0},{4,5},{5,6},{6,7},{7,4},{8,9},{9,10},{10,1... | collective-permute-start | bytes 1572872 | tf_op jit(solution)/shard_map/ppermute | solution.py:105
  687.7 12.9 %collective-permute-start.32 = (bf16[64,1024]{1,0:T(8,128)(2,1)S(1)}, bf16[64,1024]{1,0:T(8,128)(2,1)S(1)}, u32[]{:S(2)}, u32[]{:S(2)}) collective-permute-start(bf16[64,1024]{1,0:T(8,128)(2,1)S(1)} %get-tuple-element.167), channel_id=1, source_target_pairs={{0,3},{1,0},{2,1},{3,2},{4,7},{5,4},{6,5},{7,6},{8,11},{9,8},{10,9... | collective-permute-start | bytes 393224 | tf_op jit(solution)/shard_map/ppermute | solution.py:105
  691.5 13.6 %collective-permute-start.30 = (bf16[64,1024]{1,0:T(8,128)(2,1)S(1)}, bf16[64,1024]{1,0:T(8,128)(2,1)S(1)}, u32[]{:S(2)}, u32[]{:S(2)}) collective-permute-start(bf16[64,1024]{1,0:T(8,128)(2,1)S(1)} %get-tuple-element.168), channel_id=1, source_target_pairs={{0,1},{1,2},{2,3},{3,0},{4,5},{5,6},{6,7},{7,4},{8,9},{9,10},{10,1... | collective-permute-start | bytes 393224 | tf_op jit(solution)/shard_map/ppermute | solution.py:105
  691.5 16.3 %collective-permute-start.31 = (bf16[64,1024]{1,0:T(8,128)(2,1)S(1)}, bf16[64,1024]{1,0:T(8,128)(2,1)S(1)}, u32[]{:S(2)}, u32[]{:S(2)}) collective-permute-start(bf16[64,1024]{1,0:T(8,128)(2,1)S(1)} %get-tuple-element.169), channel_id=1, source_target_pairs={{0,2},{1,3},{2,0},{3,1},{4,6},{5,7},{6,4},{7,5},{8,10},{9,11},{10,... | collective-permute-start | bytes 393224 | tf_op jit(solution)/shard_map/ppermute | solution.py:105
  710.4 72.2 %all-gather.19.cloned.1.call-start = ((), (), s32[]{:S(2)}) async-start(), calls=%async_computation.5 | async-start | bytes 2064384 | tf_op jit(solution)/shard_map/all_gather | solution.py:845
  720.0 10.0 %collective-permute-start.40 = (bf16[56,2048]{1,0:T(8,128)(2,1)S(1)}, bf16[56,2048]{1,0:T(8,128)(2,1)S(1)}, u32[]{:S(2)}, u32[]{:S(2)}) collective-permute-start(bf16[56,2048]{1,0:T(8,128)(2,1)S(1)} %pad_maximum_fusion), channel_id=1, source_target_pairs={{0,1},{1,2},{2,3},{3,0},{4,5},{5,6},{6,7},{7,4},{8,9},{9,10},{10,1... | collective-permute-start | bytes 688136 | tf_op jit(solution)/shard_map/ppermute | solution.py:105
  720.1 14.9 %collective-permute-start.39 = (bf16[56,2048]{1,0:T(8,128)(2,1)S(1)}, bf16[56,2048]{1,0:T(8,128)(2,1)S(1)}, u32[]{:S(2)}, u32[]{:S(2)}) collective-permute-start(bf16[56,2048]{1,0:T(8,128)(2,1)S(1)} %pad_maximum_fusion), channel_id=1, source_target_pairs={{0,2},{1,3},{2,0},{3,1},{4,6},{5,7},{6,4},{7,5},{8,10},{9,11},{10,... | collective-permute-start | bytes 688136 | tf_op jit(solution)/shard_map/ppermute | solution.py:105
  720.1 14.8 %collective-permute-start.41 = (bf16[56,2048]{1,0:T(8,128)(2,1)S(1)}, bf16[56,2048]{1,0:T(8,128)(2,1)S(1)}, u32[]{:S(2)}, u32[]{:S(2)}) collective-permute-start(bf16[56,2048]{1,0:T(8,128)(2,1)S(1)} %pad_maximum_fusion), channel_id=1, source_target_pairs={{0,3},{1,0},{2,1},{3,2},{4,7},{5,4},{6,5},{7,6},{8,11},{9,8},{10,9... | collective-permute-start | bytes 688136 | tf_op jit(solution)/shard_map/ppermute | solution.py:105
  746.7 9.2 %collective-permute-start.34 = (f32[1,128]{1,0:T(1,128)S(1)}, f32[1,128]{1,0:T(1,128)S(1)}, u32[]{:S(2)}, u32[]{:S(2)}) collective-permute-start(f32[1,128]{1,0:T(1,128)S(1)} %broadcast_in_dim.149), channel_id=1, source_target_pairs={{0,1},{1,2},{2,3},{3,0},{4,5},{5,6},{6,7},{7,4},{8,9},{9,10},{10,1... | collective-permute-start | bytes 1544 | tf_op jit(solution)/shard_map/ppermute | solution.py:105
  751.3 4.6 collective-permute-start.35
  751.7 4.4 collective-permute-start.33
  759.8 19.0 %collective-permute-start.37 = (bf16[256,512]{1,0:T(8,128)(2,1)}, bf16[256,512]{1,0:T(8,128)(2,1)S(1)}, u32[]{:S(2)}, u32[]{:S(2)}) collective-permute-start(bf16[256,512]{1,0:T(8,128)(2,1)} %get-tuple-element.130), channel_id=1, source_target_pairs={{0,2},{1,3},{2,0},{3,1},{4,6},{5,7},{6,4},{7,5},{8,10},{9,11},{10,... | collective-permute-start | bytes 786440 | tf_op jit(solution)/shard_map/ppermute | solution.py:105
  761.5 14.5 %collective-permute-start.36 = (bf16[256,512]{1,0:T(8,128)(2,1)}, bf16[256,512]{1,0:T(8,128)(2,1)S(1)}, u32[]{:S(2)}, u32[]{:S(2)}) collective-permute-start(bf16[256,512]{1,0:T(8,128)(2,1)} %get-tuple-element.131), channel_id=1, source_target_pairs={{0,1},{1,2},{2,3},{3,0},{4,5},{5,6},{6,7},{7,4},{8,9},{9,10},{10,1... | collective-permute-start | bytes 786440 | tf_op jit(solution)/shard_map/ppermute | solution.py:105
  764.2 16.7 %collective-permute-start.38 = (bf16[256,512]{1,0:T(8,128)(2,1)S(1)}, bf16[256,512]{1,0:T(8,128)(2,1)S(1)}, u32[]{:S(2)}, u32[]{:S(2)}) collective-permute-start(bf16[256,512]{1,0:T(8,128)(2,1)S(1)} %get-tuple-element.129), channel_id=1, source_target_pairs={{0,3},{1,0},{2,1},{3,2},{4,7},{5,4},{6,5},{7,6},{8,11},{9,8},{10,9... | collective-permute-start | bytes 786440 | tf_op jit(solution)/shard_map/ppermute | solution.py:105
  (89 other events, 997.6 us)
Sparse Core Ops, SparseCore 0:
  15.3 105.6 all-gather.10
  123.5 89.8 all-gather.8
  215.8 93.1 all-gather.12
  310.7 125.4 all-gather.14
  710.5 20.7 all-gather.16
  736.7 28.6 all-gather.18

commit v2 on v1

--- a/solution.py
+++ b/solution.py
@@ -205,6 +205,88 @@
     )(*parts, *waits)
 
 
+def cut_kernel(place_ref, *refs):
+    half = len(refs) // 2
+    for ref, out_ref in zip(refs[:half], refs[half:]):
+        out_ref[...] = ref[...]
+
+
+def cut_and_send(values, rows, waits):
+    count = lax.axis_size("col")
+    cols = values.shape[1]
+    places = [origin(0)] + [origin(count - k) for k in range(1, count)]
+
+    def block(k):
+        return pl.BlockSpec((rows, cols), lambda i, p: (p[k], 0))
+
+    pieces = pl.pallas_call(
+        held(cut_kernel, 1 + count, len(waits)),
+        grid_spec=pltpu.PrefetchScalarGridSpec(
+            num_scalar_prefetch=1,
+            grid=(1,),
+            in_specs=[block(k) for k in range(count)] + [anywhere] * len(waits),
+            out_specs=[pl.BlockSpec((rows, cols), lambda i, p: (0, 0))] * count,
+        ),
+        out_shape=[jax.ShapeDtypeStruct((rows, cols), values.dtype)] * count,
+        compiler_params=pltpu.CompilerParams(vmem_limit_bytes=60 << 20),
+        name="cut",
+    )(jnp.stack(places), *[values] * count, *waits)
+    return [pieces[0]] + [shift(pieces[k], k) for k in range(1, count)]
+
+
+def narrow_kernel(left_ref, right_ref, out_ref):
+    out_ref[...] = contract_last(left_ref[...], right_ref[...]).astype(low)
+
+
+def narrow(left, right, waits):
+    return pl.pallas_call(
+        held(narrow_kernel, 2, len(waits)),
+        grid=(1,),
+        in_specs=[
+            pl.BlockSpec(left.shape, lambda i: (0, 0)),
+            pl.BlockSpec(right.shape, lambda i: (0, 0)),
+            *[anywhere] * len(waits),
+        ],
+        out_specs=pl.BlockSpec((left.shape[0], right.shape[0]), lambda i: (0, 0)),
+        out_shape=jax.ShapeDtypeStruct((left.shape[0], right.shape[0]), low),
+        compiler_params=pltpu.CompilerParams(vmem_limit_bytes=60 << 20),
+        name="narrow",
+    )(left, right, *waits)
+
+
+def portions_kernel(left_ref, grad_ref, middle_ref, heads_ref, out_ref):
+    rank = left_ref.shape[1]
+    out_ref[:rank] = contract_leading(left_ref[...], grad_ref[...]).astype(low)
+    out_ref[rank:] = contract_leading(middle_ref[...], heads_ref[...]).astype(low)
+
+
+def portions(left, grad, middle, heads, waits):
+    tokens, cols = grad.shape
+    rank, block = left.shape[1], 1024
+
+    def whole(j):
+        return (0, 0)
+
+    def part(j):
+        return (0, j)
+
+    return pl.pallas_call(
+        held(portions_kernel, 4, len(waits)),
+        grid=(cols // block,),
+        in_specs=[
+            pl.BlockSpec((tokens, rank), whole),
+            pl.BlockSpec((tokens, block), part),
+            pl.BlockSpec((tokens, rank), whole),
+            pl.BlockSpec((tokens, block), part),
+            *[anywhere] * len(waits),
+        ],
+        out_specs=pl.BlockSpec((2 * rank, block), part),
+        out_shape=jax.ShapeDtypeStruct((2 * rank, cols), low),
+        compiler_params=pltpu.CompilerParams(vmem_limit_bytes=60 << 20),
+        name="portions",
+    )(left, grad, middle, heads, *waits)
+
+
 def head_forward(proj, gain, cos, sin):
     inv = lax.rsqrt(jnp.mean(proj * proj, axis=-1, keepdims=True) + norm_eps)
     scaled = proj * inv * gain
@@ -228,31 +310,34 @@
 
 
 def attend_back_kernel(share, proj_ref, cos_ref, sin_ref, gain_ref, bias_ref, key_ref, value_ref,
-                       lse_ref, branch_ref, weight_ref, middle_ref, down_ref,
-                       out_ref, key_grad_ref, value_grad_ref, key_t):
+                       lse_ref, grad_ref, out_ref, kv_grad_ref, key_t, key_sum, value_sum):
     @pl.when(lax.rem(pl.program_id(0), share) == 0)
     def _():
         key_t[...] = key_ref[...].T
-        key_grad_ref[...] = jnp.zeros_like(key_grad_ref)
-        value_grad_ref[...] = jnp.zeros_like(value_grad_ref)
+        key_sum[...] = jnp.zeros_like(key_sum)
+        value_sum[...] = jnp.zeros_like(value_sum)
 
     proj, gain, cos, sin = proj_ref[...], gain_ref[...], cos_ref[...], sin_ref[...]
     query, inv = head_forward(proj, gain, cos, sin)
     query = query.astype(low)
-    grad = contract_last(branch_ref[...], weight_ref[...])
-    grad = (grad + product(middle_ref[...], down_ref[...])).astype(low)
+    grad = grad_ref[...]
     scores = contract_last(key_ref[...], query) * score_scale + bias_ref[...]
     probs = jnp.exp(scores - lse_ref[0])
     probs_grad = contract_last(value_ref[...], grad)
     delta = jnp.sum(probs * probs_grad, axis=0, keepdims=True)
     scores_grad = (probs * (probs_grad - delta)).astype(low)
-    value_grad_ref[...] += product(probs.astype(low), grad)
-    key_grad_ref[...] += product(scores_grad, query) * score_scale
+    value_sum[...] += product(probs.astype(low), grad)
+    key_sum[...] += product(scores_grad, query)
     rotated = product(key_t[...], scores_grad).T * score_scale
     scaled = rotated * cos + pltpu.roll(rotated * sin, HEAD_WIDTH // 2, 1)
     scaled = scaled * gain
     slope = jnp.mean(scaled * proj, axis=-1, keepdims=True)
     out_ref[...] = (inv * scaled - proj * (inv * inv * inv * slope)).astype(low)
+
+    @pl.when(lax.rem(pl.program_id(0), share) == share - 1)
+    def _():
+        kv_grad_ref[:, :HEAD_WIDTH] = (key_sum[...] * score_scale).astype(low)
+        kv_grad_ref[:, HEAD_WIDTH:] = value_sum[...].astype(low)
 
 
 def head_specs(tokens, length, first, share, kv_total):
@@ -305,51 +390,43 @@
     )(proj, cos, sin, gain, bias, keys_values, keys_values)
 
 
-def attend_back(part, parts, proj, cos, sin, gain, bias, keys_values, lse, branch, weight, middle, down,
-                filled, waits):
+def attend_back(first, heads, proj, cos, sin, gain, bias, keys_values, lse, grad, kv_span, filled, waits):
     tokens, length = proj.shape[0], keys_values.shape[0]
-    total, width, rank = proj.shape[1] // HEAD_WIDTH, branch.shape[1], middle.shape[1]
+    total = proj.shape[1] // HEAD_WIDTH
     kv_total = keys_values.shape[1] // (2 * HEAD_WIDTH)
-    share, heads = total // kv_total, total // parts
-    first = part * heads
-
-    def fixed(h):
-        return (0, 0)
+    share = total // kv_total
+    kv_first, kv_end = kv_span
 
     def head(h):
         return (0, first + h)
 
-    def kv_head(h):
-        return (0, (first + h) // share)
-
     return pl.pallas_call(
-        held(functools.partial(attend_back_kernel, share), 12, len(filled) + len(waits)),
+        held(functools.partial(attend_back_kernel, share), 9, len(filled) + len(waits)),
         grid=(heads,),
         in_specs=head_specs(tokens, length, first, share, kv_total)
         + [
             pl.BlockSpec((1, 1, tokens), lambda h: (first + h, 0, 0)),
-            pl.BlockSpec((tokens, width), fixed),
-            pl.BlockSpec((HEAD_WIDTH, width), lambda h: (first + h, 0)),
-            pl.BlockSpec((tokens, rank), fixed),
-            pl.BlockSpec((rank, HEAD_WIDTH), head),
+            pl.BlockSpec((tokens, HEAD_WIDTH), head),
             *[anywhere] * (len(filled) + len(waits)),
         ],
         out_specs=[
             pl.BlockSpec((tokens, HEAD_WIDTH), head),
-            pl.BlockSpec((length, HEAD_WIDTH), kv_head),
-            pl.BlockSpec((length, HEAD_WIDTH), kv_head),
-        ],
-        scratch_shapes=[pltpu.VMEM((HEAD_WIDTH, length), low)],
+            pl.BlockSpec((length, 2 * HEAD_WIDTH), lambda h: (0, (first + h) // share - kv_first)),
+        ],
+        scratch_shapes=[
+            pltpu.VMEM((HEAD_WIDTH, length), low),
+            pltpu.VMEM((length, HEAD_WIDTH), wide),
+            pltpu.VMEM((length, HEAD_WIDTH), wide),
+        ],
         out_shape=[
             jax.ShapeDtypeStruct(proj.shape, low),
-            jax.ShapeDtypeStruct((length, kv_total * HEAD_WIDTH), wide),
-            jax.ShapeDtypeStruct((length, kv_total * HEAD_WIDTH), wide),
-        ],
-        input_output_aliases={12 + i: i for i in range(len(filled))},
+            jax.ShapeDtypeStruct((length, (kv_end - kv_first) * 2 * HEAD_WIDTH), low),
+        ],
+        input_output_aliases={9 + i: i for i in range(len(filled))},
         compiler_params=pltpu.CompilerParams(vmem_limit_bytes=60 << 20),
         cost_estimate=pl.CostEstimate(flops=0, bytes_accessed=0, transcendentals=0),
         name="attend_back",
-    )(proj, cos, sin, gain, bias, keys_values, keys_values, lse, branch, weight, middle, down, *filled, *waits)
+    )(proj, cos, sin, gain, bias, keys_values, keys_values, lse, grad, *filled, *waits)
 
 
 def experts_kernel(place_ref, normed_ref, back_ref, weight_ref, gate_ref, up_ref, down_ref,
@@ -481,47 +558,59 @@
     )(arrived, post, probs, router, resid, gain, cot, up)
 
 
-def update_kernel(rates, count, slot_ref, square_ref, *refs):
-    size = len(rates)
-    whole, own = refs[:count], refs[count : count + size]
-    state = refs[count + size : count + 4 * size]
-    norm_ref = refs[count + 4 * size]
-    outs = refs[count + 4 * size + 1 : count + 7 * size + 1]
-    sums, factor_ref = refs[count + 7 * size + 1 : -1], refs[-1]
+def update_kernel(rates, rank, row_width, slot_ref, place_ref, square_ref, head_ref, last_ref, *refs):
+    size = 3 * len(rates)
+    state, norm_ref, outs = refs[:size], refs[size], refs[size + 1 : 2 * size + 1]
+    head_sum, last_sum, factor_ref = refs[2 * size + 1 :]
     now = pl.program_id(0)
 
     @pl.when(now == 0)
     def _():
-        total = square_ref[...]
-        for trees_ref, sum_ref in zip((*whole, *own), sums):
-            sum_ref[...] = jnp.zeros_like(sum_ref)
-
-            def tree(t, carry, trees_ref=trees_ref, sum_ref=sum_ref):
-                at = slot_ref[t]
-                sum_ref[at] += trees_ref[t].astype(wide)
-                return carry
-
-            lax.fori_loop(0, trees_ref.shape[0], tree, 0)
-        for sum_ref in sums[:count]:
-
-            def square(s, carry, sum_ref=sum_ref):
-                part = jnp.sum(sum_ref[s] * sum_ref[s], axis=0, keepdims=True)
-                return carry + jnp.sum(part, axis=1, keepdims=True)
-
-            total = lax.fori_loop(0, sum_ref.shape[0], square, total)
-        norm = jnp.sqrt(total)
+        head_sum[...] = jnp.zeros_like(head_sum)
+        last_sum[...] = jnp.zeros_like(last_sum)
+
+        def tree(t, carry):
+            at = slot_ref[t]
+            head_sum[at] += head_ref[t].astype(wide)
+            last_sum[at] += last_ref[t].astype(wide)
+            return carry
+
+        lax.fori_loop(0, head_ref.shape[0], tree, 0)
+
+        def square(s, carry):
+            head, last = head_sum[s, 2 * rank :], last_sum[s]
+            head = jnp.sum(head * head, axis=0, keepdims=True)
+            last = jnp.sum(last * last, axis=0, keepdims=True)
+            return carry + jnp.sum(head, axis=1, keepdims=True) + jnp.sum(last, axis=1, keepdims=True)
+
+        norm = jnp.sqrt(lax.fori_loop(0, head_sum.shape[0], square, square_ref[...]))
         norm_ref[...] = norm
         factor_ref[...] = jnp.minimum(1.0, clip_limit / (norm + 1e-06))
 
+    chunk = pl.multiple_of(2 * rank * (1 + place_ref[0]), 2 * rank)
+    inside = pl.ds(pl.multiple_of(place_ref[1], HEAD_WIDTH), row_width)
+    across = pl.ds(pl.multiple_of(place_ref[2], HEAD_WIDTH), row_width)
+    up = head_sum[now, pl.ds(chunk, rank), inside]
+    query_in = head_sum[now, pl.ds(chunk + rank, rank), inside]
+    kv_in = last_sum[now, : 2 * rank, across]
+    kv = last_sum[now, 2 * rank :, :]
+    kv_cols = state[-1].shape[2]
+    grads = (
+        head_sum[now, :rank, :],
+        head_sum[now, rank : 2 * rank, :],
+        up,
+        jnp.concatenate([query_in, kv_in], axis=0),
+        jnp.concatenate([kv[:, i : i + kv_cols] for i in range(0, kv.shape[1], kv_cols)], axis=0),
+    )
     factor = factor_ref[...]
-    for i, rate in enumerate(rates):
+    for i, (grad, rate) in enumerate(zip(grads, rates)):
         weight, first, second = (ref[0] for ref in state[3 * i : 3 * i + 3])
-        new = moment_update(weight, first, second, sums[count + i][now] * factor, rate)
+        new = moment_update(weight, first, second, grad * factor, rate)
         for ref, value in zip(outs[3 * i : 3 * i + 3], new):
             ref[0] = value
 
 
-def update(slots, square, whole, own, states, rates):
+def update(slots, place, square, head_trees, last_trees, states, rates, rank, row_width):
     state = [array for triple in states for array in triple]
     adapters = state[0].shape[0]
 
@@ -532,19 +621,22 @@
         return pl.BlockSpec((1, *array.shape[1:]), lambda s: (s, 0, 0))
 
     out = pl.pallas_call(
-        functools.partial(update_kernel, tuple(rates), len(whole)),
+        functools.partial(update_kernel, tuple(rates), rank, row_width),
         grid=(adapters,),
-        in_specs=[pl.BlockSpec(memory_space=pltpu.SMEM)]
-        + [all_of(a) for a in (square, *whole, *own)]
+        in_specs=[pl.BlockSpec(memory_space=pltpu.SMEM)] * 2
+        + [all_of(a) for a in (square, head_trees, last_trees)]
         + [one_of(a) for a in state],
         out_specs=[all_of(square)] + [one_of(a) for a in state],
         out_shape=[jax.ShapeDtypeStruct((1, 1), wide)]
         + [jax.ShapeDtypeStruct(a.shape, wide) for a in state],
-        scratch_shapes=[pltpu.VMEM((adapters, *a.shape[1:]), wide) for a in (*whole, *own)]
-        + [pltpu.VMEM((1, 1), wide)],
+        scratch_shapes=[
+            pltpu.VMEM((adapters, *head_trees.shape[1:]), wide),
+            pltpu.VMEM((adapters, *last_trees.shape[1:]), wide),
+            pltpu.VMEM((1, 1), wide),
+        ],
         compiler_params=pltpu.CompilerParams(vmem_limit_bytes=60 << 20),
         name="update",
-    )(slots, square, *whole, *own, *state)
+    )(slots, place, square, head_trees, last_trees, *state)
     return out[0], [out[1 + 3 * i : 4 + 3 * i] for i in range(len(states))]
 
 
@@ -750,15 +842,13 @@
         arrived, post, own_probs, router_rows, resid, expert_norm_gain[None, :], cot_own, up_output
     )
     mixture_sent = mixture_hop(1, None, low, arrived)
-    filled = ()
-    for part in range(4):
-        waits = ()
-        if part in (1, 3):
-            mixture_sent = mixture_hop(part // 2 + 2, shift(mixture_sent, 1), low, filled[0])
-            waits = (mixture_sent,)
-        filled = attend_back(
-            part,
-            4,
+    heads_grad = project(branch_grad, out_weight, mid_out_grad, down_output, True, low)
+    head_count = proj.shape[1] // HEAD_WIDTH
+
+    def heads_back(first, count, kv_span, filled, *waits):
+        return attend_back(
+            first * head_count // 4,
+            count * head_count // 4,
             proj,
             cos,
             sin,
@@ -766,36 +856,30 @@
             bias,
             keys_values,
             totals,
-            branch_grad,
-            out_weight,
-            mid_out_grad,
-            down_output,
+            heads_grad,
+            kv_span,
             filled,
             waits,
         )
-    query_grad, *kv_grads = filled
-    mid_query_grad = contract_last(query_grad, query_raise).astype(low)
+
+    filled = heads_back(0, 1, (0, kv_total // 2), ())
+    mixture_sent = mixture_hop(2, shift(mixture_sent, 1), low, filled[0])
+    query_grad, kv_grad = heads_back(1, 1, (0, kv_total // 2), filled, mixture_sent)
+    pieces = cut_and_send(kv_grad, tokens, ())
     mixture_arrived = shift(mixture_sent, 1)
-
-    def kv_hop(k, arrived, dtype, *waits):
-        return hop(origin(k), arrived, kv_grads, (tokens, kv_cols), dtype, waits)
-
-    kv_sent = kv_hop(1, None, low, mixture_arrived)
-    normed_query_grad = project(query_grad, query_weight, mid_query_grad, down_input[:rank], True, wide, (kv_sent,))
-    for k in range(2, col_count):
-        kv_sent = kv_hop(k, shift(kv_sent, 1), low, normed_query_grad)
-        if k == 2:
-            kv_second = kv_sent
-    kv_own = kv_hop(col_count, shift(kv_sent, 1), wide)
-    for k in range(3, col_count):
-        last = k == col_count - 1
-        mixture_sent = mixture_hop(k + 1, mixture_arrived, wide if last else low)
-        mixture_arrived = None if last else shift(mixture_sent, 1)
-    moe_slice = mixture_sent
-    resid_slice = lax.dynamic_slice_in_dim(resid_full, col_index * col_width, col_width, 1)
-    layer_output = resid_slice.astype(wide) + moe_slice
-    key_grad = keys_back(kv_own[:, :kv_cols])[0].astype(low)
-    value_grad = kv_own[:, kv_cols:].astype(low)
+    query_grad, kv_grad = heads_back(2, 2, (kv_total // 2, kv_total), (query_grad,))
+    kv_own = [summed(pieces, (query_grad, mixture_arrived)), None]
+    pieces = cut_and_send(kv_grad, tokens, (kv_own[0],))
+    mid_query_grad = narrow(query_grad, query_raise, (pieces[0],))
+    head_part = portions(middle[:, :rank], query_grad, mid_out_grad, heads, (pieces[0],))
+    normed_query_grad = project(
+        query_grad, query_weight, mid_query_grad, down_input[:rank], True, wide, (head_part,)
+    )
+    kv_own[1] = tree_sum(pieces)
+    kv_own = jnp.concatenate([half.astype(wide) for half in kv_own], axis=1)
+    kv_split = [kv_own[:, i : i + HEAD_WIDTH] for i in range(0, 2 * kv_cols, HEAD_WIDTH)]
+    key_grad = keys_back(jnp.concatenate(kv_split[0::2], axis=1))[0].astype(low)
+    value_grad = jnp.concatenate(kv_split[1::2], axis=1).astype(low)
     kv_proj_grad = jnp.concatenate([key_grad, value_grad], axis=1)
     mid_kv_grad = jnp.concatenate(
         [
@@ -804,35 +888,17 @@
         ],
         axis=1,
     ).astype(low)
-    mid_grad = jnp.concatenate([mid_query_grad, mid_kv_grad], axis=1)
-    normed_in_grad = (
-        normed_query_grad
-        + product(kv_proj_grad, key_value_weight)
-        + product(mid_kv_grad, local_in)
-    )
-    input_grad_own = (resid_grad + norm_in_back(normed_in_grad)[0]).astype(low)
-    def of_all(part):
-        return tree_sum([part] + [shift(part, k) for k in range(1, col_count)])
-
-    up_part = contract_leading(middle_output, branch_grad).astype(low).reshape(-1, group_cols)
-    head_part = jnp.concatenate(
-        [contract_leading(middle[:, :rank], query_grad), contract_leading(mid_out_grad, heads)]
+
+    def folded(part, cols):
+        return jnp.concatenate([part[:, i : i + cols] for i in range(0, part.shape[1], cols)])
+
+    early_part = jnp.concatenate(
+        [contract_leading(middle_output, branch_grad), contract_leading(mid_query_grad, normalized)]
     ).astype(low)
-
+    early_part = folded(early_part, group_cols)
     def head_piece(c):
         piece = lax.dynamic_slice_in_dim(head_part, c * group_cols, group_cols, 1)
-        return jnp.concatenate([piece, up_part])
-
-    head_trees = lax.all_gather(summed(exchange(head_piece), (kv_second,)), "row", axis=0)
-    slot_hot = (slots[None, :] == jnp.arange(adapters, dtype=jnp.int32)[:, None]).astype(low)
-    up_trees = head_trees[:, 2 * rank :].reshape(-1, rank, width)
-    head_own = head_trees[:, : 2 * rank]
-    head_square = jnp.einsum("st,tij->sij", slot_hot, head_own, preferred_element_type=wide)
-    head_square = jnp.full((1, HEAD_WIDTH), jnp.sum(head_square * head_square))
-    head_square = of_all(head_square)[:, :1]
-    wait = nought(head_square)
-    pieces = exchange(lambda c: lax.dynamic_slice_in_dim(input_grad_own, c * col_width + wait, col_width, 1))
-    input_grad = in_order(pieces, 0).astype(wide)
+        return jnp.concatenate([piece, early_part])
 
     kv_portion = jnp.concatenate(
         [
@@ -840,13 +906,40 @@
             contract_leading(middle[:, 2 * rank :], value_grad),
         ]
     )
-    in_portion = contract_leading(mid_grad, normalized)
-    last_part = of_all(jnp.concatenate([in_portion, kv_portion.reshape(-1, width)]).astype(low))
-    last_trees = lax.all_gather(last_part.astype(low), "row", axis=0)
-    row_start = row_index * row_width
-    in_own = lax.dynamic_slice_in_dim(last_trees[:, : 3 * rank], row_start, row_width, 2)
-    up_own = lax.dynamic_slice_in_dim(up_trees, row_start, row_width, 2)
-    kv_own_trees = last_trees[:, 3 * rank :].reshape(-1, 2 * rank, kv_cols)
+    kv_rows = 2 * rank * kv_cols // width
+    kv_portion = jnp.concatenate(
+        [kv_portion[i : i + kv_rows] for i in range(0, 2 * rank, kv_rows)], axis=1
+    )
+    last_part = jnp.concatenate([contract_leading(mid_kv_grad, normalized), kv_portion]).astype(low)
+    last_pieces = [last_part] + [shift(last_part, k) for k in range(1, col_count)]
+    last_trees = lax.all_gather(tree_sum(last_pieces).astype(low), "row", axis=0)
+    head_trees = lax.all_gather(summed(exchange(head_piece), ()), "row", axis=0)
+    slot_hot = (slots[None, :] == jnp.arange(adapters, dtype=jnp.int32)[:, None]).astype(low)
+    head_square = jnp.einsum(
+        "st,tij->sij", slot_hot, head_trees[:, : 2 * rank], preferred_element_type=wide
+    )
+    head_square = jnp.full((1, HEAD_WIDTH), jnp.sum(head_square * head_square))
+    head_square = tree_sum([head_square] + [shift(head_square, k) for k in range(1, col_count)])[:, :1]
+    wait = nought(head_square)
+
+    normed_in_grad = (
+        normed_query_grad
+        + product(kv_proj_grad, key_value_weight)
+        + product(mid_kv_grad, local_in)
+    )
+    input_grad_own = (resid_grad + norm_in_back(normed_in_grad)[0]).astype(low)
+    pieces = exchange(
+        lambda c: lax.dynamic_slice_in_dim(input_grad_own, c * col_width + wait, col_width, 1)
+    )
+    input_grad = in_order(pieces, 0).astype(wide)
+    for k in range(2, col_count):
+        last = k == col_count - 1
+        waits = (last_part,) if k == 2 else ()
+        mixture_sent = mixture_hop(k + 1, mixture_arrived, wide if last else low, *waits)
+        mixture_arrived = None if last else shift(mixture_sent, 1)
+    moe_slice = mixture_sent
+    resid_slice = lax.dynamic_slice_in_dim(resid_full, col_index * col_width, col_width, 1)
+    layer_output = resid_slice.astype(wide) + moe_slice
 
     def flip(array):
         return array.transpose(0, 2, 1)
@@ -854,11 +947,14 @@
     def rows_of(array):
         return array.reshape(adapters, 2 * rank, kv_cols)
 
+    row_start = row_index * row_width
+    place = jnp.stack([row_start // group_cols, lax.rem(row_start, group_cols), row_start])
     grad_norm, following = update(
         slots,
+        place,
         head_square,
-        (up_trees, last_trees),
-        (head_own[:, :rank], head_own[:, rank:], up_own, in_own, kv_own_trees),
+        head_trees,
+        last_trees,
         (
             (adapter_query_up, query_first_moment, query_second_moment),
             tuple(map(flip, (adapter_output_down, output_down_first_moment, output_down_second_moment))),
@@ -873,6 +969,8 @@
             learning_rate_lower,
             learning_rate_upper,
         ),
+        rank,
+        row_width,
     )
     query_following, down_following, up_following, input_following, key_value_following = following
     return (

time: 818 us -> 808 us (0.988)
  waiting for transfers between devices: 302 us -> 289 us
  starting transfers between devices: 50.7 us -> 60.2 us
    pallas_call x8 -> x4, Pallas kernels: 28.4 us -> 14.3 us  [hop(): pl.pallas_call(held(functools.partial(hop_kernel, len(arrivals), len(own)...]
    ppermute x42 -> x45, waiting for transfers between devices: 266 us -> 253 us  [shift(): return lax.ppermute(values, 'col', pairs)]
    pallas_call x3 -> x4, Pallas kernels: 37.5 us -> 49.5 us  [project(): pl.pallas_call(held(functools.partial(project_kernel, turned), 4, len(wai...]
    ppermute x42 -> x45, starting transfers between devices: 50.4 us -> 60 us  [shift(): return lax.ppermute(values, 'col', pairs)]
    pallas_call x5 -> x8, Pallas kernels: 81.9 us -> 78.9 us  [the longest x3 53.9 us: attend_back(): pl.pallas_call(held(functools.partial(attend_back_kernel, share), 9, len(...]
    dot_general x9 -> x8, matrix products: 29.6 us -> 29 us  [contract_last(): lax.dot_general(left, right, (((1,), (1,)), ((), ())), preferred_element_...]
    unnamed x186 -> x175, local copies, waits for them, and re-layouts: 17.6 us -> 17.5 us
  transfers between devices with their start and end apart: 48 -> 51, of which waited for: 31 -> 24; matrix products, arithmetic and copies ran while one was open for 14% -> 14% of each run, Pallas kernels for 29% -> 31%
where the time goes in v2:
time: 808 us; the launch traced here: 798 us
  waiting for transfers between devices  289 us (36%)
  Pallas kernels  289 us (36%)
  local copies, waits for them, and re-layouts  65.6 us (8%)
  starting transfers between devices  60.2 us (7%)
  other arithmetic  38.8 us (5%)
  matrix products  38 us (5%)
  between operations  16.7 us (2%)
    ppermute x45, waiting for transfers between devices, shift(): return lax.ppermute(values, 'col', pairs)  253 us
    pallas_call x4, Pallas kernels, experts(): pl.pallas_call(held(experts_kernel, 7, len(waits)), grid_spec=pltpu.Prefe...  99.4 us
    ppermute x45, starting transfers between devices, shift(): return lax.ppermute(values, 'col', pairs)  60 us
    pallas_call x3, Pallas kernels, attend_back(): pl.pallas_call(held(functools.partial(attend_back_kernel, share), 9, len(...  53.9 us
    pallas_call x4, Pallas kernels, project(): pl.pallas_call(held(functools.partial(project_kernel, turned), 4, len(wai...  49.5 us
    pallas_call x1, Pallas kernels, attend(): pl.pallas_call(functools.partial(attend_kernel, share), grid=(heads,), in...  36.4 us
    all_gather x4, waiting for transfers between devices, gather_rows(): return lax.all_gather(values, 'row', axis=axis, tiled=True)  35.6 us
    dot_general x8, matrix products, contract_last(): lax.dot_general(left, right, (((1,), (1,)), ((), ())), preferred_element_...  29 us
  transfers between devices with their start and end apart: 51, of which 24 were waited for; matrix products, arithmetic and copies ran while one was open for 14% of the time, Pallas kernels for 31%

profile of v2, /device:TPU:0, one launch (start us, length us, event | category | flops | bytes accessed | tf_op | source)
XLA Modules:
  0.0 797.7 jit_solution(6586813051186287905)
XLA Ops:
  18.3 14.2 %collective-permute-done.3 = bf16[256,1024]{1,0:T(8,128)(2,1)S(1)} collective-permute-done((bf16[256,1024]{1,0:T(8,128)(2,1)}, bf16[256,1024]{1,0:T(8,128)(2,1)S(1)}, u32[]{:S(2)}, u32[]{:S(2)}) %collective-permute-start.3) | collective-permute-done | bytes 524320 | tf_op jit(solution)/shard_map/ppermute | solution.py:105
  32.5 15.0 %collective-permute-done.4 = bf16[256,1024]{1,0:T(8,128)(2,1)} collective-permute-done((bf16[256,1024]{1,0:T(8,128)(2,1)S(1)}, bf16[256,1024]{1,0:T(8,128)(2,1)}, u32[]{:S(2)}, u32[]{:S(2)}) %collective-permute-start.4) | collective-permute-done | bytes 524320 | tf_op jit(solution)/shard_map/ppermute | solution.py:105
  49.0 12.8 %collective-permute-done.5 = bf16[256,1024]{1,0:T(8,128)(2,1)} collective-permute-done((bf16[256,1024]{1,0:T(8,128)(2,1)}, bf16[256,1024]{1,0:T(8,128)(2,1)}, u32[]{:S(2)}, u32[]{:S(2)}) %collective-permute-start.5) | collective-permute-done | bytes 524320 | tf_op jit(solution)/shard_map/ppermute | solution.py:105
  64.5 12.9 %collective-permute-done.12 = bf16[1024,256]{1,0:T(8,128)(2,1)S(1)} collective-permute-done((bf16[1024,256]{1,0:T(8,128)(2,1)S(1)}, bf16[1024,256]{1,0:T(8,128)(2,1)S(1)}, u32[]{:S(2)}, u32[]{:S(2)}) %collective-permute-start.12) | collective-permute-done | bytes 524320 | tf_op jit(solution)/shard_map/ppermute | solution.py:105
  77.4 12.1 %collective-permute-done.13 = bf16[1024,256]{1,0:T(8,128)(2,1)S(1)} collective-permute-done((bf16[1024,256]{1,0:T(8,128)(2,1)S(1)}, bf16[1024,256]{1,0:T(8,128)(2,1)S(1)}, u32[]{:S(2)}, u32[]{:S(2)}) %collective-permute-start.13) | collective-permute-done | bytes 524320 | tf_op jit(solution)/shard_map/ppermute | solution.py:105
  89.8 10.8 %collective-permute-done.14 = bf16[1024,256]{1,0:T(8,128)(2,1)S(1)} collective-permute-done((bf16[1024,256]{1,0:T(8,128)(2,1)S(1)}, bf16[1024,256]{1,0:T(8,128)(2,1)S(1)}, u32[]{:S(2)}, u32[]{:S(2)}) %collective-permute-start.14) | collective-permute-done | bytes 524320 | tf_op jit(solution)/shard_map/ppermute | solution.py:105
  106.9 3.8 collective-permute-start.2
  111.2 3.8 collective-permute-start.15
  125.4 22.6 %collective-permute-done.7 = bf16[32,1024]{1,0:T(8,128)(2,1)S(1)} collective-permute-done((bf16[32,1024]{1,0:T(8,128)(2,1)}, bf16[32,1024]{1,0:T(8,128)(2,1)S(1)}, u32[]{:S(2)}, u32[]{:S(2)}) %collective-permute-start.7) | collective-permute-done | bytes 65568 | tf_op jit(solution)/shard_map/ppermute | solution.py:105
  148.0 3.2 collective-permute-start.8
  159.7 19.1 %collective-permute-done.16 = bf16[1024,512]{1,0:T(8,128)(2,1)} collective-permute-done((bf16[1024,512]{1,0:T(8,128)(2,1)S(1)}, bf16[1024,512]{1,0:T(8,128)(2,1)}, u32[]{:S(2)}, u32[]{:S(2)}) %collective-permute-start.16) | collective-permute-done | bytes 1048608 | tf_op jit(solution)/shard_map/ppermute | solution.py:105
  181.4 3.6 fusion.7
  195.5 10.8 %collective-permute-done.17 = bf16[1024,512]{1,0:T(8,128)(2,1)} collective-permute-done((bf16[1024,512]{1,0:T(8,128)(2,1)}, bf16[1024,512]{1,0:T(8,128)(2,1)}, u32[]{:S(2)}, u32[]{:S(2)}) %collective-permute-start.17) | collective-permute-done | bytes 1048608 | tf_op jit(solution)/shard_map/ppermute | solution.py:105
  208.6 4.8 collective-permute-done.9
  214.8 17.0 %fusion.refs_4_.refs_2_ = f32[1024,3072]{1,0:T(8,128)} fusion(bf16[1024,2048]{1,0:T(8,128)(2,1)} %constant_dynamic-update-slice_fusion.17, bf16[4640,2048]{1,0:T(8,128)(2,1)S(1)} %copy-done), kind=kOutput, calls=%fused_computation | convolution fusion | flops 12884901888 | bytes 29360128 | tf_op jit(solution)/shard_map/dot_general | solution.py:31
  234.9 12.4 %project.4.proj_ref.refs_0_ = f32[256,4096]{1,0:T(8,128)} custom-call(bf16[256,2048]{1,0:T(8,128)(2,1)} %copy-done.5, bf16[2048,4096]{1,0:T(8,128)(2,1)} %all-gather.9.cloned.1.call-done.refs_1_, bf16[256,16]{1,0:T(8,128)(2,1)} %bitcast.113, bf16[16,4096]{1,0:T(8,128)(2,1)} %get-tuple-element.162.refs_3_.refs_1_), custom_call_target="tpu_custom_call" | custom-call | tf_op jit(solution)/shard_map/project/pallas_call | solution.py:84
  252.1 36.4 %attend.1 = (bf16[256,4096]{1,0:T(8,128)(2,1)}, f32[32,1,256]{2,1,0:T(1,128)}) custom-call(f32[256,4096]{1,0:T(8,128)} %project.4.proj_ref.refs_0_, f32[256,128]{1,0:T(8,128)} %pad_maximum_fusion.6.cos_ref.refs_1_, f32[256,128]{1,0:T(8,128)} %copy-done.9, f32[1,128]{1,0:T(1,128)} %bitcast.132, f32[1024,256]{1,0:T(8,128)} %fusion.16.bias_ref.refs_4_, ...), custom_call_target="tpu_custom_call" | custom-call | flops 12884901888 | bytes 8388608 | tf_op jit(solution)/shard_map/attend/pallas_call | solution.py:374
  291.4 17.6 %all-gather.13.cloned.1.call-done.refs_1_ = bf16[4096,2048]{1,0:T(8,128)(2,1)} async-done(((bf16[4096,256]{1,0:T(8,128)(2,1)}), bf16[4096,2048]{1,0:T(8,128)(2,1)}) %all-gather.13.cloned.1.call-update) | async-done | bytes 16777232 | tf_op jit(solution)/shard_map/all_gather | solution.py:723
  309.0 12.8 %project.5 = f32[256,2048]{1,0:T(8,128)} custom-call(bf16[256,4096]{1,0:T(8,128)(2,1)} %get-tuple-element.62.refs_0_.refs_3_, bf16[4096,2048]{1,0:T(8,128)(2,1)} %all-gather.13.cloned.1.call-done.refs_1_, bf16[256,16]{1,0:T(8,128)(2,1)} %convolution_convert_fusion.5.refs_2_, bf16[16,2048]{1,0:T(8,128)(2,1)} %get-tuple-element.130.refs_3_.up_ref, ...), custom_call_target="tpu_custom_call" | custom-call | tf_op jit(solution)/shard_map/project/pallas_call | solution.py:84
  328.3 25.6 %collective-permute-done.18 = bf16[256,2048]{1,0:T(8,128)(2,1)S(1)} collective-permute-done((bf16[256,2048]{1,0:T(8,128)(2,1)S(1)}, bf16[256,2048]{1,0:T(8,128)(2,1)S(1)}, u32[]{:S(2)}, u32[]{:S(2)}) %collective-permute-start.18) | collective-permute-done | bytes 1048608 | tf_op jit(solution)/shard_map/ppermute | solution.py:105
  355.4 24.8 %collective-permute-done.19 = bf16[256,2048]{1,0:T(8,128)(2,1)S(1)} collective-permute-done((bf16[256,2048]{1,0:T(8,128)(2,1)S(1)}, bf16[256,2048]{1,0:T(8,128)(2,1)S(1)}, u32[]{:S(2)}, u32[]{:S(2)}) %collective-permute-start.19) | collective-permute-done | bytes 1048608 | tf_op jit(solution)/shard_map/ppermute | solution.py:105
  387.8 18.0 %collective-permute-done.20 = bf16[256,2048]{1,0:T(8,128)(2,1)S(1)} collective-permute-done((bf16[256,2048]{1,0:T(8,128)(2,1)S(1)}, bf16[256,2048]{1,0:T(8,128)(2,1)S(1)}, u32[]{:S(2)}, u32[]{:S(2)}) %collective-permute-start.20) | collective-permute-done | bytes 1048608 | tf_op jit(solution)/shard_map/ppermute | solution.py:105
  406.9 3.1 fusion.2
  410.0 3.2 fusion.4.refs_1_
  418.0 18.1 %all-gather.15.cloned.1.call-done.refs_4_.refs_5_ = bf16[4,2048,1536]{2,1,0:T(8,128)(2,1)} async-done(((bf16[4,256,1536]{2,1,0:T(8,128)(2,1)}), bf16[4,2048,1536]{2,1,0:T(8,128)(2,1)}) %all-gather.15.cloned.1.call-update) | async-done | bytes 25165840 | tf_op jit(solution)/shard_map/all_gather | solution.py:723
  436.1 24.9 %experts.4 = (f32[256,2176]{1,0:T(8,128)}, bf16[1024,2048]{1,0:T(8,128)(2,1)}) custom-call(s32[2]{0:T(128)} %get-tuple-element.199.refs_0_, bf16[1024,2048]{1,0:T(8,128)(2,1)} %copy-done.1, f32[1024,3072]{1,0:T(8,128)} %fusion.refs_4_.refs_2_, f32[1024,4]{1,0:T(8,128)} %constant_dynamic-slice_fusion.10.refs_3_, ...), custom_call_target="tpu_custom_call" | custom-call | flops 16106127360 | bytes 37748736 | tf_op jit(solution)/shard_map/experts/pallas_call | solution.py:471
  464.7 24.9 %experts.5 = (f32[256,2176]{1,0:T(8,128)}, bf16[1024,2048]{1,0:T(8,128)(2,1)}) custom-call(s32[2]{0:T(128)} %get-tuple-element.198.refs_0_, bf16[1024,2048]{1,0:T(8,128)(2,1)} %copy-done.1, f32[1024,3072]{1,0:T(8,128)} %fusion.refs_4_.refs_2_, f32[1024,4]{1,0:T(8,128)} %constant_dynamic-slice_fusion.10.refs_3_, ...), custom_call_target="tpu_custom_call", output_to_operand_aliasing={{1}: (7, {})} | custom-call | flops 16106127360 | bytes 37748736 | tf_op jit(solution)/shard_map/experts/pallas_call | solution.py:471
  494.6 24.8 %experts.6 = (f32[256,2176]{1,0:T(8,128)}, bf16[1024,2048]{1,0:T(8,128)(2,1)}) custom-call(s32[2]{0:T(128)} %pad_add_fusion.1.refs_0_, bf16[1024,2048]{1,0:T(8,128)(2,1)} %copy-done.1, f32[1024,3072]{1,0:T(8,128)} %fusion.refs_4_.refs_2_, f32[1024,4]{1,0:T(8,128)} %constant_dynamic-slice_fusion.10.refs_3_, ...), custom_call_target="tpu_custom_call", output_to_operand_aliasing={{1}: (7, {})} | custom-call | flops 16106127360 | bytes 37748736 | tf_op jit(solution)/shard_map/experts/pallas_call | solution.py:471
  524.2 24.8 %experts.7 = (f32[256,2176]{1,0:T(8,128)}, bf16[1024,2048]{1,0:T(8,128)(2,1)}) custom-call(s32[2]{0:T(128)} %pad_add_fusion.refs_0_, bf16[1024,2048]{1,0:T(8,128)(2,1)} %copy-done.1, f32[1024,3072]{1,0:T(8,128)} %fusion.refs_4_.refs_2_, f32[1024,4]{1,0:T(8,128)} %constant_dynamic-slice_fusion.10.refs_3_, ...), custom_call_target="tpu_custom_call", output_to_operand_aliasing={{1}: (7, {})} | custom-call | flops 16106127360 | bytes 37748736 | tf_op jit(solution)/shard_map/experts/pallas_call | solution.py:471
  551.2 3.4 hop.4
  554.6 6.4 settle.1
  561.0 12.0 %project.6.refs_8_ = bf16[256,4096]{1,0:T(8,128)(2,1)} custom-call(bf16[256,2048]{1,0:T(8,128)(2,1)} %get-tuple-element.72.refs_0_, bf16[4096,2048]{1,0:T(8,128)(2,1)} %all-gather.13.cloned.1.call-done.refs_1_, bf16[256,16]{1,0:T(8,128)(2,1)} %get-tuple-element.73.refs_2_, bf16[16,4096]{1,0:T(8,128)(2,1)} %get-tuple-element.161.refs_3_), custom_call_target="tpu_custom_call" | custom-call | tf_op jit(solution)/shard_map/project/pallas_call | solution.py:84
  572.9 14.0 %attend_back.3 = (bf16[256,4096]{1,0:T(8,128)(2,1)}, bf16[1024,512]{1,0:T(8,128)(2,1)}) custom-call(f32[256,4096]{1,0:T(8,128)} %project.4.proj_ref.refs_0_, f32[256,128]{1,0:T(8,128)} %pad_maximum_fusion.6.cos_ref.refs_1_, f32[256,128]{1,0:T(8,128)} %copy-done.9, f32[1,128]{1,0:T(1,128)} %bitcast.133, f32[1024,256]{1,0:T(8,128)} %fusion.16.bias_ref.refs_4_, ...), custom_call_target="tpu_custom_call" | custom-call | tf_op jit(solution)/shard_map/attend_back/pallas_call | solution.py:403
  588.0 3.6 hop.5.refs_11_
  592.3 14.0 %attend_back.4 = (bf16[256,4096]{1,0:T(8,128)(2,1)}, bf16[1024,512]{1,0:T(8,128)(2,1)}) custom-call(f32[256,4096]{1,0:T(8,128)} %project.4.proj_ref.refs_0_, f32[256,128]{1,0:T(8,128)} %pad_maximum_fusion.6.cos_ref.refs_1_, f32[256,128]{1,0:T(8,128)} %copy-done.9, f32[1,128]{1,0:T(1,128)} %bitcast.134, ...), custom_call_target="tpu_custom_call", output_to_operand_aliasing={{0}: (9, {}), {1}: (10, {})} | custom-call | tf_op jit(solution)/shard_map/attend_back/pallas_call | solution.py:403
  616.7 25.8 %attend_back.5 = (bf16[256,4096]{1,0:T(8,128)(2,1)}, bf16[1024,512]{1,0:T(8,128)(2,1)}) custom-call(f32[256,4096]{1,0:T(8,128)} %project.4.proj_ref.refs_0_, f32[256,128]{1,0:T(8,128)} %pad_maximum_fusion.6.cos_ref.refs_1_, f32[256,128]{1,0:T(8,128)} %copy-done.9, f32[1,128]{1,0:T(1,128)} %bitcast.135, ...), custom_call_target="tpu_custom_call", output_to_operand_aliasing={{0}: (9, {})} | custom-call | tf_op jit(solution)/shard_map/attend_back/pallas_call | solution.py:403
  648.6 4.3 portions.1.refs_4_
  666.7 6.1 collective-permute-start.34
  672.9 12.3 %project.7 = f32[256,2048]{1,0:T(8,128)} custom-call(bf16[256,4096]{1,0:T(8,128)(2,1)} %get-tuple-element.83.refs_4_.refs_0_.refs_1_, bf16[2048,4096]{1,0:T(8,128)(2,1)} %all-gather.9.cloned.1.call-done.refs_1_, bf16[256,16]{1,0:T(8,128)(2,1)} %narrow.1.refs_2_, bf16[16,2048]{1,0:T(8,128)(2,1)} %get-tuple-element.128.refs_3_, bf16[32,4096]{1,0:T(8,128)(2,1)} %portions.1.refs_4_), custom_call_target="tpu_custom_call" | custom-call | tf_op jit(solution)/shard_map/project/pallas_call | solution.py:84
  685.2 10.7 %collective-permute-done.34.refs_2_ = bf16[96,1024]{1,0:T(8,128)(2,1)S(1)} collective-permute-done((bf16[96,1024]{1,0:T(8,128)(2,1)S(1)}, bf16[96,1024]{1,0:T(8,128)(2,1)S(1)}, u32[]{:S(2)}, u32[]{:S(2)}) %collective-permute-start.34) | collective-permute-done | bytes 196640 | tf_op jit(solution)/shard_map/ppermute | solution.py:105
  703.1 3.3 collective-permute-start.42
  706.9 3.6 hop.6
  712.0 4.8 fusion.5
  716.8 23.0 %collective-permute-done.42 = bf16[40,2048]{1,0:T(8,128)(2,1)S(1)} collective-permute-done((bf16[40,2048]{1,0:T(8,128)(2,1)S(1)}, bf16[40,2048]{1,0:T(8,128)(2,1)S(1)}, u32[]{:S(2)}, u32[]{:S(2)}) %collective-permute-start.42) | collective-permute-done | bytes 163872 | tf_op jit(solution)/shard_map/ppermute | solution.py:105
  747.2 4.0 collective-permute-start.37
  755.8 3.8 hop.7
  769.6 12.0 %update.1 = (f32[1,1]{1,0:T(1,128)}, f32[8,16,1024]{2,1,0:T(8,128)}, f32[8,16,1024]{2,1,0:T(8,128)}, f32[8,16,1024]{2,1,0:T(8,128)}, f32[8,16,1024]{2,1,0:T(8,12...) custom-call(s32[8]{0:T(128)} %copy-done.81, ...), custom_call_target="tpu_custom_call" | custom-call | tf_op jit(solution)/shard_map/update/pallas_call | solution.py:623
  784.4 3.6 collective-permute-done.40
  (405 shorter events, 172.4 us)
Async XLA Ops:
  7.2 172.8 %all-gather.11.cloned.1.call-start = ((), (), s32[]{:S(2)}) async-start(), calls=%async_computation.1 | async-start | bytes 21381120 | tf_op jit(solution)/shard_map/all_gather | solution.py:723
  15.2 219.8 %all-gather.9.cloned.1.call-start = ((), (), s32[]{:S(2)}) async-start(), calls=%async_computation | async-start | bytes 18874368 | tf_op jit(solution)/shard_map/all_gather | solution.py:723
  15.2 17.2 %collective-permute-start.3 = (bf16[256,1024]{1,0:T(8,128)(2,1)}, bf16[256,1024]{1,0:T(8,128)(2,1)S(1)}, u32[]{:S(2)}, u32[]{:S(2)}) collective-permute-start(bf16[256,1024]{1,0:T(8,128)(2,1)} %param.38), channel_id=1, source_target_pairs={{0,1},{1,2},{2,3},{3,0},{4,5},{5,6},{6,7},{7,4},{8,9},{9,10},{10,1... | collective-permute-start | bytes 1572872 | tf_op jit(solution)/shard_map/ppermute | solution.py:105
  32.5 15.0 %collective-permute-start.4 = (bf16[256,1024]{1,0:T(8,128)(2,1)S(1)}, bf16[256,1024]{1,0:T(8,128)(2,1)}, u32[]{:S(2)}, u32[]{:S(2)}) collective-permute-start(bf16[256,1024]{1,0:T(8,128)(2,1)S(1)} %collective-permute-done.3), channel_id=1, source_target_pairs={{0,1},{1,2},{2,3},{3,0},{4,5},{5,6},{6,7},{7,4},{8,9},{9,10},{10,1... | collective-permute-start | bytes 1572872 | tf_op jit(solution)/shard_map/ppermute | solution.py:105
  47.5 14.3 %collective-permute-start.5 = (bf16[256,1024]{1,0:T(8,128)(2,1)}, bf16[256,1024]{1,0:T(8,128)(2,1)}, u32[]{:S(2)}, u32[]{:S(2)}) collective-permute-start(bf16[256,1024]{1,0:T(8,128)(2,1)} %collective-permute-done.4), channel_id=1, source_target_pairs={{0,1},{1,2},{2,3},{3,0},{4,5},{5,6},{6,7},{7,4},{8,9},{9,10},{10,1... | collective-permute-start | bytes 1572872 | tf_op jit(solution)/shard_map/ppermute | solution.py:105
  64.4 244.6 %all-gather.13.cloned.1.call-start = ((), (), s32[]{:S(2)}) async-start(), calls=%async_computation.2 | async-start | bytes 18874368 | tf_op jit(solution)/shard_map/all_gather | solution.py:723
  64.4 13.0 %collective-permute-start.12 = (bf16[1024,256]{1,0:T(8,128)(2,1)S(1)}, bf16[1024,256]{1,0:T(8,128)(2,1)S(1)}, u32[]{:S(2)}, u32[]{:S(2)}) collective-permute-start(bf16[1024,256]{1,0:T(8,128)(2,1)S(1)} %copy-done.39), channel_id=1, source_target_pairs={{0,1},{1,2},{2,3},{3,0},{4,5},{5,6},{6,7},{7,4},{8,9},{9,10},{10,1... | collective-permute-start | bytes 1572872 | tf_op jit(solution)/shard_map/ppermute | solution.py:105
  77.4 12.1 %collective-permute-start.13 = (bf16[1024,256]{1,0:T(8,128)(2,1)S(1)}, bf16[1024,256]{1,0:T(8,128)(2,1)S(1)}, u32[]{:S(2)}, u32[]{:S(2)}) collective-permute-start(bf16[1024,256]{1,0:T(8,128)(2,1)S(1)} %collective-permute-done.12), channel_id=1, source_target_pairs={{0,1},{1,2},{2,3},{3,0},{4,5},{5,6},{6,7},{7,4},{8,9},{9,10},{10,1... | collective-permute-start | bytes 1572872 | tf_op jit(solution)/shard_map/ppermute | solution.py:105
  89.5 11.1 %collective-permute-start.14 = (bf16[1024,256]{1,0:T(8,128)(2,1)S(1)}, bf16[1024,256]{1,0:T(8,128)(2,1)S(1)}, u32[]{:S(2)}, u32[]{:S(2)}) collective-permute-start(bf16[1024,256]{1,0:T(8,128)(2,1)S(1)} %collective-permute-done.13), channel_id=1, source_target_pairs={{0,1},{1,2},{2,3},{3,0},{4,5},{5,6},{6,7},{7,4},{8,9},{9,10},{10,1... | collective-permute-start | bytes 1572872 | tf_op jit(solution)/shard_map/ppermute | solution.py:105
  102.0 334.1 %all-gather.15.cloned.1.call-start = ((), (), s32[]{:S(2)}) async-start(), calls=%async_computation.3 | async-start | bytes 28311552 | tf_op jit(solution)/shard_map/all_gather | solution.py:723
  102.6 641.8 %all-gather.17.cloned.1.call-start = ((), (), s32[]{:S(2)}) async-start(), calls=%async_computation.4 | async-start | bytes 1769472 | tf_op jit(solution)/shard_map/all_gather | solution.py:916
  105.8 18.0 %collective-permute-start.6 = (bf16[32,1024]{1,0:T(8,128)(2,1)}, bf16[32,1024]{1,0:T(8,128)(2,1)}, u32[]{:S(2)}, u32[]{:S(2)}) collective-permute-start(bf16[32,1024]{1,0:T(8,128)(2,1)} %get-tuple-element.185), channel_id=1, source_target_pairs={{0,1},{1,2},{2,3},{3,0},{4,5},{5,6},{6,7},{7,4},{8,9},{9,10},{10,1... | collective-permute-start | bytes 196616 | tf_op jit(solution)/shard_map/ppermute | solution.py:105
  106.9 51.2 %collective-permute-start.2 = (bf16[256,512]{1,0:T(8,128)(2,1)}, bf16[256,512]{1,0:T(8,128)(2,1)}, u32[]{:S(2)}, u32[]{:S(2)}) collective-permute-start(bf16[256,512]{1,0:T(8,128)(2,1)} %get-tuple-element.135), channel_id=1, source_target_pairs={{0,3},{1,0},{2,1},{3,2},{4,7},{5,4},{6,5},{7,6},{8,11},{9,8},{10,9... | collective-permute-start | bytes 786440 | tf_op jit(solution)/shard_map/ppermute | solution.py:105
  110.7 44.1 %collective-permute-start = (bf16[256,512]{1,0:T(8,128)(2,1)}, bf16[256,512]{1,0:T(8,128)(2,1)}, u32[]{:S(2)}, u32[]{:S(2)}) collective-permute-start(bf16[256,512]{1,0:T(8,128)(2,1)} %get-tuple-element.136), channel_id=1, source_target_pairs={{0,1},{1,2},{2,3},{3,0},{4,5},{5,6},{6,7},{7,4},{8,9},{9,10},{10,1... | collective-permute-start | bytes 786440 | tf_op jit(solution)/shard_map/ppermute | solution.py:105
  110.7 46.4 %collective-permute-start.1 = (bf16[256,512]{1,0:T(8,128)(2,1)}, bf16[256,512]{1,0:T(8,128)(2,1)}, u32[]{:S(2)}, u32[]{:S(2)}) collective-permute-start(bf16[256,512]{1,0:T(8,128)(2,1)} %get-tuple-element.138), channel_id=1, source_target_pairs={{0,2},{1,3},{2,0},{3,1},{4,6},{5,7},{6,4},{7,5},{8,10},{9,11},{10,... | collective-permute-start | bytes 786440 | tf_op jit(solution)/shard_map/ppermute | solution.py:105
  111.2 44.5 %collective-permute-start.15 = (bf16[1024,512]{1,0:T(8,128)(2,1)S(1)}, bf16[1024,512]{1,0:T(8,128)(2,1)S(1)}, u32[]{:S(2)}, u32[]{:S(2)}) collective-permute-start(bf16[1024,512]{1,0:T(8,128)(2,1)S(1)} %copy-done.32), channel_id=1, source_target_pairs={{0,1},{1,2},{2,3},{3,0},{4,5},{5,6},{6,7},{7,4},{8,9},{9,10},{10,1... | collective-permute-start | bytes 3145736 | tf_op jit(solution)/shard_map/ppermute | solution.py:105
  123.8 24.2 %collective-permute-start.7 = (bf16[32,1024]{1,0:T(8,128)(2,1)}, bf16[32,1024]{1,0:T(8,128)(2,1)S(1)}, u32[]{:S(2)}, u32[]{:S(2)}) collective-permute-start(bf16[32,1024]{1,0:T(8,128)(2,1)} %collective-permute-done.6), channel_id=1, source_target_pairs={{0,1},{1,2},{2,3},{3,0},{4,5},{5,6},{6,7},{7,4},{8,9},{9,10},{10,1... | collective-permute-start | bytes 196616 | tf_op jit(solution)/shard_map/ppermute | solution.py:105
  155.7 23.2 %collective-permute-start.16 = (bf16[1024,512]{1,0:T(8,128)(2,1)S(1)}, bf16[1024,512]{1,0:T(8,128)(2,1)}, u32[]{:S(2)}, u32[]{:S(2)}) collective-permute-start(bf16[1024,512]{1,0:T(8,128)(2,1)S(1)} %collective-permute-done.15), channel_id=1, source_target_pairs={{0,1},{1,2},{2,3},{3,0},{4,5},{5,6},{6,7},{7,4},{8,9},{9,10},{10,1... | collective-permute-start | bytes 3145736 | tf_op jit(solution)/shard_map/ppermute | solution.py:105
  178.9 27.4 %collective-permute-start.17 = (bf16[1024,512]{1,0:T(8,128)(2,1)}, bf16[1024,512]{1,0:T(8,128)(2,1)}, u32[]{:S(2)}, u32[]{:S(2)}) collective-permute-start(bf16[1024,512]{1,0:T(8,128)(2,1)} %collective-permute-done.16), channel_id=1, source_target_pairs={{0,1},{1,2},{2,3},{3,0},{4,5},{5,6},{6,7},{7,4},{8,9},{9,10},{10,1... | collective-permute-start | bytes 3145736 | tf_op jit(solution)/shard_map/ppermute | solution.py:105
  187.7 25.7 %collective-permute-start.9 = (bf16[256,1024]{1,0:T(8,128)(2,1)S(1)}, bf16[256,1024]{1,0:T(8,128)(2,1)S(1)}, u32[]{:S(2)}, u32[]{:S(2)}) collective-permute-start(bf16[256,1024]{1,0:T(8,128)(2,1)S(1)} %fusion.25), channel_id=1, source_target_pairs={{0,1},{1,2},{2,3},{3,0},{4,5},{5,6},{6,7},{7,4},{8,9},{9,10},{10,1... | collective-permute-start | bytes 1572872 | tf_op jit(solution)/shard_map/ppermute | solution.py:105
  213.4 18.4 %collective-permute-start.10 = (bf16[256,1024]{1,0:T(8,128)(2,1)S(1)}, bf16[256,1024]{1,0:T(8,128)(2,1)}, u32[]{:S(2)}, u32[]{:S(2)}) collective-permute-start(bf16[256,1024]{1,0:T(8,128)(2,1)S(1)} %collective-permute-done.9), channel_id=1, source_target_pairs={{0,1},{1,2},{2,3},{3,0},{4,5},{5,6},{6,7},{7,4},{8,9},{9,10},{10,1... | collective-permute-start | bytes 1572872 | tf_op jit(solution)/shard_map/ppermute | solution.py:105
  231.8 17.9 %collective-permute-start.11 = (bf16[256,1024]{1,0:T(8,128)(2,1)}, bf16[256,1024]{1,0:T(8,128)(2,1)}, u32[]{:S(2)}, u32[]{:S(2)}) collective-permute-start(bf16[256,1024]{1,0:T(8,128)(2,1)} %collective-permute-done.10), channel_id=1, source_target_pairs={{0,1},{1,2},{2,3},{3,0},{4,5},{5,6},{6,7},{7,4},{8,9},{9,10},{10,1... | collective-permute-start | bytes 1572872 | tf_op jit(solution)/shard_map/ppermute | solution.py:105
  326.7 27.2 %collective-permute-start.18 = (bf16[256,2048]{1,0:T(8,128)(2,1)S(1)}, bf16[256,2048]{1,0:T(8,128)(2,1)S(1)}, u32[]{:S(2)}, u32[]{:S(2)}) collective-permute-start(bf16[256,2048]{1,0:T(8,128)(2,1)S(1)} %get-tuple-element.124), channel_id=1, source_target_pairs={{0,1},{1,2},{2,3},{3,0},{4,5},{5,6},{6,7},{7,4},{8,9},{9,10},{10,1... | collective-permute-start | bytes 3145736 | tf_op jit(solution)/shard_map/ppermute | solution.py:105
  353.9 26.3 %collective-permute-start.19 = (bf16[256,2048]{1,0:T(8,128)(2,1)S(1)}, bf16[256,2048]{1,0:T(8,128)(2,1)S(1)}, u32[]{:S(2)}, u32[]{:S(2)}) collective-permute-start(bf16[256,2048]{1,0:T(8,128)(2,1)S(1)} %collective-permute-done.18), channel_id=1, source_target_pairs={{0,1},{1,2},{2,3},{3,0},{4,5},{5,6},{6,7},{7,4},{8,9},{9,10},{10,1... | collective-permute-start | bytes 3145736 | tf_op jit(solution)/shard_map/ppermute | solution.py:105
  380.2 25.6 %collective-permute-start.20 = (bf16[256,2048]{1,0:T(8,128)(2,1)S(1)}, bf16[256,2048]{1,0:T(8,128)(2,1)S(1)}, u32[]{:S(2)}, u32[]{:S(2)}) collective-permute-start(bf16[256,2048]{1,0:T(8,128)(2,1)S(1)} %collective-permute-done.19), channel_id=1, source_target_pairs={{0,1},{1,2},{2,3},{3,0},{4,5},{5,6},{6,7},{7,4},{8,9},{9,10},{10,1... | collective-permute-start | bytes 3145736 | tf_op jit(solution)/shard_map/ppermute | solution.py:105
  462.8 29.0 %collective-permute-start.21 = (bf16[256,2176]{1,0:T(8,128)(2,1)S(1)}, bf16[256,2176]{1,0:T(8,128)(2,1)S(1)}, u32[]{:S(2)}, u32[]{:S(2)}) collective-permute-start(bf16[256,2176]{1,0:T(8,128)(2,1)S(1)} %convert_element_type.148.refs_8_), channel_id=1, source_target_pairs={{0,1},{1,2},{2,3},{3,0},{4,5},{5,6},{6,7},{7,4},{8,9},{9,10},{10,1... | collective-permute-start | bytes 3342344 | tf_op jit(solution)/shard_map/ppermute | solution.py:105
  493.6 27.8 %collective-permute-start.22 = (bf16[256,2176]{1,0:T(8,128)(2,1)S(1)}, bf16[256,2176]{1,0:T(8,128)(2,1)S(1)}, u32[]{:S(2)}, u32[]{:S(2)}) collective-permute-start(bf16[256,2176]{1,0:T(8,128)(2,1)S(1)} %add_convert_fusion.1.refs_8_), channel_id=1, source_target_pairs={{0,1},{1,2},{2,3},{3,0},{4,5},{5,6},{6,7},{7,4},{8,9},{9,10},{10,1... | collective-permute-start | bytes 3342344 | tf_op jit(solution)/shard_map/ppermute | solution.py:105
  523.2 27.0 %collective-permute-start.23 = (bf16[256,2176]{1,0:T(8,128)(2,1)S(1)}, bf16[256,2176]{1,0:T(8,128)(2,1)S(1)}, u32[]{:S(2)}, u32[]{:S(2)}) collective-permute-start(bf16[256,2176]{1,0:T(8,128)(2,1)S(1)} %add_convert_fusion.refs_8_), channel_id=1, source_target_pairs={{0,1},{1,2},{2,3},{3,0},{4,5},{5,6},{6,7},{7,4},{8,9},{9,10},{10,1... | collective-permute-start | bytes 3342344 | tf_op jit(solution)/shard_map/ppermute | solution.py:105
  554.6 32.4 %collective-permute-start.24 = (bf16[1024,512]{1,0:T(8,128)(2,1)}, bf16[1024,512]{1,0:T(8,128)(2,1)S(1)}, u32[]{:S(2)}, u32[]{:S(2)}) collective-permute-start(bf16[1024,512]{1,0:T(8,128)(2,1)} %hop.4), channel_id=1, source_target_pairs={{0,1},{1,2},{2,3},{3,0},{4,5},{5,6},{6,7},{7,4},{8,9},{9,10},{10,1... | collective-permute-start | bytes 3145736 | tf_op jit(solution)/shard_map/ppermute | solution.py:105
  591.6 51.0 %collective-permute-start.25 = (bf16[1024,512]{1,0:T(8,128)(2,1)}, bf16[1024,512]{1,0:T(8,128)(2,1)S(1)}, u32[]{:S(2)}, u32[]{:S(2)}) collective-permute-start(bf16[1024,512]{1,0:T(8,128)(2,1)} %hop.5.refs_11_), channel_id=1, source_target_pairs={{0,1},{1,2},{2,3},{3,0},{4,5},{5,6},{6,7},{7,4},{8,9},{9,10},{10,1... | collective-permute-start | bytes 3145736 | tf_op jit(solution)/shard_map/ppermute | solution.py:105
  609.3 33.2 %collective-permute-start.26 = (bf16[256,512]{1,0:T(8,128)(2,1)}, bf16[256,512]{1,0:T(8,128)(2,1)S(1)}, u32[]{:S(2)}, u32[]{:S(2)}) collective-permute-start(bf16[256,512]{1,0:T(8,128)(2,1)} %get-tuple-element.80), channel_id=1, source_target_pairs={{0,1},{1,2},{2,3},{3,0},{4,5},{5,6},{6,7},{7,4},{8,9},{9,10},{10,1... | collective-permute-start | bytes 786440 | tf_op jit(solution)/shard_map/ppermute | solution.py:105
  612.2 30.3 %collective-permute-start.27 = (bf16[256,512]{1,0:T(8,128)(2,1)}, bf16[256,512]{1,0:T(8,128)(2,1)S(1)}, u32[]{:S(2)}, u32[]{:S(2)}) collective-permute-start(bf16[256,512]{1,0:T(8,128)(2,1)} %get-tuple-element.81), channel_id=1, source_target_pairs={{0,2},{1,3},{2,0},{3,1},{4,6},{5,7},{6,4},{7,5},{8,10},{9,11},{10,... | collective-permute-start | bytes 786440 | tf_op jit(solution)/shard_map/ppermute | solution.py:105
  613.6 29.0 %collective-permute-start.28 = (bf16[256,512]{1,0:T(8,128)(2,1)}, bf16[256,512]{1,0:T(8,128)(2,1)S(1)}, u32[]{:S(2)}, u32[]{:S(2)}) collective-permute-start(bf16[256,512]{1,0:T(8,128)(2,1)} %get-tuple-element.82), channel_id=1, source_target_pairs={{0,3},{1,0},{2,1},{3,2},{4,7},{5,4},{6,5},{7,6},{8,11},{9,8},{10,9... | collective-permute-start | bytes 786440 | tf_op jit(solution)/shard_map/ppermute | solution.py:105
  657.9 8.8 %collective-permute-start.35 = (bf16[96,1024]{1,0:T(8,128)(2,1)S(1)}, bf16[96,1024]{1,0:T(8,128)(2,1)S(1)}, u32[]{:S(2)}, u32[]{:S(2)}) collective-permute-start(bf16[96,1024]{1,0:T(8,128)(2,1)S(1)} %get-tuple-element.163), channel_id=1, source_target_pairs={{0,3},{1,0},{2,1},{3,2},{4,7},{5,4},{6,5},{7,6},{8,11},{9,8},{10,9... | collective-permute-start | bytes 589832 | tf_op jit(solution)/shard_map/ppermute | solution.py:105
  658.0 40.6 %collective-permute-start.29 = (bf16[256,512]{1,0:T(8,128)(2,1)}, bf16[256,512]{1,0:T(8,128)(2,1)S(1)}, u32[]{:S(2)}, u32[]{:S(2)}) collective-permute-start(bf16[256,512]{1,0:T(8,128)(2,1)} %get-tuple-element.85), channel_id=1, source_target_pairs={{0,2},{1,3},{2,0},{3,1},{4,6},{5,7},{6,4},{7,5},{8,10},{9,11},{10,... | collective-permute-start | bytes 786440 | tf_op jit(solution)/shard_map/ppermute | solution.py:105
  658.5 40.2 %collective-permute-start.30 = (bf16[256,512]{1,0:T(8,128)(2,1)}, bf16[256,512]{1,0:T(8,128)(2,1)S(1)}, u32[]{:S(2)}, u32[]{:S(2)}) collective-permute-start(bf16[256,512]{1,0:T(8,128)(2,1)} %get-tuple-element.86), channel_id=1, source_target_pairs={{0,1},{1,2},{2,3},{3,0},{4,5},{5,6},{6,7},{7,4},{8,9},{9,10},{10,1... | collective-permute-start | bytes 786440 | tf_op jit(solution)/shard_map/ppermute | solution.py:105
  660.0 38.8 %collective-permute-start.31 = (bf16[256,512]{1,0:T(8,128)(2,1)}, bf16[256,512]{1,0:T(8,128)(2,1)}, u32[]{:S(2)}, u32[]{:S(2)}) collective-permute-start(bf16[256,512]{1,0:T(8,128)(2,1)} %get-tuple-element.87), channel_id=1, source_target_pairs={{0,3},{1,0},{2,1},{3,2},{4,7},{5,4},{6,5},{7,6},{8,11},{9,8},{10,9... | collective-permute-start | bytes 786440 | tf_op jit(solution)/shard_map/ppermute | solution.py:105
  663.8 21.5 %collective-permute-start.33 = (bf16[96,1024]{1,0:T(8,128)(2,1)}, bf16[96,1024]{1,0:T(8,128)(2,1)S(1)}, u32[]{:S(2)}, u32[]{:S(2)}) collective-permute-start(bf16[96,1024]{1,0:T(8,128)(2,1)} %get-tuple-element.164), channel_id=1, source_target_pairs={{0,1},{1,2},{2,3},{3,0},{4,5},{5,6},{6,7},{7,4},{8,9},{9,10},{10,1... | collective-permute-start | bytes 589832 | tf_op jit(solution)/shard_map/ppermute | solution.py:105
  666.7 29.2 %collective-permute-start.34 = (bf16[96,1024]{1,0:T(8,128)(2,1)S(1)}, bf16[96,1024]{1,0:T(8,128)(2,1)S(1)}, u32[]{:S(2)}, u32[]{:S(2)}) collective-permute-start(bf16[96,1024]{1,0:T(8,128)(2,1)S(1)} %get-tuple-element.165), channel_id=1, source_target_pairs={{0,2},{1,3},{2,0},{3,1},{4,6},{5,7},{6,4},{7,5},{8,10},{9,11},{10,... | collective-permute-start | bytes 589832 | tf_op jit(solution)/shard_map/ppermute | solution.py:105
  698.6 70.9 %all-gather.19.cloned.1.call-start = ((), (), s32[]{:S(2)}) async-start(), calls=%async_computation.5 | async-start | bytes 1474560 | tf_op jit(solution)/shard_map/all_gather | solution.py:915
  703.0 13.8 %collective-permute-start.43 = (bf16[40,2048]{1,0:T(8,128)(2,1)S(1)}, bf16[40,2048]{1,0:T(8,128)(2,1)S(1)}, u32[]{:S(2)}, u32[]{:S(2)}) collective-permute-start(bf16[40,2048]{1,0:T(8,128)(2,1)S(1)} %maximum_maximum_fusion.refs_3_), channel_id=1, source_target_pairs={{0,1},{1,2},{2,3},{3,0},{4,5},{5,6},{6,7},{7,4},{8,9},{9,10},{10,1... | collective-permute-start | bytes 491528 | tf_op jit(solution)/shard_map/ppermute | solution.py:105
  703.1 36.7 %collective-permute-start.42 = (bf16[40,2048]{1,0:T(8,128)(2,1)S(1)}, bf16[40,2048]{1,0:T(8,128)(2,1)S(1)}, u32[]{:S(2)}, u32[]{:S(2)}) collective-permute-start(bf16[40,2048]{1,0:T(8,128)(2,1)S(1)} %maximum_maximum_fusion.refs_3_), channel_id=1, source_target_pairs={{0,2},{1,3},{2,0},{3,1},{4,6},{5,7},{6,4},{7,5},{8,10},{9,11},{10,... | collective-permute-start | bytes 491528 | tf_op jit(solution)/shard_map/ppermute | solution.py:105
  706.4 33.4 %collective-permute-start.44 = (bf16[40,2048]{1,0:T(8,128)(2,1)S(1)}, bf16[40,2048]{1,0:T(8,128)(2,1)S(1)}, u32[]{:S(2)}, u32[]{:S(2)}) collective-permute-start(bf16[40,2048]{1,0:T(8,128)(2,1)S(1)} %maximum_maximum_fusion.refs_3_), channel_id=1, source_target_pairs={{0,3},{1,0},{2,1},{3,2},{4,7},{5,4},{6,5},{7,6},{8,11},{9,8},{10,9... | collective-permute-start | bytes 491528 | tf_op jit(solution)/shard_map/ppermute | solution.py:105
  710.5 45.3 %collective-permute-start.32 = (bf16[1024,512]{1,0:T(8,128)(2,1)}, bf16[1024,512]{1,0:T(8,128)(2,1)}, u32[]{:S(2)}, u32[]{:S(2)}) collective-permute-start(bf16[1024,512]{1,0:T(8,128)(2,1)} %hop.6), channel_id=1, source_target_pairs={{0,1},{1,2},{2,3},{3,0},{4,5},{5,6},{6,7},{7,4},{8,9},{9,10},{10,1... | collective-permute-start | bytes 3145736 | tf_op jit(solution)/shard_map/ppermute | solution.py:105
  747.2 12.4 %collective-permute-start.37 = (f32[1,128]{1,0:T(1,128)S(1)}, f32[1,128]{1,0:T(1,128)S(1)}, u32[]{:S(2)}, u32[]{:S(2)}) collective-permute-start(f32[1,128]{1,0:T(1,128)S(1)} %broadcast_in_dim.149), channel_id=1, source_target_pairs={{0,1},{1,2},{2,3},{3,0},{4,5},{5,6},{6,7},{7,4},{8,9},{9,10},{10,1... | collective-permute-start | bytes 1544 | tf_op jit(solution)/shard_map/ppermute | solution.py:105
  763.3 25.8 %collective-permute-start.41 = (bf16[256,512]{1,0:T(8,128)(2,1)}, bf16[256,512]{1,0:T(8,128)(2,1)S(1)}, u32[]{:S(2)}, u32[]{:S(2)}) collective-permute-start(bf16[256,512]{1,0:T(8,128)(2,1)} %get-tuple-element.131), channel_id=1, source_target_pairs={{0,3},{1,0},{2,1},{3,2},{4,7},{5,4},{6,5},{7,6},{8,11},{9,8},{10,9... | collective-permute-start | bytes 786440 | tf_op jit(solution)/shard_map/ppermute | solution.py:105
  766.1 21.9 %collective-permute-start.40 = (bf16[256,512]{1,0:T(8,128)(2,1)}, bf16[256,512]{1,0:T(8,128)(2,1)}, u32[]{:S(2)}, u32[]{:S(2)}) collective-permute-start(bf16[256,512]{1,0:T(8,128)(2,1)} %get-tuple-element.132), channel_id=1, source_target_pairs={{0,2},{1,3},{2,0},{3,1},{4,6},{5,7},{6,4},{7,5},{8,10},{9,11},{10,... | collective-permute-start | bytes 786440 | tf_op jit(solution)/shard_map/ppermute | solution.py:105
  766.1 17.3 %collective-permute-start.39 = (bf16[256,512]{1,0:T(8,128)(2,1)}, bf16[256,512]{1,0:T(8,128)(2,1)}, u32[]{:S(2)}, u32[]{:S(2)}) collective-permute-start(bf16[256,512]{1,0:T(8,128)(2,1)} %get-tuple-element.133), channel_id=1, source_target_pairs={{0,1},{1,2},{2,3},{3,0},{4,5},{5,6},{6,7},{7,4},{8,9},{9,10},{10,1... | collective-permute-start | bytes 786440 | tf_op jit(solution)/shard_map/ppermute | solution.py:105
  (85 other events, 970.1 us)
Sparse Core Ops, SparseCore 0:
  15.3 105.6 all-gather.10
  123.5 89.8 all-gather.8
  215.8 93.1 all-gather.12
  310.7 125.3 all-gather.14
  698.7 25.0 all-gather.16
  740.7 25.2 all-gather.18

commit v3 on v2

--- a/solution.py
+++ b/solution.py
@@ -66,29 +66,30 @@
 anywhere = pl.BlockSpec(memory_space=pl.ANY)
 
 
-def project_kernel(turned, left_ref, weight_ref, thin_ref, thin_weight_ref, out_ref):
+def project_kernel(turned, left_ref, weight_ref, *refs):
     whole = contract_last if turned else product
-    total = whole(left_ref[...], weight_ref[...]) + product(thin_ref[...], thin_weight_ref[...])
-    out_ref[...] = total.astype(out_ref.dtype)
-
-
-def project(left, weight, thin, thin_weight, turned, dtype, waits=()):
+    total = whole(left_ref[...], weight_ref[...])
+    if len(refs) > 1:
+        total = total + product(refs[0][...], refs[1][...])
+    refs[-1][...] = total.astype(refs[-1].dtype)
+
+
+def project(left, weight, thins, turned, dtype, waits=()):
     tokens, depth = left.shape
     cols = weight.shape[0 if turned else 1]
-    rank = thin.shape[1]
     block = 512 if depth <= 2048 else 256
     if turned:
         weight_spec = pl.BlockSpec((block, depth), lambda j: (j, 0))
     else:
         weight_spec = pl.BlockSpec((depth, block), lambda j: (0, j))
     return pl.pallas_call(
-        held(functools.partial(project_kernel, turned), 4, len(waits)),
+        held(functools.partial(project_kernel, turned), 2 + len(thins), len(waits)),
         grid=(cols // block,),
         in_specs=[
             pl.BlockSpec((tokens, depth), lambda j: (0, 0)),
             weight_spec,
-            pl.BlockSpec((tokens, rank), lambda j: (0, 0)),
-            pl.BlockSpec((rank, block), lambda j: (0, j)),
+            *[pl.BlockSpec(a.shape, lambda j: (0, 0)) for a in thins[:1]],
+            *[pl.BlockSpec((a.shape[0], block), lambda j: (0, j)) for a in thins[1:]],
             *[anywhere] * len(waits),
         ],
         out_specs=pl.BlockSpec((tokens, block), lambda j: (0, j)),
@@ -96,7 +97,7 @@
         compiler_params=pltpu.CompilerParams(vmem_limit_bytes=60 << 20),
         cost_estimate=pl.CostEstimate(flops=0, bytes_accessed=0, transcendentals=0),
         name="project",
-    )(left, weight, thin, thin_weight, *waits)
+    )(left, weight, *thins, *waits)
 
 
 def shift(values, step):
@@ -205,86 +206,58 @@
     )(*parts, *waits)
 
 
-def cut_kernel(place_ref, *refs):
-    half = len(refs) // 2
-    for ref, out_ref in zip(refs[:half], refs[half:]):
-        out_ref[...] = ref[...]
-
-
-def cut_and_send(values, rows, waits):
-    count = lax.axis_size("col")
-    cols = values.shape[1]
-    places = [origin(0)] + [origin(count - k) for k in range(1, count)]
-
-    def block(k):
-        return pl.BlockSpec((rows, cols), lambda i, p: (p[k], 0))
-
-    pieces = pl.pallas_call(
-        held(cut_kernel, 1 + count, len(waits)),
+def relay_kernel(count, mids, place_ref, *refs):
+    parts, pieces = refs[:count], refs[count : 2 * count]
+    mid_refs = refs[2 * count : 2 * count + mids]
+    up_ref, normed_ref, sum_ref, *out_refs = refs[2 * count + mids :]
+    mid_ref = out_refs.pop()
+    sum_ref[...] = tree_sum([ref[...] for ref in parts]).astype(low)
+    mid = mid_refs[0][...]
+    for ref in mid_refs[1:]:
+        mid = mid + ref[...]
+    mid = mid.astype(low)
+    mid_ref[...] = mid
+    query_in = contract_leading(mid, normed_ref[...]).astype(low)
+    rank, width = query_in.shape
+    tokens, cols = pieces[0].shape
+    group = up_ref.shape[1] // count
+    for k, (ref, out_ref) in enumerate(zip(pieces, out_refs)):
+        out_ref[:tokens] = ref[...]
+        at = tokens
+        for i in range(0, group, cols):
+            start = pl.multiple_of(place_ref[k] * group + i, cols)
+            out_ref[at : at + rank] = up_ref[:, pl.ds(start, cols)]
+            at += rank
+        for i in range(0, width, cols):
+            out_ref[at : at + rank] = query_in[:, i : i + cols]
+            at += rank
+
+
+def relay(parts, pieces, mids, up, normed, waits):
+    count, rank = len(parts), up.shape[0]
+    tokens, cols = pieces[0].shape
+    rows = tokens + rank * (up.shape[1] // count + normed.shape[1]) // cols
+    places = jnp.stack([origin(0)] + [origin(count - k) for k in range(1, count)])
+    inputs = (*parts, *pieces, *mids, up, normed)
+
+    def whole(shape):
+        return pl.BlockSpec(shape, lambda i, p: (0, 0))
+
+    out = pl.pallas_call(
+        held(functools.partial(relay_kernel, count, len(mids)), 1 + len(inputs), len(waits)),
         grid_spec=pltpu.PrefetchScalarGridSpec(
             num_scalar_prefetch=1,
             grid=(1,),
-            in_specs=[block(k) for k in range(count)] + [anywhere] * len(waits),
-            out_specs=[pl.BlockSpec((rows, cols), lambda i, p: (0, 0))] * count,
-        ),
-        out_shape=[jax.ShapeDtypeStruct((rows, cols), values.dtype)] * count,
+            in_specs=[whole(a.shape) for a in inputs] + [anywhere] * len(waits),
+            out_specs=[whole(parts[0].shape)] + [whole((rows, cols))] * count + [whole((tokens, rank))],
+        ),
+        out_shape=[jax.ShapeDtypeStruct(parts[0].shape, low)]
+        + [jax.ShapeDtypeStruct((rows, cols), low)] * count
+        + [jax.ShapeDtypeStruct((tokens, rank), low)],
         compiler_params=pltpu.CompilerParams(vmem_limit_bytes=60 << 20),
-        name="cut",
-    )(jnp.stack(places), *[values] * count, *waits)
-    return [pieces[0]] + [shift(pieces[k], k) for k in range(1, count)]
-
-
-def narrow_kernel(left_ref, right_ref, out_ref):
-    out_ref[...] = contract_last(left_ref[...], right_ref[...]).astype(low)
-
-
-def narrow(left, right, waits):
-    return pl.pallas_call(
-        held(narrow_kernel, 2, len(waits)),
-        grid=(1,),
-        in_specs=[
-            pl.BlockSpec(left.shape, lambda i: (0, 0)),
-            pl.BlockSpec(right.shape, lambda i: (0, 0)),
-            *[anywhere] * len(waits),
-        ],
-        out_specs=pl.BlockSpec((left.shape[0], right.shape[0]), lambda i: (0, 0)),
-        out_shape=jax.ShapeDtypeStruct((left.shape[0], right.shape[0]), low),
-        compiler_params=pltpu.CompilerParams(vmem_limit_bytes=60 << 20),
-        name="narrow",
-    )(left, right, *waits)
-
-
-def portions_kernel(left_ref, grad_ref, middle_ref, heads_ref, out_ref):
-    rank = left_ref.shape[1]
-    out_ref[:rank] = contract_leading(left_ref[...], grad_ref[...]).astype(low)
-    out_ref[rank:] = contract_leading(middle_ref[...], heads_ref[...]).astype(low)
-
-
-def portions(left, grad, middle, heads, waits):
-    tokens, cols = grad.shape
-    rank, block = left.shape[1], 1024
-
-    def whole(j):
-        return (0, 0)
-
-    def part(j):
-        return (0, j)
-
-    return pl.pallas_call(
-        held(portions_kernel, 4, len(waits)),
-        grid=(cols // block,),
-        in_specs=[
-            pl.BlockSpec((tokens, rank), whole),
-            pl.BlockSpec((tokens, block), part),
-            pl.BlockSpec((tokens, rank), whole),
-            pl.BlockSpec((tokens, block), part),
-            *[anywhere] * len(waits),
-        ],
-        out_specs=pl.BlockSpec((2 * rank, block), part),
-        out_shape=jax.ShapeDtypeStruct((2 * rank, cols), low),
-        compiler_params=pltpu.CompilerParams(vmem_limit_bytes=60 << 20),
-        name="portions",
-    )(left, grad, middle, heads, *waits)
+        name="relay",
+    )(places, *inputs, *waits)
+    return out[0], out[1:-1], out[-1]
 
 
 def head_forward(proj, gain, cos, sin):
@@ -309,8 +282,16 @@
     lse_ref[0] = top + jnp.log(total)
 
 
-def attend_back_kernel(share, proj_ref, cos_ref, sin_ref, gain_ref, bias_ref, key_ref, value_ref,
-                       lse_ref, grad_ref, out_ref, kv_grad_ref, key_t, key_sum, value_sum):
+def attend_back_kernel(share, pieces, extras, place_ref, proj_ref, cos_ref, sin_ref, gain_ref, bias_ref, key_ref, value_ref,
+                       lse_ref, grad_ref, middle_ref, raise_ref, *refs):
+    extra_refs, refs = refs[:extras], refs[extras:]
+    out_ref, up_ref, *kv_refs = refs[: 2 + pieces]
+    mid_ref, key_t, key_sum, value_sum = refs[2 + pieces :]
+
+    @pl.when(pl.program_id(0) == 0)
+    def _():
+        mid_ref[...] = jnp.zeros_like(mid_ref)
+
     @pl.when(lax.rem(pl.program_id(0), share) == 0)
     def _():
         key_t[...] = key_ref[...].T
@@ -332,12 +313,23 @@
     scaled = rotated * cos + pltpu.roll(rotated * sin, HEAD_WIDTH // 2, 1)
     scaled = scaled * gain
     slope = jnp.mean(scaled * proj, axis=-1, keepdims=True)
-    out_ref[...] = (inv * scaled - proj * (inv * inv * inv * slope)).astype(low)
+    proj_grad = (inv * scaled - proj * (inv * inv * inv * slope)).astype(low)
+    out_ref[...] = proj_grad
+    up_ref[...] = contract_leading(middle_ref[...], proj_grad).astype(low)
+    mid_ref[...] += contract_last(proj_grad, raise_ref[...])
 
     @pl.when(lax.rem(pl.program_id(0), share) == share - 1)
     def _():
-        kv_grad_ref[:, :HEAD_WIDTH] = (key_sum[...] * score_scale).astype(low)
-        kv_grad_ref[:, HEAD_WIDTH:] = value_sum[...].astype(low)
+        for k, ref in enumerate(kv_refs):
+            rows = proj_ref.shape[0]
+            span = pl.ds(pl.multiple_of(place_ref[k] * rows, rows), rows)
+            ref[:rows, :HEAD_WIDTH] = (key_sum[span, :] * score_scale).astype(low)
+            ref[:rows, HEAD_WIDTH:] = value_sum[span, :].astype(low)
+            if extras:
+                common, mine = extra_refs
+                more = mine.shape[0] // pieces
+                ref[rows : rows + common.shape[0], :] = common[...]
+                ref[rows + common.shape[0] :, :] = mine[pl.ds(pl.multiple_of(place_ref[k] * more, more), more), :]
 
 
 def head_specs(tokens, length, first, share, kv_total):
@@ -390,47 +382,71 @@
     )(proj, cos, sin, gain, bias, keys_values, keys_values)
 
 
-def attend_back(first, heads, proj, cos, sin, gain, bias, keys_values, lse, grad, kv_span, filled, waits):
+def attend_back(first, heads, kv_span, proj, cos, sin, gain, bias, keys_values, lse, grad, middle, raised,
+                extras, filled, waits):
     tokens, length = proj.shape[0], keys_values.shape[0]
+    rank = middle.shape[1]
     total = proj.shape[1] // HEAD_WIDTH
     kv_total = keys_values.shape[1] // (2 * HEAD_WIDTH)
-    share = total // kv_total
-    kv_first, kv_end = kv_span
-
-    def head(h):
+    share, count = total // kv_total, length // tokens
+    places = jnp.stack([origin(0)] + [origin(count - k) for k in range(1, count)])
+    rows = tokens + (extras[0].shape[0] + extras[1].shape[0] // count if extras else 0)
+
+    def with_place(spec):
+        return pl.BlockSpec(spec.block_shape, lambda h, p: spec.index_map(h))
+
+    def head(h, p):
         return (0, first + h)
 
+    def kv_head(h, p):
+        return (0, (first + h) // share - kv_span[0])
+
     return pl.pallas_call(
-        held(functools.partial(attend_back_kernel, share), 9, len(filled) + len(waits)),
-        grid=(heads,),
-        in_specs=head_specs(tokens, length, first, share, kv_total)
-        + [
-            pl.BlockSpec((1, 1, tokens), lambda h: (first + h, 0, 0)),
-            pl.BlockSpec((tokens, HEAD_WIDTH), head),
-            *[anywhere] * (len(filled) + len(waits)),
-        ],
-        out_specs=[
-            pl.BlockSpec((tokens, HEAD_WIDTH), head),
-            pl.BlockSpec((length, 2 * HEAD_WIDTH), lambda h: (0, (first + h) // share - kv_first)),
-        ],
-        scratch_shapes=[
-            pltpu.VMEM((HEAD_WIDTH, length), low),
-            pltpu.VMEM((length, HEAD_WIDTH), wide),
-            pltpu.VMEM((length, HEAD_WIDTH), wide),
-        ],
+        held(
+            functools.partial(attend_back_kernel, share, count, len(extras)),
+            12 + len(extras),
+            len(filled) + len(waits),
+        ),
+        grid_spec=pltpu.PrefetchScalarGridSpec(
+            num_scalar_prefetch=1,
+            grid=(heads,),
+            in_specs=[with_place(spec) for spec in head_specs(tokens, length, first, share, kv_total)]
+            + [
+                pl.BlockSpec((1, 1, tokens), lambda h, p: (first + h, 0, 0)),
+                pl.BlockSpec((tokens, HEAD_WIDTH), head),
+                pl.BlockSpec((tokens, rank), lambda h, p: (0, 0)),
+                pl.BlockSpec((rank, HEAD_WIDTH), head),
+                *[pl.BlockSpec((a.shape[0], 2 * HEAD_WIDTH), kv_head) for a in extras],
+                *[anywhere] * (len(filled) + len(waits)),
+            ],
+            out_specs=[
+                pl.BlockSpec((tokens, HEAD_WIDTH), head),
+                pl.BlockSpec((rank, HEAD_WIDTH), head),
+                *[pl.BlockSpec((rows, 2 * HEAD_WIDTH), kv_head)] * count,
+                pl.BlockSpec((tokens, rank), lambda h, p: (0, 0)),
+            ],
+            scratch_shapes=[
+                pltpu.VMEM((HEAD_WIDTH, length), low),
+                pltpu.VMEM((length, HEAD_WIDTH), wide),
+                pltpu.VMEM((length, HEAD_WIDTH), wide),
+            ],
+        ),
         out_shape=[
             jax.ShapeDtypeStruct(proj.shape, low),
-            jax.ShapeDtypeStruct((length, (kv_end - kv_first) * 2 * HEAD_WIDTH), low),
+            jax.ShapeDtypeStruct((rank, proj.shape[1]), low),
+            *[jax.ShapeDtypeStruct((rows, (kv_span[1] - kv_span[0]) * 2 * HEAD_WIDTH), low)] * count,
+            jax.ShapeDtypeStruct((tokens, rank), wide),
         ],
-        input_output_aliases={9 + i: i for i in range(len(filled))},
+        input_output_aliases={12 + len(extras) + i: i for i in range(len(filled))},
         compiler_params=pltpu.CompilerParams(vmem_limit_bytes=60 << 20),
         cost_estimate=pl.CostEstimate(flops=0, bytes_accessed=0, transcendentals=0),
         name="attend_back",
-    )(proj, cos, sin, gain, bias, keys_values, keys_values, lse, grad, *filled, *waits)
+    )(places, proj, cos, sin, gain, bias, keys_values, keys_values, lse, grad, middle, raised,
+      *extras, *filled, *waits)
 
 
 def experts_kernel(place_ref, normed_ref, back_ref, weight_ref, gate_ref, up_ref, down_ref,
-                   post_ref, out_ref, out_sum):
+                   post_ref, out_ref, slice_ref, out_sum):
     e = pl.program_id(0)
     width = normed_ref.shape[1]
 
@@ -461,10 +477,12 @@
     @pl.when(e == pl.num_programs(0) - 1)
     def _():
         out_ref[...] = out_sum[...].astype(low)
-
-
-def experts(chunk, first_expert, tokens, normed, back, weights, gate_up, down, mixture, waits):
-    filled = () if mixture is None else (mixture,)
+        cols = slice_ref.shape[1]
+        start = pl.multiple_of(place_ref[2] * cols, cols)
+        slice_ref[...] = out_sum[:, pl.ds(start, cols)].astype(low)
+
+
+def experts(place, tokens, slice_cols, normed, back, weights, gate_up, down, filled, waits):
     waits = (*filled, *waits)
     width = normed.shape[1]
     count, inner_width = gate_up.shape[0], gate_up.shape[2] // 2
@@ -485,14 +503,16 @@
             out_specs=[
                 pl.BlockSpec((tokens, width + HEAD_WIDTH), lambda e, p: (0, 0)),
                 pl.BlockSpec((tokens, width), lambda e, p: (p[0], 0)),
+                pl.BlockSpec((tokens, slice_cols), lambda e, p: (p[0], 0)),
             ],
             scratch_shapes=[pltpu.VMEM((tokens, width), wide)],
         ),
         out_shape=[
             jax.ShapeDtypeStruct((tokens, width + HEAD_WIDTH), wide),
             jax.ShapeDtypeStruct(normed.shape, low),
+            jax.ShapeDtypeStruct((normed.shape[0], slice_cols), low),
         ],
-        input_output_aliases={7: 1} if filled else {},
+        input_output_aliases={7 + i: 1 + i for i in range(len(filled))},
         compiler_params=pltpu.CompilerParams(vmem_limit_bytes=60 << 20),
         cost_estimate=pl.CostEstimate(
             flops=10 * tokens * width * count * inner_width,
@@ -500,11 +520,11 @@
             transcendentals=tokens * count * inner_width,
         ),
         name="experts",
-    )(jnp.stack([chunk, first_expert]), normed, back, weights, gate_up, gate_up, down, *waits)
+    )(jnp.stack(place), normed, back, weights, gate_up, gate_up, down, *waits)
 
 
 def settle_kernel(arrived_ref, post_ref, probs_ref, router_ref, resid_ref, gain_ref, cot_ref, up_ref,
-                  grad_ref, branch_ref, middle_ref):
+                  branch_ref, middle_ref):
     width = resid_ref.shape[1]
     gate_grad = arrived_ref[:, width:].astype(wide) + post_ref[:, width:]
     probs = probs_ref[...]
@@ -515,7 +535,6 @@
     inv = lax.rsqrt(jnp.mean(resid * resid, axis=1, keepdims=True) + norm_eps)
     slope = jnp.mean(grad * resid, axis=1, keepdims=True)
     grad = cot_ref[...].astype(wide) + inv * grad - resid * (inv * inv * inv * slope)
-    grad_ref[...] = grad
     branch = grad.astype(low)
     branch_ref[...] = branch
     middle_ref[...] = contract_last(branch, up_ref[...]).astype(low)
@@ -546,9 +565,8 @@
             rows(width),
             whole(rank, width),
         ],
-        out_specs=[rows(width), rows(width), rows(rank)],
+        out_specs=[rows(width), rows(rank)],
         out_shape=[
-            jax.ShapeDtypeStruct((tokens, width), wide),
             jax.ShapeDtypeStruct((tokens, width), low),
             jax.ShapeDtypeStruct((tokens, rank), low),
         ],
@@ -563,6 +581,8 @@
     state, norm_ref, outs = refs[:size], refs[size], refs[size + 1 : 2 * size + 1]
     head_sum, last_sum, factor_ref = refs[2 * size + 1 :]
     now = pl.program_id(0)
+    across_rows = rank * last_ref.shape[2] // head_ref.shape[2]
+    in_start = head_ref.shape[1] - across_rows
 
     @pl.when(now == 0)
     def _():
@@ -578,28 +598,32 @@
         lax.fori_loop(0, head_ref.shape[0], tree, 0)
 
         def square(s, carry):
-            head, last = head_sum[s, 2 * rank :], last_sum[s]
-            head = jnp.sum(head * head, axis=0, keepdims=True)
-            last = jnp.sum(last * last, axis=0, keepdims=True)
-            return carry + jnp.sum(head, axis=1, keepdims=True) + jnp.sum(last, axis=1, keepdims=True)
+            for part in (head_sum[s, :across_rows], head_sum[s, in_start:], last_sum[s]):
+                part = jnp.sum(part * part, axis=0, keepdims=True)
+                carry = carry + jnp.sum(part, axis=1, keepdims=True)
+            return carry
 
         norm = jnp.sqrt(lax.fori_loop(0, head_sum.shape[0], square, square_ref[...]))
         norm_ref[...] = norm
         factor_ref[...] = jnp.minimum(1.0, clip_limit / (norm + 1e-06))
 
-    chunk = pl.multiple_of(2 * rank * (1 + place_ref[0]), 2 * rank)
+    chunk = pl.multiple_of(rank * place_ref[0], rank)
     inside = pl.ds(pl.multiple_of(place_ref[1], HEAD_WIDTH), row_width)
     across = pl.ds(pl.multiple_of(place_ref[2], HEAD_WIDTH), row_width)
-    up = head_sum[now, pl.ds(chunk, rank), inside]
-    query_in = head_sum[now, pl.ds(chunk + rank, rank), inside]
-    kv_in = last_sum[now, : 2 * rank, across]
+
+    def side_by_side(start, end):
+        return jnp.concatenate([head_sum[now, i : i + rank] for i in range(start, end, rank)], axis=1)
+
+    down_end = (across_rows + in_start) // 2
     kv = last_sum[now, 2 * rank :, :]
     kv_cols = state[-1].shape[2]
     grads = (
-        head_sum[now, :rank, :],
-        head_sum[now, rank : 2 * rank, :],
-        up,
-        jnp.concatenate([query_in, kv_in], axis=0),
+        side_by_side(down_end, in_start),
+        side_by_side(across_rows, down_end),
+        head_sum[now, pl.ds(chunk, rank), inside],
+        jnp.concatenate(
+            [head_sum[now, pl.ds(in_start + chunk, rank), inside], last_sum[now, : 2 * rank, across]], axis=0
+        ),
         jnp.concatenate([kv[:, i : i + kv_cols] for i in range(0, kv.shape[1], kv_cols)], axis=0),
     )
     factor = factor_ref[...]
@@ -794,12 +818,12 @@
         ring_gather(jnp.concatenate([key_rot.astype(low), value_proj.astype(low)], axis=1)), 0
     )
     query_gain = query_norm_gain[None, :]
-    proj = project(normalized, query_weight, middle[:, :rank], query_raise, False, wide)
+    proj = project(normalized, query_weight, (middle[:, :rank], query_raise), False, wide)
     heads, totals = attend(proj, cos, sin, query_gain, bias, keys_values)
     inner_back = contract_last(cot_full, first[:local_inner])
     middle_output = contract_last(heads, down_output).astype(low)
     resid = hidden_input + project(
-        heads, out_weight, middle_output, up_output, False, wide, (inner_back,)
+        heads, out_weight, (middle_output, up_output), False, wide, (inner_back,)
     )
 
     resid_full = in_order(ring_gather(resid.astype(low)), 0)
@@ -816,39 +840,49 @@
         ((0, 0), (0, HEAD_WIDTH - expert_total)),
     )
     router_rows = jnp.pad(router, ((0, HEAD_WIDTH - expert_total), (0, 0)))
-    local_in = down_input[rank:]
-    mixture, arrived, sent = None, None, ()
+    filled, arrived, sent = (), None, ()
     for k in range(col_count):
-        post, mixture = experts(
-            origin(k + 1),
-            col_index * local_experts,
+        post, *filled = experts(
+            (origin(k + 1), col_index * local_experts, origin(1)),
             tokens,
+            col_width,
             normed_post,
             inner_back,
             local_probs,
             gate_up_weight,
             first,
-            mixture,
-            sent if k < col_count - 1 else (*sent, own_probs, router_rows, cot_own, local_in),
+            filled,
+            sent if k < col_count - 1 else (*sent, own_probs, router_rows, cot_own),
         )
         if k < col_count - 1:
             sent = ((post if k == 0 else arrived.astype(wide) + post).astype(low),)
             arrived = shift(sent[0], 1)
 
+    mixture, mixture_sent = filled
+
     def mixture_hop(k, arrived, dtype, *waits):
         return hop(origin(k), arrived, (mixture,), (length, col_width), dtype, waits)
 
-    resid_grad, branch_grad, mid_out_grad = settle(
+    branch_grad, mid_out_grad = settle(
         arrived, post, own_probs, router_rows, resid, expert_norm_gain[None, :], cot_own, up_output
     )
-    mixture_sent = mixture_hop(1, None, low, arrived)
-    heads_grad = project(branch_grad, out_weight, mid_out_grad, down_output, True, low)
+    heads_grad = project(branch_grad, out_weight, (mid_out_grad, down_output), True, low)
+
+    def folded(part, cols):
+        return jnp.concatenate([part[:, i : i + cols] for i in range(0, part.shape[1], cols)])
+
+    query_middle = middle[:, :rank]
+    half_cols = kv_cols
+    down_portion = folded(contract_leading(mid_out_grad, heads).astype(low), half_cols)
+    up_portion = folded(contract_leading(middle_output, branch_grad).astype(low), half_cols)
     head_count = proj.shape[1] // HEAD_WIDTH
-
-    def heads_back(first, count, kv_span, filled, *waits):
+    quarter, half_kv = head_count // 4, kv_total // 2
+
+    def heads_back(first, count, kv_first, extras, filled, waits):
         return attend_back(
-            first * head_count // 4,
-            count * head_count // 4,
+            first * quarter,
+            count * quarter,
+            (kv_first, kv_first + half_kv),
             proj,
             cos,
             sin,
@@ -857,26 +891,33 @@
             keys_values,
             totals,
             heads_grad,
-            kv_span,
+            query_middle,
+            query_raise,
+            extras,
             filled,
             waits,
         )
 
-    filled = heads_back(0, 1, (0, kv_total // 2), ())
+    def sent_on(pieces):
+        return [pieces[0]] + [shift(pieces[k], k) for k in range(1, col_count)]
+
+    extras = (up_portion, down_portion)
+    *filled, mid_a = heads_back(0, 1, 0, extras, (), ())
     mixture_sent = mixture_hop(2, shift(mixture_sent, 1), low, filled[0])
-    query_grad, kv_grad = heads_back(1, 1, (0, kv_total // 2), filled, mixture_sent)
-    pieces = cut_and_send(kv_grad, tokens, ())
     mixture_arrived = shift(mixture_sent, 1)
-    query_grad, kv_grad = heads_back(2, 2, (kv_total // 2, kv_total), (query_grad,))
-    kv_own = [summed(pieces, (query_grad, mixture_arrived)), None]
-    pieces = cut_and_send(kv_grad, tokens, (kv_own[0],))
-    mid_query_grad = narrow(query_grad, query_raise, (pieces[0],))
-    head_part = portions(middle[:, :rank], query_grad, mid_out_grad, heads, (pieces[0],))
-    normed_query_grad = project(
-        query_grad, query_weight, mid_query_grad, down_input[:rank], True, wide, (head_part,)
-    )
-    kv_own[1] = tree_sum(pieces)
-    kv_own = jnp.concatenate([half.astype(wide) for half in kv_own], axis=1)
+    query_grad, query_portion, *pieces, mid_b = heads_back(1, 1, 0, extras, filled, (mixture_sent,))
+    pieces = sent_on(pieces)
+    query_grad, query_portion, *leaving, mid_c = heads_back(
+        2, 2, half_kv, (), (query_grad, query_portion), ()
+    )
+    first_sum, leaving, mid_query_grad = relay(
+        pieces, leaving, (mid_a, mid_b, mid_c), query_portion, normalized, (mixture_arrived,)
+    )
+    pieces = sent_on(leaving)
+    normed_query_grad = project(query_grad, query_weight, (), True, wide, (first_sum,))
+    second_sum = summed(pieces, (normed_query_grad,))
+    kv_own = jnp.concatenate([first_sum[:tokens], second_sum[:tokens]], axis=1).astype(wide)
+    head_sum = jnp.concatenate([first_sum[tokens:], second_sum[tokens:]])
     kv_split = [kv_own[:, i : i + HEAD_WIDTH] for i in range(0, 2 * kv_cols, HEAD_WIDTH)]
     key_grad = keys_back(jnp.concatenate(kv_split[0::2], axis=1))[0].astype(low)
     value_grad = jnp.concatenate(kv_split[1::2], axis=1).astype(low)
@@ -889,17 +930,6 @@
         axis=1,
     ).astype(low)
 
-    def folded(part, cols):
-        return jnp.concatenate([part[:, i : i + cols] for i in range(0, part.shape[1], cols)])
-
-    early_part = jnp.concatenate(
-        [contract_leading(middle_output, branch_grad), contract_leading(mid_query_grad, normalized)]
-    ).astype(low)
-    early_part = folded(early_part, group_cols)
-    def head_piece(c):
-        piece = lax.dynamic_slice_in_dim(head_part, c * group_cols, group_cols, 1)
-        return jnp.concatenate([piece, early_part])
-
     kv_portion = jnp.concatenate(
         [
             contract_leading(middle[:, rank : 2 * rank], key_grad),
@@ -911,33 +941,43 @@
         [kv_portion[i : i + kv_rows] for i in range(0, 2 * rank, kv_rows)], axis=1
     )
     last_part = jnp.concatenate([contract_leading(mid_kv_grad, normalized), kv_portion]).astype(low)
-    last_pieces = [last_part] + [shift(last_part, k) for k in range(1, col_count)]
-    last_trees = lax.all_gather(tree_sum(last_pieces).astype(low), "row", axis=0)
-    head_trees = lax.all_gather(summed(exchange(head_piece), ()), "row", axis=0)
-    slot_hot = (slots[None, :] == jnp.arange(adapters, dtype=jnp.int32)[:, None]).astype(low)
+    last_sum = tree_sum([last_part] + [shift(last_part, k) for k in range(1, col_count)]).astype(low)
+    last_trees = lax.all_gather(last_sum, "row", axis=0)
+    head_trees = lax.all_gather(head_sum, "row", axis=0)
+    wait = nought(last_sum)
+    slot_hot = slots[None, :] == wait + jnp.arange(adapters, dtype=jnp.int32)[:, None]
+    slot_hot = slot_hot.astype(low)
+    across_rows = rank * width // half_cols
     head_square = jnp.einsum(
-        "st,tij->sij", slot_hot, head_trees[:, : 2 * rank], preferred_element_type=wide
+        "st,tij->sij",
+        slot_hot,
+        head_trees[:, across_rows : head_sum.shape[0] - across_rows],
+        preferred_element_type=wide,
     )
     head_square = jnp.full((1, HEAD_WIDTH), jnp.sum(head_square * head_square))
-    head_square = tree_sum([head_square] + [shift(head_square, k) for k in range(1, col_count)])[:, :1]
-    wait = nought(head_square)
+    step = 1
+    while step < col_count:
+        pairs = [(i, i ^ step) for i in range(col_count)]
+        head_square = head_square + lax.ppermute(head_square, "col", pairs)
+        step *= 2
+    head_square = head_square[:, :1]
 
     normed_in_grad = (
         normed_query_grad
         + product(kv_proj_grad, key_value_weight)
-        + product(mid_kv_grad, local_in)
-    )
-    input_grad_own = (resid_grad + norm_in_back(normed_in_grad)[0]).astype(low)
+        + product(jnp.concatenate([mid_query_grad, mid_kv_grad], axis=1), down_input)
+    )
+    input_grad_own = (branch_grad.astype(wide) + norm_in_back(normed_in_grad)[0]).astype(low)
     pieces = exchange(
         lambda c: lax.dynamic_slice_in_dim(input_grad_own, c * col_width + wait, col_width, 1)
     )
     input_grad = in_order(pieces, 0).astype(wide)
-    for k in range(2, col_count):
-        last = k == col_count - 1
-        waits = (last_part,) if k == 2 else ()
-        mixture_sent = mixture_hop(k + 1, mixture_arrived, wide if last else low, *waits)
-        mixture_arrived = None if last else shift(mixture_sent, 1)
-    moe_slice = mixture_sent
+    waits = (head_square, *pieces[1:])
+    for k in range(2, col_count - 1):
+        mixture_sent = mixture_hop(k + 1, mixture_arrived, low, *waits)
+        mixture_arrived, waits = shift(mixture_sent, 1), ()
+    own_slice = lax.dynamic_slice_in_dim(mixture, col_index * col_width, col_width, 1)
+    moe_slice = mixture_arrived.astype(wide) + own_slice.astype(wide)
     resid_slice = lax.dynamic_slice_in_dim(resid_full, col_index * col_width, col_width, 1)
     layer_output = resid_slice.astype(wide) + moe_slice
 
@@ -948,7 +988,7 @@
         return array.reshape(adapters, 2 * rank, kv_cols)
 
     row_start = row_index * row_width
-    place = jnp.stack([row_start // group_cols, lax.rem(row_start, group_cols), row_start])
+    place = jnp.stack([row_start // half_cols, lax.rem(row_start, half_cols), row_start])
     grad_norm, following = update(
         slots,
         place,

time: 808 us -> 801 us (level)
  Pallas kernels: 289 us -> 279 us
    ppermute x45 -> x39, waiting for transfers between devices: 253 us -> 230 us  [shift(): return lax.ppermute(values, 'col', pairs)]
    ppermute x0 -> x2, waiting for transfers between devices: none -> 19.8 us  [shards(): head_square = head_square + lax.ppermute(head_square, 'col', pairs)]
    pallas_call x11 -> x8, Pallas kernels: 117 us -> 114 us  [the longest x3 60.2 us: attend_back(): pl.pallas_call(held(functools.partial(attend_back_kernel, share, count, l...]
    dynamic_update_slice x28 -> x29, local copies, waits for them, and re-layouts: 22.5 us -> 24 us  [in_order(): lax.dynamic_update_slice_in_dim(out, part, origin(k) * size + wait, axis)]
    ppermute x45 -> x39, starting transfers between devices: 60 us -> 58.6 us  [shift(): return lax.ppermute(values, 'col', pairs)]
    unnamed x175 -> x182, local copies, waits for them, and re-layouts: 17.5 us -> 17.1 us
  transfers between devices with their start and end apart: 51 -> 47, of which waited for: 24 -> 25; matrix products, arithmetic and copies ran while one was open for 14% -> 14% of each run, Pallas kernels for 31% -> 31%
where the time goes in v3:
time: 801 us; the launch traced here: 792 us
  waiting for transfers between devices  289 us (36%)
  Pallas kernels  279 us (35%)
  local copies, waits for them, and re-layouts  68.3 us (9%)
  starting transfers between devices  61.3 us (8%)
  matrix products  39.4 us (5%)
  other arithmetic  37.4 us (5%)
  between operations  18 us (2%)
    ppermute x39, waiting for transfers between devices, shift(): return lax.ppermute(values, 'col', pairs)  230 us
    pallas_call x4, Pallas kernels, experts(): pl.pallas_call(held(experts_kernel, 7, len(waits)), grid_spec=pltpu.Prefe...  99.9 us
    pallas_call x3, Pallas kernels, attend_back(): pl.pallas_call(held(functools.partial(attend_back_kernel, share, count, l...  60.2 us
    ppermute x39, starting transfers between devices, shift(): return lax.ppermute(values, 'col', pairs)  58.6 us
    pallas_call x4, Pallas kernels, project(): pl.pallas_call(held(functools.partial(project_kernel, turned), 2 + len(th...  49.5 us
    pallas_call x1, Pallas kernels, attend(): pl.pallas_call(functools.partial(attend_kernel, share), grid=(heads,), in...  36.4 us
    all_gather x4, waiting for transfers between devices, gather_rows(): return lax.all_gather(values, 'row', axis=axis, tiled=True)  35.7 us
    dot_general x8, matrix products, contract_last(): lax.dot_general(left, right, (((1,), (1,)), ((), ())), preferred_element_...  28.9 us
  transfers between devices with their start and end apart: 47, of which 25 were waited for; matrix products, arithmetic and copies ran while one was open for 14% of the time, Pallas kernels for 31%

profile of v3, /device:TPU:0, one launch (start us, length us, event | category | flops | bytes accessed | tf_op | source)
XLA Modules:
  0.0 791.7 jit_solution(6495219119138896237)
XLA Ops:
  18.3 14.2 %collective-permute-done.3 = bf16[256,1024]{1,0:T(8,128)(2,1)S(1)} collective-permute-done((bf16[256,1024]{1,0:T(8,128)(2,1)}, bf16[256,1024]{1,0:T(8,128)(2,1)S(1)}, u32[]{:S(2)}, u32[]{:S(2)}) %collective-permute-start.3) | collective-permute-done | bytes 524320 | tf_op jit(solution)/shard_map/ppermute | solution.py:106
  32.5 15.0 %collective-permute-done.4 = bf16[256,1024]{1,0:T(8,128)(2,1)} collective-permute-done((bf16[256,1024]{1,0:T(8,128)(2,1)S(1)}, bf16[256,1024]{1,0:T(8,128)(2,1)}, u32[]{:S(2)}, u32[]{:S(2)}) %collective-permute-start.4) | collective-permute-done | bytes 524320 | tf_op jit(solution)/shard_map/ppermute | solution.py:106
  49.0 12.8 %collective-permute-done.5 = bf16[256,1024]{1,0:T(8,128)(2,1)} collective-permute-done((bf16[256,1024]{1,0:T(8,128)(2,1)}, bf16[256,1024]{1,0:T(8,128)(2,1)}, u32[]{:S(2)}, u32[]{:S(2)}) %collective-permute-start.5) | collective-permute-done | bytes 524320 | tf_op jit(solution)/shard_map/ppermute | solution.py:106
  64.5 12.9 %collective-permute-done.12 = bf16[1024,256]{1,0:T(8,128)(2,1)S(1)} collective-permute-done((bf16[1024,256]{1,0:T(8,128)(2,1)S(1)}, bf16[1024,256]{1,0:T(8,128)(2,1)S(1)}, u32[]{:S(2)}, u32[]{:S(2)}) %collective-permute-start.12) | collective-permute-done | bytes 524320 | tf_op jit(solution)/shard_map/ppermute | solution.py:106
  77.4 12.1 %collective-permute-done.13 = bf16[1024,256]{1,0:T(8,128)(2,1)S(1)} collective-permute-done((bf16[1024,256]{1,0:T(8,128)(2,1)S(1)}, bf16[1024,256]{1,0:T(8,128)(2,1)S(1)}, u32[]{:S(2)}, u32[]{:S(2)}) %collective-permute-start.13) | collective-permute-done | bytes 524320 | tf_op jit(solution)/shard_map/ppermute | solution.py:106
  89.8 10.8 %collective-permute-done.14 = bf16[1024,256]{1,0:T(8,128)(2,1)S(1)} collective-permute-done((bf16[1024,256]{1,0:T(8,128)(2,1)S(1)}, bf16[1024,256]{1,0:T(8,128)(2,1)S(1)}, u32[]{:S(2)}, u32[]{:S(2)}) %collective-permute-start.14) | collective-permute-done | bytes 524320 | tf_op jit(solution)/shard_map/ppermute | solution.py:106
  106.9 3.8 collective-permute-start.2
  111.3 3.8 collective-permute-start.15
  125.3 22.6 %collective-permute-done.7 = bf16[32,1024]{1,0:T(8,128)(2,1)S(1)} collective-permute-done((bf16[32,1024]{1,0:T(8,128)(2,1)}, bf16[32,1024]{1,0:T(8,128)(2,1)S(1)}, u32[]{:S(2)}, u32[]{:S(2)}) %collective-permute-start.7) | collective-permute-done | bytes 65568 | tf_op jit(solution)/shard_map/ppermute | solution.py:106
  148.0 3.2 collective-permute-start.8
  159.8 19.1 %collective-permute-done.16 = bf16[1024,512]{1,0:T(8,128)(2,1)} collective-permute-done((bf16[1024,512]{1,0:T(8,128)(2,1)S(1)}, bf16[1024,512]{1,0:T(8,128)(2,1)}, u32[]{:S(2)}, u32[]{:S(2)}) %collective-permute-start.16) | collective-permute-done | bytes 1048608 | tf_op jit(solution)/shard_map/ppermute | solution.py:106
  181.4 3.6 fusion.7
  195.4 10.9 %collective-permute-done.17 = bf16[1024,512]{1,0:T(8,128)(2,1)} collective-permute-done((bf16[1024,512]{1,0:T(8,128)(2,1)}, bf16[1024,512]{1,0:T(8,128)(2,1)}, u32[]{:S(2)}, u32[]{:S(2)}) %collective-permute-start.17) | collective-permute-done | bytes 1048608 | tf_op jit(solution)/shard_map/ppermute | solution.py:106
  208.6 4.8 collective-permute-done.9
  214.8 17.0 %fusion.refs_4_.refs_2_ = f32[1024,3072]{1,0:T(8,128)} fusion(bf16[1024,2048]{1,0:T(8,128)(2,1)} %constant_dynamic-update-slice_fusion.25, bf16[4640,2048]{1,0:T(8,128)(2,1)S(1)} %copy-done), kind=kOutput, calls=%fused_computation | convolution fusion | flops 12884901888 | bytes 29360128 | tf_op jit(solution)/shard_map/dot_general | solution.py:31
  234.9 12.5 %project.4.proj_ref.refs_1_ = f32[256,4096]{1,0:T(8,128)} custom-call(bf16[256,2048]{1,0:T(8,128)(2,1)} %copy-done.6, bf16[2048,4096]{1,0:T(8,128)(2,1)} %all-gather.9.cloned.1.call-done.refs_1_, bf16[256,16]{1,0:T(8,128)(2,1)} %bitcast.110, bf16[16,4096]{1,0:T(8,128)(2,1)} %get-tuple-element.197.refs_3_.refs_11_), custom_call_target="tpu_custom_call" | custom-call | tf_op jit(solution)/shard_map/project/pallas_call | solution.py:85
  252.1 36.4 %attend.1 = (bf16[256,4096]{1,0:T(8,128)(2,1)}, f32[32,1,256]{2,1,0:T(1,128)}) custom-call(f32[256,4096]{1,0:T(8,128)} %project.4.proj_ref.refs_1_, f32[256,128]{1,0:T(8,128)} %pad_maximum_fusion.2.cos_ref.refs_2_, f32[256,128]{1,0:T(8,128)} %copy-done.12, f32[1,128]{1,0:T(1,128)} %bitcast.133, f32[1024,256]{1,0:T(8,128)} %fusion.25.bias_ref.refs_5_, ...), custom_call_target="tpu_custom_call" | custom-call | flops 12884901888 | bytes 8388608 | tf_op jit(solution)/shard_map/attend/pallas_call | solution.py:366
  291.4 17.6 %all-gather.13.cloned.1.call-done.refs_1_ = bf16[4096,2048]{1,0:T(8,128)(2,1)} async-done(((bf16[4096,256]{1,0:T(8,128)(2,1)}), bf16[4096,2048]{1,0:T(8,128)(2,1)}) %all-gather.13.cloned.1.call-update) | async-done | bytes 16777232 | tf_op jit(solution)/shard_map/all_gather | solution.py:747
  309.0 12.8 %project.5 = f32[256,2048]{1,0:T(8,128)} custom-call(bf16[256,4096]{1,0:T(8,128)(2,1)} %get-tuple-element.78.refs_0_, bf16[4096,2048]{1,0:T(8,128)(2,1)} %all-gather.13.cloned.1.call-done.refs_1_, bf16[256,16]{1,0:T(8,128)(2,1)} %convolution_convert_fusion.4.refs_2_, bf16[16,2048]{1,0:T(8,128)(2,1)} %get-tuple-element.167.refs_3_.up_ref, ...), custom_call_target="tpu_custom_call" | custom-call | tf_op jit(solution)/shard_map/project/pallas_call | solution.py:85
  328.3 25.6 %collective-permute-done.18 = bf16[256,2048]{1,0:T(8,128)(2,1)S(1)} collective-permute-done((bf16[256,2048]{1,0:T(8,128)(2,1)S(1)}, bf16[256,2048]{1,0:T(8,128)(2,1)S(1)}, u32[]{:S(2)}, u32[]{:S(2)}) %collective-permute-start.18) | collective-permute-done | bytes 1048608 | tf_op jit(solution)/shard_map/ppermute | solution.py:106
  354.8 25.4 %collective-permute-done.19 = bf16[256,2048]{1,0:T(8,128)(2,1)S(1)} collective-permute-done((bf16[256,2048]{1,0:T(8,128)(2,1)S(1)}, bf16[256,2048]{1,0:T(8,128)(2,1)S(1)}, u32[]{:S(2)}, u32[]{:S(2)}) %collective-permute-start.19) | collective-permute-done | bytes 1048608 | tf_op jit(solution)/shard_map/ppermute | solution.py:106
  387.5 18.4 %collective-permute-done.20 = bf16[256,2048]{1,0:T(8,128)(2,1)S(1)} collective-permute-done((bf16[256,2048]{1,0:T(8,128)(2,1)S(1)}, bf16[256,2048]{1,0:T(8,128)(2,1)S(1)}, u32[]{:S(2)}, u32[]{:S(2)}) %collective-permute-start.20) | collective-permute-done | bytes 1048608 | tf_op jit(solution)/shard_map/ppermute | solution.py:106
  406.9 3.1 fusion.2
  410.0 3.2 fusion.4.refs_1_
  418.0 18.1 %all-gather.15.cloned.1.call-done.refs_4_.refs_5_ = bf16[4,2048,1536]{2,1,0:T(8,128)(2,1)} async-done(((bf16[4,256,1536]{2,1,0:T(8,128)(2,1)}), bf16[4,2048,1536]{2,1,0:T(8,128)(2,1)}) %all-gather.15.cloned.1.call-update) | async-done | bytes 25165840 | tf_op jit(solution)/shard_map/all_gather | solution.py:747
  436.1 25.0 %experts.4 = (f32[256,2176]{1,0:T(8,128)}, bf16[1024,2048]{1,0:T(8,128)(2,1)}, bf16[1024,512]{1,0:T(8,128)(2,1)}) custom-call(s32[3]{0:T(128)} %get-tuple-element.234.refs_0_, bf16[1024,2048]{1,0:T(8,128)(2,1)} %copy-done.1, f32[1024,3072]{1,0:T(8,128)} %fusion.refs_4_.refs_2_, f32[1024,4]{1,0:T(8,128)} %constant_dynamic-slice_fusion.5.refs_3_, ...), custom_call_target="tpu_custom_call" | custom-call | flops 16106127360 | bytes 37748736 | tf_op jit(solution)/shard_map/experts/pallas_call | solution.py:489
  464.8 25.0 %experts.5 = (f32[256,2176]{1,0:T(8,128)}, bf16[1024,2048]{1,0:T(8,128)(2,1)}, bf16[1024,512]{1,0:T(8,128)(2,1)}) custom-call(s32[3]{0:T(128)} %get-tuple-element.233.refs_0_, bf16[1024,2048]{1,0:T(8,128)(2,1)} %copy-done.1, f32[1024,3072]{1,0:T(8,128)} %fusion.refs_4_.refs_2_, ...), custom_call_target="tpu_custom_call", output_to_operand_aliasing={{1}: (7, {}), {2}: (8, {})} | custom-call | flops 16106127360 | bytes 37748736 | tf_op jit(solution)/shard_map/experts/pallas_call | solution.py:489
  494.7 25.0 %experts.6 = (f32[256,2176]{1,0:T(8,128)}, bf16[1024,2048]{1,0:T(8,128)(2,1)}, bf16[1024,512]{1,0:T(8,128)(2,1)}) custom-call(s32[3]{0:T(128)} %add_add_fusion.6.refs_0_, bf16[1024,2048]{1,0:T(8,128)(2,1)} %copy-done.1, f32[1024,3072]{1,0:T(8,128)} %fusion.refs_4_.refs_2_, ...), custom_call_target="tpu_custom_call", output_to_operand_aliasing={{1}: (7, {}), {2}: (8, {})} | custom-call | flops 16106127360 | bytes 37748736 | tf_op jit(solution)/shard_map/experts/pallas_call | solution.py:489
  524.3 25.0 %experts.7 = (f32[256,2176]{1,0:T(8,128)}, bf16[1024,2048]{1,0:T(8,128)(2,1)}, bf16[1024,512]{1,0:T(8,128)(2,1)}) custom-call(s32[3]{0:T(128)} %add_add_fusion.5.refs_0_, bf16[1024,2048]{1,0:T(8,128)(2,1)} %copy-done.1, f32[1024,3072]{1,0:T(8,128)} %fusion.refs_4_.refs_2_, ...), custom_call_target="tpu_custom_call", output_to_operand_aliasing={{1}: (7, {}), {2}: (8, {})} | custom-call | flops 16106127360 | bytes 37748736 | tf_op jit(solution)/shard_map/experts/pallas_call | solution.py:489
  551.4 6.2 settle.1
  559.3 12.0 %project.6.refs_9_ = bf16[256,4096]{1,0:T(8,128)(2,1)} custom-call(bf16[256,2048]{1,0:T(8,128)(2,1)} %get-tuple-element.92.refs_0_, bf16[4096,2048]{1,0:T(8,128)(2,1)} %all-gather.13.cloned.1.call-done.refs_1_, bf16[256,16]{1,0:T(8,128)(2,1)} %get-tuple-element.93.refs_2_, bf16[16,4096]{1,0:T(8,128)(2,1)} %get-tuple-element.196.refs_3_), custom_call_target="tpu_custom_call" | custom-call | tf_op jit(solution)/shard_map/project/pallas_call | solution.py:85
  572.6 15.9 %attend_back.3 = (bf16[256,4096]{1,0:T(8,128)(2,1)}, bf16[16,4096]{1,0:T(8,128)(2,1)}, bf16[352,512]{1,0:T(8,128)(2,1)}, bf16[352,512]{1,0:T(8,128)(2,1)}, bf16[...) custom-call(s32[4]{0:T(128)} %pad_add_fusion.refs_0_, f32[256,4096]{1,0:T(8,128)} %project.4.proj_ref.refs_1_, ...), custom_call_target="tpu_custom_call" | custom-call | tf_op jit(solution)/shard_map/attend_back/pallas_call | solution.py:404
  588.5 3.7 hop.2.refs_20_
  592.6 15.9 %attend_back.4 = (bf16[256,4096]{1,0:T(8,128)(2,1)}, bf16[16,4096]{1,0:T(8,128)(2,1)}, bf16[352,512]{1,0:T(8,128)(2,1)}, bf16[352,512]{1,0:T(8,128)(2,1)}, bf16[...) custom-call(s32[4]{0:T(128)} %pad_add_fusion.refs_0_, ...), custom_call_target="tpu_custom_call", output_to_operand_aliasing={{0}: (14, {}), {1}: (15, {}), {2}: (16, {}), {3}: (17, {}),... | custom-call | tf_op jit(solution)/shard_map/attend_back/pallas_call | solution.py:404
  614.3 28.4 %attend_back.5 = (bf16[256,4096]{1,0:T(8,128)(2,1)}, bf16[16,4096]{1,0:T(8,128)(2,1)}, bf16[256,512]{1,0:T(8,128)(2,1)}, bf16[256,512]{1,0:T(8,128)(2,1)}, bf16[...) custom-call(s32[4]{0:T(128)} %pad_add_fusion.refs_0_, ...), custom_call_target="tpu_custom_call", output_to_operand_aliasing={{0}: (12, {}), {1}: (13, {})} | custom-call | tf_op jit(solution)/shard_map/attend_back/pallas_call | solution.py:404
  644.1 4.3 relay.1
  648.4 5.3 collective-permute-start.29
  660.0 12.2 %project.7.refs_4_ = f32[256,2048]{1,0:T(8,128)} custom-call(bf16[256,4096]{1,0:T(8,128)(2,1)} %get-tuple-element.119.refs_0_, bf16[2048,4096]{1,0:T(8,128)(2,1)} %all-gather.9.cloned.1.call-done.refs_1_, bf16[352,512]{1,0:T(8,128)(2,1)} %get-tuple-element.114.refs_2_), custom_call_target="tpu_custom_call" | custom-call | tf_op jit(solution)/shard_map/project/pallas_call | solution.py:85
  672.2 4.5 collective-permute-done.30.refs_2_
  686.3 8.1 %collective-permute-start.33 = (bf16[40,2048]{1,0:T(8,128)(2,1)S(1)}, bf16[40,2048]{1,0:T(8,128)(2,1)S(1)}, u32[]{:S(2)}, u32[]{:S(2)}) collective-permute-start(bf16[40,2048]{1,0:T(8,128)(2,1)S(1)} %maximum_maximum_fusion), channel_id=1, source_target_pairs={{0,1},{1,2},{2,3},{3,0},{4,5},{5,6},{6,7},{7,4},{8,9},{9,10},{10,1... | collective-permute-start | bytes 491528 | tf_op jit(solution)/shard_map/ppermute | solution.py:106
  694.4 3.3 collective-permute-start.32
  699.1 5.0 fusion.23
  704.2 3.9 collective-permute-done.32
  727.6 19.8 %collective-permute-done.36 = f32[1,128]{1,0:T(1,128)S(1)} collective-permute-done((f32[1,128]{1,0:T(1,128)S(1)}, f32[1,128]{1,0:T(1,128)S(1)}, u32[]{:S(2)}, u32[]{:S(2)}) %collective-permute-start.36) | collective-permute-done | bytes 544 | tf_op jit(solution)/shard_map/ppermute | solution.py:961
  749.5 4.3 hop.3
  759.6 12.0 %update.1 = (f32[1,1]{1,0:T(1,128)}, f32[8,16,1024]{2,1,0:T(8,128)}, f32[8,16,1024]{2,1,0:T(8,128)}, f32[8,16,1024]{2,1,0:T(8,128)}, f32[8,16,1024]{2,1,0:T(8,12...) custom-call(s32[8]{0:T(128)} %copy-done.81, ...), custom_call_target="tpu_custom_call" | custom-call | tf_op jit(solution)/shard_map/update/pallas_call | solution.py:647
  771.7 8.8 %collective-permute-done.40 = bf16[1024,512]{1,0:T(8,128)(2,1)S(1)} collective-permute-done((bf16[1024,512]{1,0:T(8,128)(2,1)}, bf16[1024,512]{1,0:T(8,128)(2,1)S(1)}, u32[]{:S(2)}, u32[]{:S(2)}) %collective-permute-start.40) | collective-permute-done | bytes 1048608 | tf_op jit(solution)/shard_map/ppermute | solution.py:106
  780.5 4.2 convert_add_fusion.2
  (403 shorter events, 156.4 us)
Async XLA Ops:
  7.2 172.8 %all-gather.11.cloned.1.call-start = ((), (), s32[]{:S(2)}) async-start(), calls=%async_computation.1 | async-start | bytes 21381120 | tf_op jit(solution)/shard_map/all_gather | solution.py:747
  15.2 219.7 %all-gather.9.cloned.1.call-start = ((), (), s32[]{:S(2)}) async-start(), calls=%async_computation | async-start | bytes 18874368 | tf_op jit(solution)/shard_map/all_gather | solution.py:747
  15.2 17.2 %collective-permute-start.3 = (bf16[256,1024]{1,0:T(8,128)(2,1)}, bf16[256,1024]{1,0:T(8,128)(2,1)S(1)}, u32[]{:S(2)}, u32[]{:S(2)}) collective-permute-start(bf16[256,1024]{1,0:T(8,128)(2,1)} %param.38), channel_id=1, source_target_pairs={{0,1},{1,2},{2,3},{3,0},{4,5},{5,6},{6,7},{7,4},{8,9},{9,10},{10,1... | collective-permute-start | bytes 1572872 | tf_op jit(solution)/shard_map/ppermute | solution.py:106
  32.5 15.0 %collective-permute-start.4 = (bf16[256,1024]{1,0:T(8,128)(2,1)S(1)}, bf16[256,1024]{1,0:T(8,128)(2,1)}, u32[]{:S(2)}, u32[]{:S(2)}) collective-permute-start(bf16[256,1024]{1,0:T(8,128)(2,1)S(1)} %collective-permute-done.3), channel_id=1, source_target_pairs={{0,1},{1,2},{2,3},{3,0},{4,5},{5,6},{6,7},{7,4},{8,9},{9,10},{10,1... | collective-permute-start | bytes 1572872 | tf_op jit(solution)/shard_map/ppermute | solution.py:106
  47.5 14.3 %collective-permute-start.5 = (bf16[256,1024]{1,0:T(8,128)(2,1)}, bf16[256,1024]{1,0:T(8,128)(2,1)}, u32[]{:S(2)}, u32[]{:S(2)}) collective-permute-start(bf16[256,1024]{1,0:T(8,128)(2,1)} %collective-permute-done.4), channel_id=1, source_target_pairs={{0,1},{1,2},{2,3},{3,0},{4,5},{5,6},{6,7},{7,4},{8,9},{9,10},{10,1... | collective-permute-start | bytes 1572872 | tf_op jit(solution)/shard_map/ppermute | solution.py:106
  64.4 244.6 %all-gather.13.cloned.1.call-start = ((), (), s32[]{:S(2)}) async-start(), calls=%async_computation.2 | async-start | bytes 18874368 | tf_op jit(solution)/shard_map/all_gather | solution.py:747
  64.4 13.0 %collective-permute-start.12 = (bf16[1024,256]{1,0:T(8,128)(2,1)S(1)}, bf16[1024,256]{1,0:T(8,128)(2,1)S(1)}, u32[]{:S(2)}, u32[]{:S(2)}) collective-permute-start(bf16[1024,256]{1,0:T(8,128)(2,1)S(1)} %copy-done.40), channel_id=1, source_target_pairs={{0,1},{1,2},{2,3},{3,0},{4,5},{5,6},{6,7},{7,4},{8,9},{9,10},{10,1... | collective-permute-start | bytes 1572872 | tf_op jit(solution)/shard_map/ppermute | solution.py:106
  77.4 12.1 %collective-permute-start.13 = (bf16[1024,256]{1,0:T(8,128)(2,1)S(1)}, bf16[1024,256]{1,0:T(8,128)(2,1)S(1)}, u32[]{:S(2)}, u32[]{:S(2)}) collective-permute-start(bf16[1024,256]{1,0:T(8,128)(2,1)S(1)} %collective-permute-done.12), channel_id=1, source_target_pairs={{0,1},{1,2},{2,3},{3,0},{4,5},{5,6},{6,7},{7,4},{8,9},{9,10},{10,1... | collective-permute-start | bytes 1572872 | tf_op jit(solution)/shard_map/ppermute | solution.py:106
  89.5 11.1 %collective-permute-start.14 = (bf16[1024,256]{1,0:T(8,128)(2,1)S(1)}, bf16[1024,256]{1,0:T(8,128)(2,1)S(1)}, u32[]{:S(2)}, u32[]{:S(2)}) collective-permute-start(bf16[1024,256]{1,0:T(8,128)(2,1)S(1)} %collective-permute-done.13), channel_id=1, source_target_pairs={{0,1},{1,2},{2,3},{3,0},{4,5},{5,6},{6,7},{7,4},{8,9},{9,10},{10,1... | collective-permute-start | bytes 1572872 | tf_op jit(solution)/shard_map/ppermute | solution.py:106
  102.0 334.1 %all-gather.15.cloned.1.call-start = ((), (), s32[]{:S(2)}) async-start(), calls=%async_computation.3 | async-start | bytes 28311552 | tf_op jit(solution)/shard_map/all_gather | solution.py:747
  102.6 613.8 %all-gather.17.cloned.1.call-start = ((), (), s32[]{:S(2)}) async-start(), calls=%async_computation.4 | async-start | bytes 1769472 | tf_op jit(solution)/shard_map/all_gather | solution.py:946
  105.8 17.9 %collective-permute-start.6 = (bf16[32,1024]{1,0:T(8,128)(2,1)}, bf16[32,1024]{1,0:T(8,128)(2,1)}, u32[]{:S(2)}, u32[]{:S(2)}) collective-permute-start(bf16[32,1024]{1,0:T(8,128)(2,1)} %get-tuple-element.218), channel_id=1, source_target_pairs={{0,1},{1,2},{2,3},{3,0},{4,5},{5,6},{6,7},{7,4},{8,9},{9,10},{10,1... | collective-permute-start | bytes 196616 | tf_op jit(solution)/shard_map/ppermute | solution.py:106
  106.9 51.2 %collective-permute-start.2 = (bf16[256,512]{1,0:T(8,128)(2,1)}, bf16[256,512]{1,0:T(8,128)(2,1)}, u32[]{:S(2)}, u32[]{:S(2)}) collective-permute-start(bf16[256,512]{1,0:T(8,128)(2,1)} %get-tuple-element.172), channel_id=1, source_target_pairs={{0,3},{1,0},{2,1},{3,2},{4,7},{5,4},{6,5},{7,6},{8,11},{9,8},{10,9... | collective-permute-start | bytes 786440 | tf_op jit(solution)/shard_map/ppermute | solution.py:106
  110.7 44.1 %collective-permute-start = (bf16[256,512]{1,0:T(8,128)(2,1)}, bf16[256,512]{1,0:T(8,128)(2,1)}, u32[]{:S(2)}, u32[]{:S(2)}) collective-permute-start(bf16[256,512]{1,0:T(8,128)(2,1)} %get-tuple-element.173), channel_id=1, source_target_pairs={{0,1},{1,2},{2,3},{3,0},{4,5},{5,6},{6,7},{7,4},{8,9},{9,10},{10,1... | collective-permute-start | bytes 786440 | tf_op jit(solution)/shard_map/ppermute | solution.py:106
  110.7 46.4 %collective-permute-start.1 = (bf16[256,512]{1,0:T(8,128)(2,1)}, bf16[256,512]{1,0:T(8,128)(2,1)}, u32[]{:S(2)}, u32[]{:S(2)}) collective-permute-start(bf16[256,512]{1,0:T(8,128)(2,1)} %get-tuple-element.175), channel_id=1, source_target_pairs={{0,2},{1,3},{2,0},{3,1},{4,6},{5,7},{6,4},{7,5},{8,10},{9,11},{10,... | collective-permute-start | bytes 786440 | tf_op jit(solution)/shard_map/ppermute | solution.py:106
  111.3 44.5 %collective-permute-start.15 = (bf16[1024,512]{1,0:T(8,128)(2,1)S(1)}, bf16[1024,512]{1,0:T(8,128)(2,1)S(1)}, u32[]{:S(2)}, u32[]{:S(2)}) collective-permute-start(bf16[1024,512]{1,0:T(8,128)(2,1)S(1)} %copy-done.30), channel_id=1, source_target_pairs={{0,1},{1,2},{2,3},{3,0},{4,5},{5,6},{6,7},{7,4},{8,9},{9,10},{10,1... | collective-permute-start | bytes 3145736 | tf_op jit(solution)/shard_map/ppermute | solution.py:106
  123.8 24.2 %collective-permute-start.7 = (bf16[32,1024]{1,0:T(8,128)(2,1)}, bf16[32,1024]{1,0:T(8,128)(2,1)S(1)}, u32[]{:S(2)}, u32[]{:S(2)}) collective-permute-start(bf16[32,1024]{1,0:T(8,128)(2,1)} %collective-permute-done.6), channel_id=1, source_target_pairs={{0,1},{1,2},{2,3},{3,0},{4,5},{5,6},{6,7},{7,4},{8,9},{9,10},{10,1... | collective-permute-start | bytes 196616 | tf_op jit(solution)/shard_map/ppermute | solution.py:106
  148.0 6.1 collective-permute-start.8
  155.7 23.2 %collective-permute-start.16 = (bf16[1024,512]{1,0:T(8,128)(2,1)S(1)}, bf16[1024,512]{1,0:T(8,128)(2,1)}, u32[]{:S(2)}, u32[]{:S(2)}) collective-permute-start(bf16[1024,512]{1,0:T(8,128)(2,1)S(1)} %collective-permute-done.15), channel_id=1, source_target_pairs={{0,1},{1,2},{2,3},{3,0},{4,5},{5,6},{6,7},{7,4},{8,9},{9,10},{10,1... | collective-permute-start | bytes 3145736 | tf_op jit(solution)/shard_map/ppermute | solution.py:106
  159.1 165.5 %copy-start.3 = (bf16[256,2048]{1,0:T(8,128)(2,1)}, bf16[256,2048]{1,0:T(8,128)(2,1)S(1)}, u32[]{:S(2)}) copy-start(bf16[256,2048]{1,0:T(8,128)(2,1)S(1)} %constant_dynamic-update-slice_fusion.45) | copy-start | bytes 3145732
  178.9 27.4 %collective-permute-start.17 = (bf16[1024,512]{1,0:T(8,128)(2,1)}, bf16[1024,512]{1,0:T(8,128)(2,1)}, u32[]{:S(2)}, u32[]{:S(2)}) collective-permute-start(bf16[1024,512]{1,0:T(8,128)(2,1)} %collective-permute-done.16), channel_id=1, source_target_pairs={{0,1},{1,2},{2,3},{3,0},{4,5},{5,6},{6,7},{7,4},{8,9},{9,10},{10,1... | collective-permute-start | bytes 3145736 | tf_op jit(solution)/shard_map/ppermute | solution.py:106
  187.6 25.8 %collective-permute-start.9 = (bf16[256,1024]{1,0:T(8,128)(2,1)S(1)}, bf16[256,1024]{1,0:T(8,128)(2,1)S(1)}, u32[]{:S(2)}, u32[]{:S(2)}) collective-permute-start(bf16[256,1024]{1,0:T(8,128)(2,1)S(1)} %fusion.34), channel_id=1, source_target_pairs={{0,1},{1,2},{2,3},{3,0},{4,5},{5,6},{6,7},{7,4},{8,9},{9,10},{10,1... | collective-permute-start | bytes 1572872 | tf_op jit(solution)/shard_map/ppermute | solution.py:106
  213.4 18.4 %collective-permute-start.10 = (bf16[256,1024]{1,0:T(8,128)(2,1)S(1)}, bf16[256,1024]{1,0:T(8,128)(2,1)}, u32[]{:S(2)}, u32[]{:S(2)}) collective-permute-start(bf16[256,1024]{1,0:T(8,128)(2,1)S(1)} %collective-permute-done.9), channel_id=1, source_target_pairs={{0,1},{1,2},{2,3},{3,0},{4,5},{5,6},{6,7},{7,4},{8,9},{9,10},{10,1... | collective-permute-start | bytes 1572872 | tf_op jit(solution)/shard_map/ppermute | solution.py:106
  231.8 17.9 %collective-permute-start.11 = (bf16[256,1024]{1,0:T(8,128)(2,1)}, bf16[256,1024]{1,0:T(8,128)(2,1)}, u32[]{:S(2)}, u32[]{:S(2)}) collective-permute-start(bf16[256,1024]{1,0:T(8,128)(2,1)} %collective-permute-done.10), channel_id=1, source_target_pairs={{0,1},{1,2},{2,3},{3,0},{4,5},{5,6},{6,7},{7,4},{8,9},{9,10},{10,1... | collective-permute-start | bytes 1572872 | tf_op jit(solution)/shard_map/ppermute | solution.py:106
  326.7 27.1 %collective-permute-start.18 = (bf16[256,2048]{1,0:T(8,128)(2,1)S(1)}, bf16[256,2048]{1,0:T(8,128)(2,1)S(1)}, u32[]{:S(2)}, u32[]{:S(2)}) collective-permute-start(bf16[256,2048]{1,0:T(8,128)(2,1)S(1)} %get-tuple-element.162), channel_id=1, source_target_pairs={{0,1},{1,2},{2,3},{3,0},{4,5},{5,6},{6,7},{7,4},{8,9},{9,10},{10,1... | collective-permute-start | bytes 3145736 | tf_op jit(solution)/shard_map/ppermute | solution.py:106
  353.9 26.3 %collective-permute-start.19 = (bf16[256,2048]{1,0:T(8,128)(2,1)S(1)}, bf16[256,2048]{1,0:T(8,128)(2,1)S(1)}, u32[]{:S(2)}, u32[]{:S(2)}) collective-permute-start(bf16[256,2048]{1,0:T(8,128)(2,1)S(1)} %collective-permute-done.18), channel_id=1, source_target_pairs={{0,1},{1,2},{2,3},{3,0},{4,5},{5,6},{6,7},{7,4},{8,9},{9,10},{10,1... | collective-permute-start | bytes 3145736 | tf_op jit(solution)/shard_map/ppermute | solution.py:106
  380.2 25.6 %collective-permute-start.20 = (bf16[256,2048]{1,0:T(8,128)(2,1)S(1)}, bf16[256,2048]{1,0:T(8,128)(2,1)S(1)}, u32[]{:S(2)}, u32[]{:S(2)}) collective-permute-start(bf16[256,2048]{1,0:T(8,128)(2,1)S(1)} %collective-permute-done.19), channel_id=1, source_target_pairs={{0,1},{1,2},{2,3},{3,0},{4,5},{5,6},{6,7},{7,4},{8,9},{9,10},{10,1... | collective-permute-start | bytes 3145736 | tf_op jit(solution)/shard_map/ppermute | solution.py:106
  462.9 29.0 %collective-permute-start.21 = (bf16[256,2176]{1,0:T(8,128)(2,1)S(1)}, bf16[256,2176]{1,0:T(8,128)(2,1)S(1)}, u32[]{:S(2)}, u32[]{:S(2)}) collective-permute-start(bf16[256,2176]{1,0:T(8,128)(2,1)S(1)} %convert_element_type.154.refs_9_), channel_id=1, source_target_pairs={{0,1},{1,2},{2,3},{3,0},{4,5},{5,6},{6,7},{7,4},{8,9},{9,10},{10,1... | collective-permute-start | bytes 3342344 | tf_op jit(solution)/shard_map/ppermute | solution.py:106
  493.7 27.8 %collective-permute-start.22 = (bf16[256,2176]{1,0:T(8,128)(2,1)S(1)}, bf16[256,2176]{1,0:T(8,128)(2,1)S(1)}, u32[]{:S(2)}, u32[]{:S(2)}) collective-permute-start(bf16[256,2176]{1,0:T(8,128)(2,1)S(1)} %add_convert_fusion.1.refs_9_), channel_id=1, source_target_pairs={{0,1},{1,2},{2,3},{3,0},{4,5},{5,6},{6,7},{7,4},{8,9},{9,10},{10,1... | collective-permute-start | bytes 3342344 | tf_op jit(solution)/shard_map/ppermute | solution.py:106
  523.3 27.0 %collective-permute-start.24 = (bf16[256,2176]{1,0:T(8,128)(2,1)S(1)}, bf16[256,2176]{1,0:T(8,128)(2,1)S(1)}, u32[]{:S(2)}, u32[]{:S(2)}) collective-permute-start(bf16[256,2176]{1,0:T(8,128)(2,1)S(1)} %add_convert_fusion.refs_9_), channel_id=1, source_target_pairs={{0,1},{1,2},{2,3},{3,0},{4,5},{5,6},{6,7},{7,4},{8,9},{9,10},{10,1... | collective-permute-start | bytes 3342344 | tf_op jit(solution)/shard_map/ppermute | solution.py:106
  549.2 39.2 %collective-permute-start.23 = (bf16[1024,512]{1,0:T(8,128)(2,1)}, bf16[1024,512]{1,0:T(8,128)(2,1)}, u32[]{:S(2)}, u32[]{:S(2)}) collective-permute-start(bf16[1024,512]{1,0:T(8,128)(2,1)} %get-tuple-element.88), channel_id=1, source_target_pairs={{0,1},{1,2},{2,3},{3,0},{4,5},{5,6},{6,7},{7,4},{8,9},{9,10},{10,1... | collective-permute-start | bytes 3145736 | tf_op jit(solution)/shard_map/ppermute | solution.py:106
  592.1 50.7 %collective-permute-start.25 = (bf16[1024,512]{1,0:T(8,128)(2,1)}, bf16[1024,512]{1,0:T(8,128)(2,1)S(1)}, u32[]{:S(2)}, u32[]{:S(2)}) collective-permute-start(bf16[1024,512]{1,0:T(8,128)(2,1)} %hop.2.refs_20_), channel_id=1, source_target_pairs={{0,1},{1,2},{2,3},{3,0},{4,5},{5,6},{6,7},{7,4},{8,9},{9,10},{10,1... | collective-permute-start | bytes 3145736 | tf_op jit(solution)/shard_map/ppermute | solution.py:106
  608.4 34.3 %collective-permute-start.26 = (bf16[352,512]{1,0:T(8,128)(2,1)}, bf16[352,512]{1,0:T(8,128)(2,1)S(1)}, u32[]{:S(2)}, u32[]{:S(2)}) collective-permute-start(bf16[352,512]{1,0:T(8,128)(2,1)} %get-tuple-element.101), channel_id=1, source_target_pairs={{0,1},{1,2},{2,3},{3,0},{4,5},{5,6},{6,7},{7,4},{8,9},{9,10},{10,1... | collective-permute-start | bytes 1081352 | tf_op jit(solution)/shard_map/ppermute | solution.py:106
  611.2 31.6 %collective-permute-start.27 = (bf16[352,512]{1,0:T(8,128)(2,1)}, bf16[352,512]{1,0:T(8,128)(2,1)S(1)}, u32[]{:S(2)}, u32[]{:S(2)}) collective-permute-start(bf16[352,512]{1,0:T(8,128)(2,1)} %get-tuple-element.102), channel_id=1, source_target_pairs={{0,2},{1,3},{2,0},{3,1},{4,6},{5,7},{6,4},{7,5},{8,10},{9,11},{10,... | collective-permute-start | bytes 1081352 | tf_op jit(solution)/shard_map/ppermute | solution.py:106
  612.5 30.4 %collective-permute-start.28 = (bf16[352,512]{1,0:T(8,128)(2,1)}, bf16[352,512]{1,0:T(8,128)(2,1)S(1)}, u32[]{:S(2)}, u32[]{:S(2)}) collective-permute-start(bf16[352,512]{1,0:T(8,128)(2,1)} %get-tuple-element.103), channel_id=1, source_target_pairs={{0,3},{1,0},{2,1},{3,2},{4,7},{5,4},{6,5},{7,6},{8,11},{9,8},{10,9... | collective-permute-start | bytes 1081352 | tf_op jit(solution)/shard_map/ppermute | solution.py:106
  648.4 23.8 %collective-permute-start.29 = (bf16[352,512]{1,0:T(8,128)(2,1)}, bf16[352,512]{1,0:T(8,128)(2,1)S(1)}, u32[]{:S(2)}, u32[]{:S(2)}) collective-permute-start(bf16[352,512]{1,0:T(8,128)(2,1)} %get-tuple-element.116), channel_id=1, source_target_pairs={{0,1},{1,2},{2,3},{3,0},{4,5},{5,6},{6,7},{7,4},{8,9},{9,10},{10,1... | collective-permute-start | bytes 1081352 | tf_op jit(solution)/shard_map/ppermute | solution.py:106
  653.7 22.9 %collective-permute-start.30 = (bf16[352,512]{1,0:T(8,128)(2,1)}, bf16[352,512]{1,0:T(8,128)(2,1)S(1)}, u32[]{:S(2)}, u32[]{:S(2)}) collective-permute-start(bf16[352,512]{1,0:T(8,128)(2,1)} %get-tuple-element.117), channel_id=1, source_target_pairs={{0,2},{1,3},{2,0},{3,1},{4,6},{5,7},{6,4},{7,5},{8,10},{9,11},{10,... | collective-permute-start | bytes 1081352 | tf_op jit(solution)/shard_map/ppermute | solution.py:106
  655.9 21.5 %collective-permute-start.31 = (bf16[352,512]{1,0:T(8,128)(2,1)}, bf16[352,512]{1,0:T(8,128)(2,1)S(1)}, u32[]{:S(2)}, u32[]{:S(2)}) collective-permute-start(bf16[352,512]{1,0:T(8,128)(2,1)} %get-tuple-element.118), channel_id=1, source_target_pairs={{0,3},{1,0},{2,1},{3,2},{4,7},{5,4},{6,5},{7,6},{8,11},{9,8},{10,9... | collective-permute-start | bytes 1081352 | tf_op jit(solution)/shard_map/ppermute | solution.py:106
  683.1 76.5 %all-gather.19.cloned.1.call-start = ((), (), s32[]{:S(2)}) async-start(), calls=%async_computation.5 | async-start | bytes 1474560 | tf_op jit(solution)/shard_map/all_gather | solution.py:945
  686.3 17.9 %collective-permute-start.33 = (bf16[40,2048]{1,0:T(8,128)(2,1)S(1)}, bf16[40,2048]{1,0:T(8,128)(2,1)S(1)}, u32[]{:S(2)}, u32[]{:S(2)}) collective-permute-start(bf16[40,2048]{1,0:T(8,128)(2,1)S(1)} %maximum_maximum_fusion), channel_id=1, source_target_pairs={{0,1},{1,2},{2,3},{3,0},{4,5},{5,6},{6,7},{7,4},{8,9},{9,10},{10,1... | collective-permute-start | bytes 491528 | tf_op jit(solution)/shard_map/ppermute | solution.py:106
  694.4 13.7 %collective-permute-start.32 = (bf16[40,2048]{1,0:T(8,128)(2,1)S(1)}, bf16[40,2048]{1,0:T(8,128)(2,1)S(1)}, u32[]{:S(2)}, u32[]{:S(2)}) collective-permute-start(bf16[40,2048]{1,0:T(8,128)(2,1)S(1)} %maximum_maximum_fusion), channel_id=1, source_target_pairs={{0,2},{1,3},{2,0},{3,1},{4,6},{5,7},{6,4},{7,5},{8,10},{9,11},{10,... | collective-permute-start | bytes 491528 | tf_op jit(solution)/shard_map/ppermute | solution.py:106
  697.7 10.4 %collective-permute-start.34 = (bf16[40,2048]{1,0:T(8,128)(2,1)S(1)}, bf16[40,2048]{1,0:T(8,128)(2,1)S(1)}, u32[]{:S(2)}, u32[]{:S(2)}) collective-permute-start(bf16[40,2048]{1,0:T(8,128)(2,1)S(1)} %maximum_maximum_fusion), channel_id=1, source_target_pairs={{0,3},{1,0},{2,1},{3,2},{4,7},{5,4},{6,5},{7,6},{8,11},{9,8},{10,9... | collective-permute-start | bytes 491528 | tf_op jit(solution)/shard_map/ppermute | solution.py:106
  719.3 6.7 collective-permute-start.35
  721.5 27.1 %collective-permute-start.39 = (bf16[256,512]{1,0:T(8,128)(2,1)S(1)}, bf16[256,512]{1,0:T(8,128)(2,1)S(1)}, u32[]{:S(2)}, u32[]{:S(2)}) collective-permute-start(bf16[256,512]{1,0:T(8,128)(2,1)S(1)} %get-tuple-element.169), channel_id=1, source_target_pairs={{0,3},{1,0},{2,1},{3,2},{4,7},{5,4},{6,5},{7,6},{8,11},{9,8},{10,9... | collective-permute-start | bytes 786440 | tf_op jit(solution)/shard_map/ppermute | solution.py:106
  723.9 24.7 %collective-permute-start.38 = (bf16[256,512]{1,0:T(8,128)(2,1)S(1)}, bf16[256,512]{1,0:T(8,128)(2,1)S(1)}, u32[]{:S(2)}, u32[]{:S(2)}) collective-permute-start(bf16[256,512]{1,0:T(8,128)(2,1)S(1)} %get-tuple-element.170), channel_id=1, source_target_pairs={{0,2},{1,3},{2,0},{3,1},{4,6},{5,7},{6,4},{7,5},{8,10},{9,11},{10,... | collective-permute-start | bytes 786440 | tf_op jit(solution)/shard_map/ppermute | solution.py:106
  724.0 24.6 %collective-permute-start.37 = (bf16[256,512]{1,0:T(8,128)(2,1)S(1)}, bf16[256,512]{1,0:T(8,128)(2,1)S(1)}, u32[]{:S(2)}, u32[]{:S(2)}) collective-permute-start(bf16[256,512]{1,0:T(8,128)(2,1)S(1)} %get-tuple-element.171), channel_id=1, source_target_pairs={{0,1},{1,2},{2,3},{3,0},{4,5},{5,6},{6,7},{7,4},{8,9},{9,10},{10,1... | collective-permute-start | bytes 786440 | tf_op jit(solution)/shard_map/ppermute | solution.py:106
  726.6 20.7 %collective-permute-start.36 = (f32[1,128]{1,0:T(1,128)S(1)}, f32[1,128]{1,0:T(1,128)S(1)}, u32[]{:S(2)}, u32[]{:S(2)}) collective-permute-start(f32[1,128]{1,0:T(1,128)S(1)} %broadcast_add_fusion), channel_id=1, source_target_pairs={{0,2},{1,3},{2,0},{3,1},{4,6},{5,7},{6,4},{7,5},{8,10},{9,11},{10,... | collective-permute-start | bytes 1544 | tf_op jit(solution)/shard_map/ppermute | solution.py:961
  753.8 26.7 %collective-permute-start.40 = (bf16[1024,512]{1,0:T(8,128)(2,1)}, bf16[1024,512]{1,0:T(8,128)(2,1)S(1)}, u32[]{:S(2)}, u32[]{:S(2)}) collective-permute-start(bf16[1024,512]{1,0:T(8,128)(2,1)} %hop.3), channel_id=1, source_target_pairs={{0,1},{1,2},{2,3},{3,0},{4,5},{5,6},{6,7},{7,4},{8,9},{9,10},{10,1... | collective-permute-start | bytes 3145736 | tf_op jit(solution)/shard_map/ppermute | solution.py:106
  (81 other events, 637.1 us)
Sparse Core Ops, SparseCore 0:
  15.3 105.6 all-gather.10
  123.5 89.8 all-gather.8
  215.8 93.1 all-gather.12
  310.7 125.3 all-gather.14
  683.2 33.1 all-gather.16
  718.7 24.6 all-gather.18
